TPU v7x, 32 devices: a whole 2x2x4 slice. The times are simulated.
32 devices in a mesh: ctx: 16 (over z, y, core), tp: 2 (over x).
Axes of the slice: x: 2, y: 2, z: 4, core: 2. Of those that a mesh axis runs over, the one named last changes fastest.
Arguments:
- layer_input: bfloat16 [2048, 2048], P('ctx'), may hold values from -6 to 6
- block_order: int32 [32], replicated, may hold values from 0 to 31, each once
- attn_gain: float32 [2048], replicated, may hold values from 0.1 to 1.9
- attn_shift: float32 [2048], replicated, may hold values from -1.75 to 1.75
- mlp_gain: float32 [2048], replicated, may hold values from 0.1 to 1.9
- mlp_shift: float32 [2048], replicated, may hold values from -1.75 to 1.75
- w_query: bfloat16 [2048, 2048], P('ctx', 'tp'), may hold values from -0.125 to 0.125
- b_query: float32 [2048], P('tp'), may hold values from -3 to 3
- w_key: bfloat16 [2048, 2048], P('ctx', 'tp'), may hold values from -0.125 to 0.125
- b_key: float32 [2048], P('tp'), may hold values from -3 to 3
- w_value: bfloat16 [2048, 2048], P('ctx', 'tp'), may hold values from -0.125 to 0.125
- b_value: float32 [2048], P('tp'), may hold values from -3 to 3
- w_out: bfloat16 [2048, 2048], P('tp', 'ctx'), may hold values from -1 to 1
- b_out: float32 [2048], replicated, may hold values from -1.75 to 1.75
- w_up: bfloat16 [2048, 8192], P('ctx', 'tp'), may hold values from -0.125 to 0.125
- b_up: float32 [8192], P('tp'), may hold values from -3 to 3
- w_down: bfloat16 [8192, 2048], P('tp', 'ctx'), may hold values from -0.0625 to 0.0625
- b_down: float32 [2048], replicated, may hold values from -1.75 to 1.75
- out_grad: bfloat16 [2048, 2048], P('ctx'), may hold values from -6 to 6
Outputs:
- layer_output: bfloat16 [2048, 2048], P('ctx')
- input_grad: float32 [2048, 2048], P('ctx')
- grad_w_query: float32 [2048, 2048], P('ctx', 'tp')
- grad_w_key: float32 [2048, 2048], P('ctx', 'tp')
- grad_w_value: float32 [2048, 2048], P('ctx', 'tp')
- grad_w_out: float32 [2048, 2048], P('tp', 'ctx')
- grad_w_up: float32 [2048, 8192], P('ctx', 'tp')
- grad_w_down: float32 [8192, 2048], P('tp', 'ctx')
- grad_b_query: float32 [2048], P('tp')
- grad_b_key: float32 [2048], P('tp')
- grad_b_value: float32 [2048], P('tp')
- grad_b_out: float32 [2048], replicated
- grad_b_up: float32 [8192], P('tp')
- grad_b_down: float32 [2048], replicated
- grad_attn_gain: float32 [2048], replicated
- grad_attn_shift: float32 [2048], replicated
- grad_mlp_gain: float32 [2048], replicated
- grad_mlp_shift: float32 [2048], replicated
Inputs may be any that keep to these rules, and one draw needn't show every extreme that they name: A permutation: device i of ctx holds sequence blocks block_order[2 i] and block_order[2 i + 1] in that order, each of 64 tokens.
All inputs are finite; a program needn't handle non-finite values.
Results may differ from a plain program's by a relative error of at most 0.018.
Values may be sent and summed in bfloat16 or wider, within the bound.
A program may use at most 192 MiB of HBM per device.

v0:
```python
import math

import jax
import jax.numpy as jnp
from jax import lax
from jax.sharding import PartitionSpec as P

HEADS = 8
HD = 256
ROT = 64


norm_epsilon = 1e-05
masked_score = -1e30


def passed_along(block, axis, distance):
    devices = range(lax.axis_size(axis))
    route = [((i - distance) % len(devices), i) for i in devices]
    return lax.ppermute(block, axis, route)


def layer_norm(values, gain, shift):
    row_mean = jnp.mean(values, -1, keepdims=True)
    centered = values - row_mean
    variance = jnp.mean(centered * centered, -1, keepdims=True)
    inverse = lax.rsqrt(variance + norm_epsilon)
    normal = centered * inverse
    return (normal * gain + shift, normal, inverse)


def norm_backward(grad_rows, normal, inverse, gain):
    scaled = grad_rows * gain
    return inverse * (
        scaled
        - jnp.mean(scaled, -1, keepdims=True)
        - normal * jnp.mean(scaled * normal, -1, keepdims=True)
    )


def rotate(values, cosine, sine_table):
    half_rot = ROT // 2
    leading = values[..., :half_rot]
    trailing = values[..., half_rot:ROT]
    cos_rows = cosine[:, None, :]
    sin_rows = sine_table[:, None, :]
    return jnp.concatenate(
        [
            leading * cos_rows - trailing * sin_rows,
            trailing * cos_rows + leading * sin_rows,
            values[..., ROT:],
        ],
        -1,
    )


def rope_tables(positions):
    freqs = 10000.0 ** (-(2.0 * jnp.arange(ROT // 2, dtype=jnp.float32)) / ROT)
    angles = positions.astype(jnp.float32)[:, None] * freqs[None, :]
    return (jnp.cos(angles), jnp.sin(angles))


def row_positions(block_order, first_row, row_total, shard_rows):
    row_index = first_row + jnp.arange(row_total, dtype=jnp.int32)
    half_block = shard_rows // 2
    device = row_index // shard_rows
    within = row_index % shard_rows
    slot_index = 2 * device + within // half_block
    table = jnp.arange(block_order.shape[0], dtype=jnp.int32)
    picked = jnp.sum(
        jnp.where(slot_index[:, None] == table[None, :], block_order[None, :], 0), axis=1
    )
    return picked * half_block + within % half_block


def gelu_slope(values):
    return 0.5 * (1.0 + lax.erf(values / math.sqrt(2.0))) + values * jnp.exp(
        -0.5 * values * values
    ) / math.sqrt(2.0 * math.pi)


def fold_blocks(step_fn, carry, members, shard_rows):
    row_total = members[0].shape[0]
    number = row_total // shard_rows
    blocked = tuple((member.reshape((number, shard_rows) + member.shape[1:]) for member in members))
    offsets = shard_rows * jnp.arange(number, dtype=jnp.int32)

    def advance(running, element):
        return (step_fn(running, element[0], element[1]), None)

    carry, _ = lax.scan(advance, carry, (blocked, offsets))
    return carry


def grad_block(
    query_rows, query_place, grad_rows, lse_rows, delta_rows, key_rows, value_rows, key_place
):
    score_scale = 1.0 / math.sqrt(HD)
    scores = (
        jnp.einsum("thd,shd->hts", query_rows, key_rows, preferred_element_type=jnp.float32)
        * score_scale
    )
    allowed = key_place[None, None, :] <= query_place[None, :, None]
    probs = jnp.where(allowed, jnp.exp(scores - lse_rows[..., None]), 0.0)
    value_part = jnp.einsum(
        "hts,thd->shd", probs.astype(jnp.bfloat16), grad_rows, preferred_element_type=jnp.float32
    )
    prob_grad = jnp.einsum(
        "thd,shd->hts", grad_rows, value_rows, preferred_element_type=jnp.float32
    )
    score_grad = (probs * (prob_grad - delta_rows[..., None]) * score_scale).astype(jnp.bfloat16)
    query_part = jnp.einsum(
        "hts,shd->thd", score_grad, key_rows, preferred_element_type=jnp.float32
    )
    key_part = jnp.einsum(
        "hts,thd->shd", score_grad, query_rows, preferred_element_type=jnp.float32
    )
    return (query_part, key_part, value_part)


def shards(
    layer_input,
    block_order,
    attn_gain,
    attn_shift,
    mlp_gain,
    mlp_shift,
    w_query,
    b_query,
    w_key,
    b_key,
    w_value,
    b_value,
    w_out,
    b_out,
    w_up,
    b_up,
    w_down,
    b_down,
    out_grad,
):
    shard_rows = layer_input.shape[0]
    cycle_size = lax.axis_size("ctx")
    head_count = HEADS // lax.axis_size("tp")
    local_width = head_count * HD
    position = lax.axis_index("ctx")
    score_scale = 1.0 / math.sqrt(HD)
    query_place = row_positions(block_order, position * shard_rows, shard_rows, shard_rows)
    cosine, sine_table = rope_tables(query_place)
    inputs32 = layer_input.astype(jnp.float32)
    normed_attn, normal_attn, inverse_attn = layer_norm(inputs32, attn_gain, attn_shift)
    normed_mlp, normal_mlp, inverse_mlp = layer_norm(inputs32, mlp_gain, mlp_shift)
    attn_in = normed_attn.astype(jnp.bfloat16)
    mlp_in = normed_mlp.astype(jnp.bfloat16)
    full_query, full_key, full_value, full_up = (
        lax.all_gather(w_query, "ctx", axis=0, tiled=True),
        lax.all_gather(w_key, "ctx", axis=0, tiled=True),
        lax.all_gather(w_value, "ctx", axis=0, tiled=True),
        lax.all_gather(w_up, "ctx", axis=0, tiled=True),
    )
    full_out, full_down = (
        lax.all_gather(w_out, "ctx", axis=1, tiled=True),
        lax.all_gather(w_down, "ctx", axis=1, tiled=True),
    )

    def project(weight, bias):
        linear = jnp.dot(attn_in, weight, preferred_element_type=jnp.float32) + bias
        return linear.reshape(shard_rows, head_count, HD)

    query = rotate(project(full_query, b_query), cosine, sine_table).astype(jnp.bfloat16)
    keys = rotate(project(full_key, b_key), cosine, sine_table).astype(jnp.bfloat16)
    values = project(full_value, b_value).astype(jnp.bfloat16)

    def forward_step(carry, members, first_row):
        running_top, running_total, running_sum = carry
        key_rows, value_rows = members
        key_place = row_positions(block_order, first_row, key_rows.shape[0], shard_rows)
        scores = (
            jnp.einsum("thd,shd->hts", query, key_rows, preferred_element_type=jnp.float32)
            * score_scale
        )
        allowed = key_place[None, None, :] <= query_place[None, :, None]
        scores = jnp.where(allowed, scores, masked_score)
        new_top = jnp.maximum(running_top, jnp.max(scores, -1))
        factor = jnp.exp(running_top - new_top)
        weights = jnp.where(allowed, jnp.exp(scores - new_top[..., None]), 0.0)
        running_total = running_total * factor + jnp.sum(weights, -1)
        running_sum = running_sum * factor[..., None] + jnp.einsum(
            "hts,shd->htd",
            weights.astype(jnp.bfloat16),
            value_rows,
            preferred_element_type=jnp.float32,
        )
        return (new_top, running_total, running_sum)

    start_state = (
        jnp.full((head_count, shard_rows), masked_score, jnp.float32),
        jnp.zeros((head_count, shard_rows), jnp.float32),
        jnp.zeros((head_count, shard_rows, HD), jnp.float32),
    )
    final_top, final_total, final_sum = fold_blocks(
        forward_step,
        start_state,
        (
            lax.all_gather(keys, "ctx", axis=0, tiled=True),
            lax.all_gather(values, "ctx", axis=0, tiled=True),
        ),
        shard_rows,
    )
    lse = final_top + jnp.log(final_total)
    attended = jnp.transpose(final_sum / final_total[..., None], (1, 0, 2))
    attn_low = attended.reshape(shard_rows, local_width).astype(jnp.bfloat16)
    hidden_pre = jnp.dot(mlp_in, full_up, preferred_element_type=jnp.float32) + b_up
    hidden = jax.nn.gelu(hidden_pre, approximate=False).astype(jnp.bfloat16)
    branches = jnp.dot(attn_low, full_out, preferred_element_type=jnp.float32) + jnp.dot(
        hidden, full_down, preferred_element_type=jnp.float32
    )
    branches = lax.psum(branches, "tp")
    layer_output = (inputs32 + branches + b_out + b_down).astype(jnp.bfloat16)
    grad32 = out_grad.astype(jnp.float32)
    grad_w_out = jnp.einsum("ti,tj->ij", attn_low, out_grad, preferred_element_type=jnp.float32)
    grad_w_down = jnp.einsum("ti,tj->ij", hidden, out_grad, preferred_element_type=jnp.float32)
    bias_grad = jnp.sum(grad32, 0)
    head_grad = jnp.einsum(
        "tj,ij->ti", out_grad, full_out, preferred_element_type=jnp.float32
    ).astype(jnp.bfloat16)
    head_grad = head_grad.reshape(shard_rows, head_count, HD)
    up_grad32 = jnp.einsum(
        "tj,ij->ti", out_grad, full_down, preferred_element_type=jnp.float32
    ) * gelu_slope(hidden_pre)
    grad_b_up = jnp.sum(up_grad32, 0)
    up_low = up_grad32.astype(jnp.bfloat16)
    grad_w_up = jnp.einsum("ti,tj->ij", mlp_in, up_low, preferred_element_type=jnp.float32)
    mlp_back = jnp.einsum("tj,ij->ti", up_low, full_up, preferred_element_type=jnp.float32)
    delta = jnp.transpose(jnp.sum(head_grad.astype(jnp.float32) * attended, -1))
    empty_rows = jnp.zeros((shard_rows, head_count, HD), jnp.float32)

    def one_step(carry, step_index):
        key_rows, value_rows, key_acc, value_acc, query_acc = carry
        owner = (position - step_index) % cycle_size
        key_place = row_positions(block_order, owner * shard_rows, shard_rows, shard_rows)
        query_part, key_part, value_part = grad_block(
            query, query_place, head_grad, lse, delta, key_rows, value_rows, key_place
        )
        key_rows, value_rows = passed_along((key_rows, value_rows), "ctx", 1)
        key_acc, value_acc = passed_along((key_acc + key_part, value_acc + value_part), "ctx", 1)
        return (key_rows, value_rows, key_acc, value_acc, query_acc + query_part)

    def turn(turn_index, carry):
        for sub_step in range(4):
            carry = one_step(carry, turn_index * 4 + sub_step)
        return carry

    carried = lax.fori_loop(
        0, cycle_size // 4, turn, (keys, values, empty_rows, empty_rows, empty_rows)
    )
    key_acc, value_acc, query_acc = (carried[2], carried[3], carried[4])
    query_lin = rotate(query_acc, cosine, -sine_table).reshape(shard_rows, local_width)
    key_lin = rotate(key_acc, cosine, -sine_table).reshape(shard_rows, local_width)
    value_lin = value_acc.reshape(shard_rows, local_width)
    grad_b_query = jnp.sum(query_lin, 0)
    grad_b_key = jnp.sum(key_lin, 0)
    grad_b_value = jnp.sum(value_lin, 0)
    query_low = query_lin.astype(jnp.bfloat16)
    key_low = key_lin.astype(jnp.bfloat16)
    value_low = value_lin.astype(jnp.bfloat16)
    grad_w_query = jnp.einsum("ti,tj->ij", attn_in, query_low, preferred_element_type=jnp.float32)
    grad_w_key = jnp.einsum("ti,tj->ij", attn_in, key_low, preferred_element_type=jnp.float32)
    grad_w_value = jnp.einsum("ti,tj->ij", attn_in, value_low, preferred_element_type=jnp.float32)
    attn_back = (
        jnp.einsum("tj,ij->ti", query_low, full_query, preferred_element_type=jnp.float32)
        + jnp.einsum("tj,ij->ti", key_low, full_key, preferred_element_type=jnp.float32)
        + jnp.einsum("tj,ij->ti", value_low, full_value, preferred_element_type=jnp.float32)
    )
    attn_back, mlp_back = lax.psum((attn_back, mlp_back), "tp")
    input_grad = (
        grad32
        + norm_backward(attn_back, normal_attn, inverse_attn, attn_gain)
        + norm_backward(mlp_back, normal_mlp, inverse_mlp, mlp_gain)
    )
    summed_small = lax.psum(
        (
            grad_b_query,
            grad_b_key,
            grad_b_value,
            grad_b_up,
            bias_grad,
            jnp.sum(attn_back * normal_attn, 0),
            jnp.sum(attn_back, 0),
            jnp.sum(mlp_back * normal_mlp, 0),
            jnp.sum(mlp_back, 0),
        ),
        "ctx",
    )
    in_shares = (
        lax.psum_scatter(grad_w_query, "ctx", scatter_dimension=0, tiled=True),
        lax.psum_scatter(grad_w_key, "ctx", scatter_dimension=0, tiled=True),
        lax.psum_scatter(grad_w_value, "ctx", scatter_dimension=0, tiled=True),
        lax.psum_scatter(grad_w_up, "ctx", scatter_dimension=0, tiled=True),
    )
    out_shares = (
        lax.psum_scatter(grad_w_out, "ctx", scatter_dimension=1, tiled=True),
        lax.psum_scatter(grad_w_down, "ctx", scatter_dimension=1, tiled=True),
    )
    return (
        layer_output,
        input_grad,
        in_shares[0],
        in_shares[1],
        in_shares[2],
        out_shares[0],
        in_shares[3],
        out_shares[1],
        summed_small[0],
        summed_small[1],
        summed_small[2],
        summed_small[4],
        summed_small[3],
        summed_small[4],
        summed_small[5],
        summed_small[6],
        summed_small[7],
        summed_small[8],
    )


def solution(mesh):
    in_specs = (
        P("ctx", None),
        P(),
        P(),
        P(),
        P(),
        P(),
        P("ctx", "tp"),
        P("tp"),
        P("ctx", "tp"),
        P("tp"),
        P("ctx", "tp"),
        P("tp"),
        P("tp", "ctx"),
        P(),
        P("ctx", "tp"),
        P("tp"),
        P("tp", "ctx"),
        P(),
        P("ctx", None),
    )
    out_specs = (
        P("ctx", None),
        P("ctx", None),
        P("ctx", "tp"),
        P("ctx", "tp"),
        P("ctx", "tp"),
        P("tp", "ctx"),
        P("ctx", "tp"),
        P("tp", "ctx"),
        P("tp"),
        P("tp"),
        P("tp"),
        P(),
        P("tp"),
        P(),
        P(),
        P(),
        P(),
        P(),
    )
    return jax.shard_map(shards, mesh=mesh, in_specs=in_specs, out_specs=out_specs, check_vma=False)
```

profile of v0, /device:TPU:0, one launch (start us, length us, event | category | flops | bytes accessed | tf_op | source)
XLA Modules:
  0.0 2215.5 jit_solution(5476027327677002193)
XLA Ops:
  14.2 49.3 %all-gather.9.cloned.1.call-done = bf16[2048,1024]{1,0:T(8,128)(2,1)} async-done(((bf16[128,1024]{1,0:T(8,128)(2,1)}), bf16[2048,1024]{1,0:T(8,128)(2,1)}) %all-gather.9.cloned.1.call-update) | async-done | bytes 4194320 | tf_op jit(solution)/shard_map/all_gather | solution.py:157
  67.4 47.4 %all-gather.13.cloned.1.call-done = bf16[2048,1024]{1,0:T(8,128)(2,1)} async-done(((bf16[128,1024]{1,0:T(8,128)(2,1)}), bf16[2048,1024]{1,0:T(8,128)(2,1)}) %all-gather.13.cloned.1.call-update) | async-done | bytes 4194320 | tf_op jit(solution)/shard_map/all_gather | solution.py:156
  119.8 48.8 %all-gather.19.cloned.1.call-done = bf16[1024,2048]{1,0:T(8,128)(2,1)} async-done(((bf16[1024,128]{1,0:T(8,128)(2,1)}), bf16[1024,2048]{1,0:T(8,128)(2,1)}) %all-gather.19.cloned.1.call-update) | async-done | bytes 4194320 | tf_op jit(solution)/shard_map/all_gather | solution.py:162
  172.4 47.1 %all-gather.15.cloned.1.call-done = bf16[2048,1024]{1,0:T(8,128)(2,1)} async-done(((bf16[128,1024]{1,0:T(8,128)(2,1)}), bf16[2048,1024]{1,0:T(8,128)(2,1)}) %all-gather.15.cloned.1.call-update) | async-done | bytes 4194320 | tf_op jit(solution)/shard_map/all_gather | solution.py:158
  226.0 44.6 %all-gather.11.cloned.1.call-done = bf16[2048,4,256]{2,0,1:T(8,128)(2,1)} async-done(((bf16[128,4,256]{2,0,1:T(8,128)(2,1)}), bf16[2048,4,256]{2,0,1:T(8,128)(2,1)}) %all-gather.11.cloned.1.call-update) | async-done | bytes 4194320 | tf_op jit(solution)/shard_map/all_gather | solution.py:205
  270.6 51.7 %all-gather.17.cloned.1.call-done = bf16[2048,4,256]{2,0,1:T(8,128)(2,1)} async-done(((bf16[128,4,256]{2,0,1:T(8,128)(2,1)}), bf16[2048,4,256]{2,0,1:T(8,128)(2,1)}) %all-gather.17.cloned.1.call-update) | async-done | bytes 4194320 | tf_op jit(solution)/shard_map/all_gather | solution.py:206
  322.3 76.6 %while.43 = (s32[]{:T(128)}, f32[4,128]{1,0:T(4,128)S(1)}, f32[4,128]{1,0:T(4,128)S(1)}, f32[4,128,256]{2,1,0:T(8,128)S(1)}, s32[16]{0:T(128)S(1)}, /*index=5*/s...) while((s32[]{:T(128)}, f32[4,128]{1,0:T(4,128)S(1)}, ...), condition=%wide.region_7.8_spmd.clone, body=%wide.region_3.7_spmd.clone.sunk | while | flops 68130944 | bytes 2724629 | solution.py:91
  400.0 440.1 %while.44 = (s32[]{:T(128)}, bf16[128,4,256]{2,0,1:T(8,128)(2,1)}, bf16[128,4,256]{2,0,1:T(8,128)(2,1)S(1)}, f32[128,4,256]{2,0,1:T(8,128)S(1)}, f32[128,4,256]{...) while((s32[]{:T(128)}, bf16[128,4,256]{2,0,1:T(8,128)(2,1)}, ...), condition=%wide.region_15.16_spmd.clone, body=%wide.region_10.15_spmd.clone.sunk | while | flops 675035712 | bytes 54163496 | solution.py:254
  437.0 15.2 collective-permute-done.8
  469.4 13.8 collective-permute-done.2
  487.4 15.5 collective-permute-done.14
  503.0 15.3 collective-permute-done.10
  520.2 25.0 %collective-permute-done.3 = bf16[128,4,256]{2,0,1:T(8,128)(2,1)} collective-permute-done((bf16[128,4,256]{2,0,1:T(8,128)(2,1)S(1)}, bf16[128,4,256]{2,0,1:T(8,128)(2,1)}, u32[]{:S(2)}, u32[]{:S(2)}) %collective-permute-start.3) | collective-permute-done | bytes 262176 | tf_op jit(solution)/shard_map/while/body/eval_jaxpr/ppermute | solution.py:20
  577.2 15.6 collective-permute-done.12
  594.2 15.5 collective-permute-done.8
  626.8 24.9 %collective-permute-done.2 = bf16[128,4,256]{2,0,1:T(8,128)(2,1)S(1)} collective-permute-done((bf16[128,4,256]{2,0,1:T(8,128)(2,1)S(1)}, bf16[128,4,256]{2,0,1:T(8,128)(2,1)S(1)}, u32[]{:S(2)}, u32[]{:S(2)}) %collective-permute-start.2) | collective-permute-done | bytes 262176 | tf_op jit(solution)/shard_map/while/body/eval_jaxpr/ppermute | solution.py:20
  670.9 12.5 collective-permute-done.3
  715.0 13.5 collective-permute-done.2
  791.8 13.5 collective-permute-done.2
  824.4 12.5 collective-permute-done.3
  862.9 14.1 fusion.123
  877.0 12.8 fusion.130
  910.9 79.0 %all-reduce.7.cloned.1.call-done = (f32[128,2048]{1,0:T(8,128)}, f32[128,2048]{1,0:T(8,128)}, f32[128,2048]{1,0:T(8,128)}) async-done(((f32[128,2048]{1,0:T(8,128)}, f32[128,2048]{1,0:T(8,128)}, f32[128,2048]{1,0:T(8,128)}), (f32[128,2048]{1,0:T(8,128)}, f32[128,2048]{1,0:T(8,128)}, f32[128,2048]{1,0:T(8,128)})) %all-reduce.7.cloned.1.call-update) | async-done | bytes 3145744 | tf_op jit(solution)/shard_map/psum | solution.py:218
  1017.4 13.3 fusion.100
  1032.3 15.1 fusion.121
  1047.5 37.6 %all-reduce.5.cloned.1.call-done = (f32[1024]{0:T(1024)}, f32[1024]{0:T(1024)}, f32[1024]{0:T(1024)}, f32[2048]{0:T(1024)}, f32[4096]{0:T(1024)}, /*index=5*/f32...) async-done(((f32[1024]{0:T(1024)}, f32[1024]{0:T(1024)}, f32[1024]{0:T(1024)}, f32[2048]{0:T(1024)}, f32[4096]{0:T(1024)}, /*index=5*/f32[2048]{0:T(1024)}, ...) | async-done | bytes 69648 | tf_op jit(solution)/shard_map/psum | solution.py:281
  1085.0 110.1 %reduce-scatter.9.cloned.1.call-done = f32[128,1024]{1,0:T(8,128)} async-done(((f32[2048,1024]{1,0:T(8,128)}), f32[128,1024]{1,0:T(8,128)}) %reduce-scatter.9.cloned.1.call-update) | async-done | bytes 524304 | tf_op jit(solution)/shard_map/reduce_scatter | solution.py:297
  1195.2 108.9 %reduce-scatter.7.cloned.1.call-done = f32[128,1024]{1,0:T(8,128)} async-done(((f32[2048,1024]{1,0:T(8,128)}), f32[128,1024]{1,0:T(8,128)}) %reduce-scatter.7.cloned.1.call-update) | async-done | bytes 524304 | tf_op jit(solution)/shard_map/reduce_scatter | solution.py:296
  1304.0 109.0 %reduce-scatter.11.cloned.1.call-done = f32[128,1024]{1,0:T(8,128)} async-done(((f32[2048,1024]{1,0:T(8,128)}), f32[128,1024]{1,0:T(8,128)}) %reduce-scatter.11.cloned.1.call-update) | async-done | bytes 524304 | tf_op jit(solution)/shard_map/reduce_scatter | solution.py:298
  1413.1 109.1 %reduce-scatter.13.cloned.1.call-done = f32[1024,128]{1,0:T(8,128)} async-done(((f32[1024,2048]{1,0:T(8,128)}), f32[1024,128]{1,0:T(8,128)}) %reduce-scatter.13.cloned.1.call-update) | async-done | bytes 524304 | tf_op jit(solution)/shard_map/reduce_scatter | solution.py:302
  1522.2 337.1 %reduce-scatter.15.cloned.1.call-done = f32[128,4096]{1,0:T(8,128)} async-done(((f32[2048,4096]{1,0:T(8,128)}), f32[128,4096]{1,0:T(8,128)}) %reduce-scatter.15.cloned.1.call-update) | async-done | bytes 2097168 | tf_op jit(solution)/shard_map/reduce_scatter | solution.py:299
  1859.2 336.5 %reduce-scatter.17.cloned.1.call-done = f32[4096,128]{1,0:T(8,128)} async-done(((f32[4096,2048]{1,0:T(8,128)}), f32[4096,128]{1,0:T(8,128)}) %reduce-scatter.17.cloned.1.call-update) | async-done | bytes 2097168 | tf_op jit(solution)/shard_map/reduce_scatter | solution.py:303
  (629 shorter events, 433.4 us)
Async XLA Ops:
  7.2 56.3 %all-gather.9.cloned.1.call-start = ((), (), s32[]{:S(2)}) async-start(), calls=%async_computation.6 | async-start | bytes 4456448 | tf_op jit(solution)/shard_map/all_gather | solution.py:157
  8.0 106.8 %all-gather.13.cloned.1.call-start = ((), (), s32[]{:S(2)}) async-start(), calls=%async_computation.8 | async-start | bytes 4456448 | tf_op jit(solution)/shard_map/all_gather | solution.py:156
  8.7 160.0 %all-gather.19.cloned.1.call-start = ((), (), s32[]{:S(2)}) async-start(), calls=%async_computation.11 | async-start | bytes 4456448 | tf_op jit(solution)/shard_map/all_gather | solution.py:162
  9.4 210.0 %all-gather.15.cloned.1.call-start = ((), (), s32[]{:S(2)}) async-start(), calls=%async_computation.9 | async-start | bytes 4456448 | tf_op jit(solution)/shard_map/all_gather | solution.py:158
  10.0 260.6 %all-gather.11.cloned.1.call-start = ((), (), s32[]{:S(2)}) async-start(), calls=%async_computation.7 | async-start | bytes 4456448 | tf_op jit(solution)/shard_map/all_gather | solution.py:205
  119.8 202.5 %all-gather.17.cloned.1.call-start = ((), (), s32[]{:S(2)}) async-start(), calls=%async_computation.10 | async-start | bytes 4456448 | tf_op jit(solution)/shard_map/all_gather | solution.py:206
  223.2 630.0 %all-gather.21.cloned.1.call-start = ((), (), s32[]{:S(2)}) async-start(), calls=%async_computation.12 | async-start | bytes 17825792 | tf_op jit(solution)/shard_map/all_gather | solution.py:159
  224.0 638.9 %all-gather.23.cloned.1.call-start = ((), (), s32[]{:S(2)}) async-start(), calls=%async_computation.13 | async-start | bytes 17825792 | tf_op jit(solution)/shard_map/all_gather | solution.py:163
  224.7 765.2 %all-reduce.7.cloned.1.call-start = ((), (), s32[]{:S(2)}) async-start(), calls=%async_computation.21 | async-start | bytes 6291456 | tf_op jit(solution)/shard_map/psum | solution.py:218
  403.4 32.2 %collective-permute-start.12 = (f32[128,4,256]{2,0,1:T(8,128)}, f32[128,4,256]{2,0,1:T(8,128)}, u32[]{:S(2)}, u32[]{:S(2)}) collective-permute-start(f32[128,4,256]{2,0,1:T(8,128)} %fusion.320), channel_id=1, source_target_pairs={{30,0},{0,2},{2,4},{4,6},{6,8},{8,10},{10,12},{12,14},{14,16},{16,... | collective-permute-start | bytes 1572872 | tf_op jit(solution)/shard_map/while/body/eval_jaxpr/ppermute | solution.py:20
  404.9 47.2 %collective-permute-start.8 = (f32[128,4,256]{2,0,1:T(8,128)}, f32[128,4,256]{2,0,1:T(8,128)}, u32[]{:S(2)}, u32[]{:S(2)}) collective-permute-start(f32[128,4,256]{2,0,1:T(8,128)} %fusion.312), channel_id=1, source_target_pairs={{30,0},{0,2},{2,4},{4,6},{6,8},{8,10},{10,12},{12,14},{14,16},{16,... | collective-permute-start | bytes 1572872 | tf_op jit(solution)/shard_map/while/body/eval_jaxpr/ppermute | solution.py:20
  414.5 46.0 %collective-permute-start.1 = (bf16[128,4,256]{2,0,1:T(8,128)(2,1)}, bf16[128,4,256]{2,0,1:T(8,128)(2,1)S(1)}, u32[]{:S(2)}, u32[]{:S(2)}) collective-permute-start(bf16[128,4,256]{2,0,1:T(8,128)(2,1)} %collective-permute-done), channel_id=1, source_target_pairs={{30,0},{0,2},{2,4},{4,6},{6,8},{8,10},{10,12},{12,14},{14,16},{16,... | collective-permute-start | bytes 786440 | tf_op jit(solution)/shard_map/while/body/eval_jaxpr/ppermute | solution.py:20
  423.0 45.9 %collective-permute-start.5 = (bf16[128,4,256]{2,0,1:T(8,128)(2,1)}, bf16[128,4,256]{2,0,1:T(8,128)(2,1)S(1)}, u32[]{:S(2)}, u32[]{:S(2)}) collective-permute-start(bf16[128,4,256]{2,0,1:T(8,128)(2,1)} %collective-permute-done.4), channel_id=1, source_target_pairs={{30,0},{0,2},{2,4},{4,6},{6,8},{8,10},{10,12},{12,14},{14,16},{16,... | collective-permute-start | bytes 786440 | tf_op jit(solution)/shard_map/while/body/eval_jaxpr/ppermute | solution.py:20
  436.9 46.6 %collective-permute-start.13 = (f32[128,4,256]{2,0,1:T(8,128)S(1)}, f32[128,4,256]{2,0,1:T(8,128)S(1)}, u32[]{:S(2)}, u32[]{:S(2)}) collective-permute-start(f32[128,4,256]{2,0,1:T(8,128)S(1)} %fusion.321), channel_id=1, source_target_pairs={{30,0},{0,2},{2,4},{4,6},{6,8},{8,10},{10,12},{12,14},{14,16},{16,... | collective-permute-start | bytes 1572872 | tf_op jit(solution)/shard_map/while/body/eval_jaxpr/ppermute | solution.py:20
  483.7 34.6 %collective-permute-start.10 = (f32[128,4,256]{2,0,1:T(8,128)S(1)}, f32[128,4,256]{2,0,1:T(8,128)S(1)}, u32[]{:S(2)}, u32[]{:S(2)}) collective-permute-start(f32[128,4,256]{2,0,1:T(8,128)S(1)} %add.1670), channel_id=1, source_target_pairs={{30,0},{0,2},{2,4},{4,6},{6,8},{8,10},{10,12},{12,14},{14,16},{16,... | collective-permute-start | bytes 1572872 | tf_op jit(solution)/shard_map/while/body/eval_jaxpr/ppermute | solution.py:20
  502.9 50.2 %collective-permute-start.15 = (f32[128,4,256]{2,0,1:T(8,128)S(1)}, f32[128,4,256]{2,0,1:T(8,128)S(1)}, u32[]{:S(2)}, u32[]{:S(2)}) collective-permute-start(f32[128,4,256]{2,0,1:T(8,128)S(1)} %add.1673), channel_id=1, source_target_pairs={{30,0},{0,2},{2,4},{4,6},{6,8},{8,10},{10,12},{12,14},{14,16},{16,... | collective-permute-start | bytes 1572872 | tf_op jit(solution)/shard_map/while/body/eval_jaxpr/ppermute | solution.py:20
  518.4 34.7 %collective-permute-start.11 = (f32[128,4,256]{2,0,1:T(8,128)S(1)}, f32[128,4,256]{2,0,1:T(8,128)S(1)}, u32[]{:S(2)}, u32[]{:S(2)}) collective-permute-start(f32[128,4,256]{2,0,1:T(8,128)S(1)} %add.1671), channel_id=1, source_target_pairs={{30,0},{0,2},{2,4},{4,6},{6,8},{8,10},{10,12},{12,14},{14,16},{16,... | collective-permute-start | bytes 1572872 | tf_op jit(solution)/shard_map/while/body/eval_jaxpr/ppermute | solution.py:20
  519.7 33.4 %collective-permute-start.7 = (bf16[128,4,256]{2,0,1:T(8,128)(2,1)S(1)}, bf16[128,4,256]{2,0,1:T(8,128)(2,1)S(1)}, u32[]{:S(2)}, u32[]{:S(2)}) collective-permute-start(bf16[128,4,256]{2,0,1:T(8,128)(2,1)S(1)} %collective-permute-done.6), channel_id=1, source_target_pairs={{30,0},{0,2},{2,4},{4,6},{6,8},{8,10},{10,12},{12,14},{14,16},{16,... | collective-permute-start | bytes 786440 | tf_op jit(solution)/shard_map/while/body/eval_jaxpr/ppermute | solution.py:20
  555.9 36.9 %collective-permute-start.12 = (f32[128,4,256]{2,0,1:T(8,128)}, f32[128,4,256]{2,0,1:T(8,128)}, u32[]{:S(2)}, u32[]{:S(2)}) collective-permute-start(f32[128,4,256]{2,0,1:T(8,128)} %fusion.320), channel_id=1, source_target_pairs={{30,0},{0,2},{2,4},{4,6},{6,8},{8,10},{10,12},{12,14},{14,16},{16,... | collective-permute-start | bytes 1572872 | tf_op jit(solution)/shard_map/while/body/eval_jaxpr/ppermute | solution.py:20
  557.2 52.5 %collective-permute-start.8 = (f32[128,4,256]{2,0,1:T(8,128)}, f32[128,4,256]{2,0,1:T(8,128)}, u32[]{:S(2)}, u32[]{:S(2)}) collective-permute-start(f32[128,4,256]{2,0,1:T(8,128)} %fusion.312), channel_id=1, source_target_pairs={{30,0},{0,2},{2,4},{4,6},{6,8},{8,10},{10,12},{12,14},{14,16},{16,... | collective-permute-start | bytes 1572872 | tf_op jit(solution)/shard_map/while/body/eval_jaxpr/ppermute | solution.py:20
  567.6 50.2 %collective-permute-start.1 = (bf16[128,4,256]{2,0,1:T(8,128)(2,1)}, bf16[128,4,256]{2,0,1:T(8,128)(2,1)S(1)}, u32[]{:S(2)}, u32[]{:S(2)}) collective-permute-start(bf16[128,4,256]{2,0,1:T(8,128)(2,1)} %collective-permute-done), channel_id=1, source_target_pairs={{30,0},{0,2},{2,4},{4,6},{6,8},{8,10},{10,12},{12,14},{14,16},{16,... | collective-permute-start | bytes 786440 | tf_op jit(solution)/shard_map/while/body/eval_jaxpr/ppermute | solution.py:20
  576.0 50.2 %collective-permute-start.5 = (bf16[128,4,256]{2,0,1:T(8,128)(2,1)}, bf16[128,4,256]{2,0,1:T(8,128)(2,1)S(1)}, u32[]{:S(2)}, u32[]{:S(2)}) collective-permute-start(bf16[128,4,256]{2,0,1:T(8,128)(2,1)} %collective-permute-done.4), channel_id=1, source_target_pairs={{30,0},{0,2},{2,4},{4,6},{6,8},{8,10},{10,12},{12,14},{14,16},{16,... | collective-permute-start | bytes 786440 | tf_op jit(solution)/shard_map/while/body/eval_jaxpr/ppermute | solution.py:20
  594.1 57.8 %collective-permute-start.13 = (f32[128,4,256]{2,0,1:T(8,128)S(1)}, f32[128,4,256]{2,0,1:T(8,128)S(1)}, u32[]{:S(2)}, u32[]{:S(2)}) collective-permute-start(f32[128,4,256]{2,0,1:T(8,128)S(1)} %fusion.321), channel_id=1, source_target_pairs={{30,0},{0,2},{2,4},{4,6},{6,8},{8,10},{10,12},{12,14},{14,16},{16,... | collective-permute-start | bytes 1572872 | tf_op jit(solution)/shard_map/while/body/eval_jaxpr/ppermute | solution.py:20
  611.0 41.1 %collective-permute-start.9 = (f32[128,4,256]{2,0,1:T(8,128)S(1)}, f32[128,4,256]{2,0,1:T(8,128)S(1)}, u32[]{:S(2)}, u32[]{:S(2)}) collective-permute-start(f32[128,4,256]{2,0,1:T(8,128)S(1)} %fusion.315), channel_id=1, source_target_pairs={{30,0},{0,2},{2,4},{4,6},{6,8},{8,10},{10,12},{12,14},{14,16},{16,... | collective-permute-start | bytes 1572872 | tf_op jit(solution)/shard_map/while/body/eval_jaxpr/ppermute | solution.py:20
  617.8 33.9 %collective-permute-start.2 = (bf16[128,4,256]{2,0,1:T(8,128)(2,1)S(1)}, bf16[128,4,256]{2,0,1:T(8,128)(2,1)S(1)}, u32[]{:S(2)}, u32[]{:S(2)}) collective-permute-start(bf16[128,4,256]{2,0,1:T(8,128)(2,1)S(1)} %collective-permute-done.1), channel_id=1, source_target_pairs={{30,0},{0,2},{2,4},{4,6},{6,8},{8,10},{10,12},{12,14},{14,16},{16,... | collective-permute-start | bytes 786440 | tf_op jit(solution)/shard_map/while/body/eval_jaxpr/ppermute | solution.py:20
  906.4 178.7 %all-reduce.5.cloned.1.call-start = ((), (), s32[]{:S(2)}) async-start(), calls=%async_computation.20 | async-start | bytes 139264 | tf_op jit(solution)/shard_map/psum | solution.py:281
  997.0 198.1 %reduce-scatter.9.cloned.1.call-start = ((), (), s32[]{:S(2)}) async-start(), calls=%async_computation.15 | async-start | bytes 8912896 | tf_op jit(solution)/shard_map/reduce_scatter | solution.py:297
  1001.8 302.2 %reduce-scatter.7.cloned.1.call-start = ((), (), s32[]{:S(2)}) async-start(), calls=%async_computation.14 | async-start | bytes 8912896 | tf_op jit(solution)/shard_map/reduce_scatter | solution.py:296
  1007.4 405.6 %reduce-scatter.11.cloned.1.call-start = ((), (), s32[]{:S(2)}) async-start(), calls=%async_computation.16 | async-start | bytes 8912896 | tf_op jit(solution)/shard_map/reduce_scatter | solution.py:298
  1012.1 510.0 %reduce-scatter.13.cloned.1.call-start = ((), (), s32[]{:S(2)}) async-start(), calls=%async_computation.17 | async-start | bytes 8912896 | tf_op jit(solution)/shard_map/reduce_scatter | solution.py:302
  1016.8 842.5 %reduce-scatter.15.cloned.1.call-start = ((), (), s32[]{:S(2)}) async-start(), calls=%async_computation.18 | async-start | bytes 35651584 | tf_op jit(solution)/shard_map/reduce_scatter | solution.py:299
  1030.7 1165.1 %reduce-scatter.17.cloned.1.call-start = ((), (), s32[]{:S(2)}) async-start(), calls=%async_computation.19 | async-start | bytes 35651584 | tf_op jit(solution)/shard_map/reduce_scatter | solution.py:303
  (93 other events, 2367.1 us)
Sparse Core Ops, SparseCore 0:
  10.2 53.2 all-gather.8
  65.7 49.0 all-gather.12
  116.9 51.6 all-gather.18
  170.7 48.7 all-gather.14
  221.5 49.0 all-gather.10
  273.2 49.0 all-gather.16
  324.5 131.9 all-gather.20
  458.6 183.1 all-gather.22
  906.5 83.3 all-reduce.6
  997.2 87.8 all-reduce.4
  1089.7 105.4 reduce-scatter.8
  1199.6 104.3 reduce-scatter.6
  1308.7 104.3 reduce-scatter.10
  1417.6 104.5 reduce-scatter.12
  1526.9 332.3 reduce-scatter.14
  1863.9 331.8 reduce-scatter.16
where the time goes:
time: 2220 us
  waiting for transfers between devices  1900 us (86%)
  matrix products  214 us (10%)
  other arithmetic  43.8 us (2%)
  local copies, waits for them, and re-layouts  35.1 us (2%)
    ppermute x64, waiting for transfers between devices, passed_along(): return lax.ppermute(block, axis, route)  377 us
    reduce_scatter x1, waiting for transfers between devices, shards(): lax.psum_scatter(grad_w_up, 'ctx', scatter_dimension=0, tiled=True)  337 us
    reduce_scatter x1, waiting for transfers between devices, shards(): lax.psum_scatter(grad_w_down, 'ctx', scatter_dimension=1, tiled=True)  337 us
    reduce_scatter x1, waiting for transfers between devices, shards(): lax.psum_scatter(grad_w_key, 'ctx', scatter_dimension=0, tiled=True)  110 us
    reduce_scatter x1, waiting for transfers between devices, shards(): lax.psum_scatter(grad_w_out, 'ctx', scatter_dimension=1, tiled=True)  109 us
    reduce_scatter x1, waiting for transfers between devices, shards(): lax.psum_scatter(grad_w_value, 'ctx', scatter_dimension=0, tiled=True)  109 us
    reduce_scatter x1, waiting for transfers between devices, shards(): lax.psum_scatter(grad_w_query, 'ctx', scatter_dimension=0, tiled=True)  109 us
    psum x1, waiting for transfers between devices, shards(): branches = lax.psum(branches, 'tp')  79 us
  transfers between devices with their start and end apart: 80, of which 62 were waited for; matrix products, arithmetic and copies ran while one was open for 10% of the time, Pallas kernels for 0%

commit v1 on v0

v1 whole, which is shorter than its diff:
```python
import functools
import math

import jax
import jax.numpy as jnp
from jax import lax
from jax.experimental import pallas as pl
from jax.experimental.pallas import tpu as pltpu
from jax.sharding import PartitionSpec as P

HEADS = 8
HD = 256
ROT = 64
CHUNK = 256

norm_epsilon = 1e-05
BF = jnp.bfloat16
F32 = jnp.float32
MESH = pl.DeviceIdType.MESH


def mm(a, b):
    return jnp.dot(a, b, preferred_element_type=F32)


def mm_tn(a, b):
    return lax.dot_general(a, b, (((0,), (0,)), ((), ())), preferred_element_type=F32)


def mm_nt(a, b):
    return lax.dot_general(a, b, (((1,), (1,)), ((), ())), preferred_element_type=F32)


class Place:
    def __init__(self, depth_size, group):
        self.depth_size = depth_size
        self.group = group
        self.bits = group.bit_length() - 1
        self.ctx = lax.axis_index("ctx")
        self.tp = lax.axis_index("tp")
        self.depth = self.ctx // group
        self.member = self.ctx % group
        slot = 0
        for stage in range(self.bits):
            slot = slot + self.bit(stage) * 2**stage
        self.slot = slot

    def bit(self, stage):
        return (self.member // 2 ** (self.bits - 1 - stage)) % 2

    def along(self, step):
        return {"ctx": lax.rem(self.depth + step, self.depth_size) * self.group + self.member}

    def across(self, stage):
        reach = 2 ** (self.bits - 1 - stage)
        return {"ctx": self.ctx + (1 - 2 * self.bit(stage)) * reach}

    def twin(self):
        return {"tp": 1 - self.tp}

    def base(self, stage):
        return (self.slot // 2**stage) * 2**stage

    def greet(self, devices):
        barrier = pltpu.get_barrier_semaphore()
        for device in devices:
            pl.semaphore_signal(barrier, inc=1, device_id=device, device_id_type=MESH)
        pl.semaphore_wait(barrier, len(devices))

    def everyone(self):
        return (
            [self.along(step) for step in range(1, self.depth_size)]
            + [self.across(stage) for stage in range(self.bits)]
            + [self.twin()]
        )


def remote(src, dst, send, recv, device):
    copy = pltpu.make_async_remote_copy(
        src_ref=src, dst_ref=dst, send_sem=send, recv_sem=recv, device_id=device, device_id_type=MESH
    )
    copy.start()
    return copy


def local(src, dst, sem):
    copy = pltpu.make_async_copy(src, dst, sem)
    copy.start()
    return copy


def gather_kernel(depth_size, group, x_in, dy_in, w_in, x_out, dy_out, w_out, tz_s, tz_r, tx_s, tx_r, t_l, z_s, z_r, z_l, g_s, g_r):
    at = Place(depth_size, group)
    at.greet(at.everyone())
    rows, half = x_in.shape[1:]
    sent = []
    mine = pl.ds(pl.multiple_of(at.depth * rows, rows), rows)
    my_cols = pl.ds(pl.multiple_of(at.tp * half, half), half)

    def token_start(i, src, dst):
        copies = [
            remote(src.at[at.tp], dst.at[mine, my_cols], tz_s.at[i, s], tz_r.at[i, s], at.along(s))
            for s in range(1, depth_size)
        ]
        copies.append(local(src.at[at.tp], dst.at[mine, my_cols], t_l.at[i]))
        return copies

    def token_swap(i, copies, dst):
        for copy in copies[:-1]:
            copy.wait_recv()
            sent.append(copy)
        copies[-1].wait()
        return remote(dst.at[:, my_cols], dst.at[:, my_cols], tx_s.at[i], tx_r.at[i], at.twin())

    chunks = w_in.shape[0]

    def z_start(k):
        copies = [
            remote(
                w_in.at[k, lax.rem(at.depth + s, depth_size)],
                w_out.at[k, at.slot, at.depth],
                z_s.at[k, s],
                z_r.at[k, s],
                at.along(s),
            )
            for s in range(1, depth_size)
        ]
        copies.append(local(w_in.at[k, at.depth], w_out.at[k, at.slot, at.depth], z_l.at[k]))
        return copies

    def z_wait(copies):
        for copy in copies[:-1]:
            copy.wait_recv()
            sent.append(copy)
        copies[-1].wait()

    def g_start(k, stage):
        held = pl.ds(at.base(stage), 2**stage)
        return remote(
            w_out.at[k, held], w_out.at[k, held], g_s.at[k, stage], g_r.at[k, stage], at.across(stage)
        )

    ahead = 2
    tokens = [token_start(0, x_in, x_out)]
    z_copies = {k: z_start(k) for k in range(min(ahead, chunks))}
    stages = {}
    swaps = []
    for step in range(chunks + at.bits):
        if step < chunks:
            z_wait(z_copies[step])
            stages[step] = [g_start(step, 0)]
            if step + ahead < chunks:
                z_copies[step + ahead] = z_start(step + ahead)
            if step == 0:
                swaps.append(token_swap(0, tokens[0], x_out))
                tokens.append(token_start(1, dy_in, dy_out))
            if step == 1:
                swaps.append(token_swap(1, tokens[1], dy_out))
        for stage in range(1, at.bits + 1):
            k = step - stage
            if 0 <= k < chunks:
                stages[k][stage - 1].wait_recv()
                if stage < at.bits:
                    stages[k].append(g_start(k, stage))
    for swap in swaps:
        swap.wait()
    for k in range(chunks):
        for copy in stages[k]:
            copy.wait_send()
    for copy in sent:
        copy.wait_send()


def gather_all(depth_size, group, x_halves, dy_halves, weights):
    tp, rows, half = x_halves.shape
    chunks, _, depth_rows, width = weights.shape
    bits = group.bit_length() - 1
    dma = pltpu.SemaphoreType.DMA
    hbm = pl.BlockSpec(memory_space=pl.ANY)
    tokens = jax.ShapeDtypeStruct((depth_size * rows, tp * half), BF)
    return pl.pallas_call(
        functools.partial(gather_kernel, depth_size, group),
        out_shape=(
            tokens,
            tokens,
            jax.ShapeDtypeStruct((chunks, group, depth_size, depth_rows, width), BF),
        ),
        in_specs=[hbm] * 3,
        out_specs=(hbm, hbm, hbm),
        scratch_shapes=[
            dma((2, depth_size)),
            dma((2, depth_size)),
            dma((2,)),
            dma((2,)),
            dma((2,)),
            dma((chunks, depth_size)),
            dma((chunks, depth_size)),
            dma((chunks,)),
            dma((chunks, bits)),
            dma((chunks, bits)),
        ],
        compiler_params=pltpu.CompilerParams(collective_id=0, has_side_effects=True),
    )(x_halves, dy_halves, weights)


def share_kernel(depth_size, group, kv_in, kv_out, send, recv, loc):
    at = Place(depth_size, group)
    at.greet([at.across(stage) for stage in range(at.bits)])
    local(kv_in, kv_out.at[at.slot], loc).wait()
    copies = []
    for stage in range(at.bits):
        held = pl.ds(at.base(stage), 2**stage)
        copy = remote(kv_out.at[held], kv_out.at[held], send.at[stage], recv.at[stage], at.across(stage))
        copy.wait_recv()
        copies.append(copy)
    for copy in copies:
        copy.wait_send()


def share_group(depth_size, group, kv):
    bits = group.bit_length() - 1
    dma = pltpu.SemaphoreType.DMA
    hbm = pl.BlockSpec(memory_space=pl.ANY)
    return pl.pallas_call(
        functools.partial(share_kernel, depth_size, group),
        out_shape=jax.ShapeDtypeStruct((group,) + kv.shape, BF),
        in_specs=[hbm],
        out_specs=hbm,
        scratch_shapes=[dma((bits,)), dma((bits,)), dma],
        compiler_params=pltpu.CompilerParams(collective_id=1, has_side_effects=True),
    )(kv)


def fold_kernel(depth_size, group, g_in, total, landing, send, recv):
    at = Place(depth_size, group)
    at.greet([at.across(stage) for stage in range(at.bits)])
    for stage in reversed(range(at.bits)):
        size = 2**stage
        own = at.base(stage)
        other = own + (1 - 2 * at.bit(stage)) * size
        source = g_in if stage == at.bits - 1 else total
        copy = remote(
            source.at[pl.ds(other, size)],
            landing.at[pl.ds(size - 1, size)],
            send.at[stage],
            recv.at[stage],
            at.across(stage),
        )
        copy.wait()

        def add(i, _):
            total[own + i] = (
                source[own + i].astype(F32) + landing[size - 1 + i].astype(F32)
            ).astype(BF)
            return 0

        lax.fori_loop(0, size, add, 0)


def fold_group(depth_size, group, grads):
    bits = group.bit_length() - 1
    dma = pltpu.SemaphoreType.DMA
    vmem = pl.BlockSpec(memory_space=pltpu.VMEM)
    return pl.pallas_call(
        functools.partial(fold_kernel, depth_size, group),
        out_shape=jax.ShapeDtypeStruct(grads.shape, BF),
        in_specs=[vmem],
        out_specs=vmem,
        scratch_shapes=[
            pltpu.VMEM((group - 1,) + grads.shape[1:], BF),
            dma((bits,)),
            dma((bits,)),
        ],
        compiler_params=pltpu.CompilerParams(
            collective_id=2, has_side_effects=True, vmem_limit_bytes=60 << 20
        ),
    )(grads)


def reduce_kernel(depth_size, group, out_in, back_in, g_in, out_sum, back_sum, g_out, total, landing, g_s, g_r, z_s, z_r, z_l, t_acc, t_swap, t_land, tx_s, tx_r, tz_s, tz_r, ty_s, ty_r):
    at = Place(depth_size, group)
    at.greet(at.everyone())
    chunks = g_in.shape[0]
    depth_rows = g_in.shape[3]
    rows = out_sum.shape[0]
    half = t_acc.shape[2]
    last = at.bits - 1
    sent = []

    def g_start(k, stage):
        size = 2**stage
        other = at.base(stage) + (1 - 2 * at.bit(stage)) * size
        source = g_in.at[k] if stage == last else total.at[k]
        return remote(
            source.at[pl.ds(other, size)],
            landing.at[k, pl.ds(size - 1, size)],
            g_s.at[k, stage],
            g_r.at[k, stage],
            at.across(stage),
        )

    def g_finish(k, stage, copy):
        copy.wait_recv()
        sent.append(copy)
        size = 2**stage
        own = at.base(stage)
        source = g_in.at[k] if stage == last else total.at[k]

        def add(i, _):
            j = i // depth_size
            z = i % depth_size
            total[k, own + j, z] = (
                source[own + j, z].astype(F32) + landing[k, size - 1 + j, z].astype(F32)
            ).astype(BF)
            return 0

        lax.fori_loop(0, size * depth_size, add, 0)

    def z_start(k):
        copies = [
            remote(
                total.at[k, at.slot, lax.rem(at.depth + s, depth_size)],
                g_out.at[k, at.depth],
                z_s.at[k, s],
                z_r.at[k, s],
                at.along(s),
            )
            for s in range(1, depth_size)
        ]
        copies.append(local(total.at[k, at.slot, at.depth], g_out.at[k, at.depth], z_l.at[k]))
        return copies

    my_cols = pl.ds(pl.multiple_of(at.tp * half, half), half)
    her_cols = pl.ds(pl.multiple_of((1 - at.tp) * half, half), half)

    def token_first(i, src):
        return remote(src.at[:, her_cols], t_swap.at[i], tx_s.at[i], tx_r.at[i], at.twin())

    def token_second(i, src, copy):
        copy.wait_recv()
        sent.append(copy)

        def add(z, _):
            block = pl.ds(pl.multiple_of(z * rows, rows), rows)
            t_acc[i, block, :] = (
                src[block, my_cols].astype(F32) + t_swap[i, block, :].astype(F32)
            ).astype(BF)
            return 0

        lax.fori_loop(0, depth_size, add, 0)
        copies = []
        for s in range(1, depth_size):
            there = lax.rem(at.depth + s, depth_size)
            block = pl.ds(pl.multiple_of(there * rows, rows), rows)
            copies.append(
                remote(
                    t_acc.at[i, block, :], t_land.at[i, s - 1], tz_s.at[i, s], tz_r.at[i, s], at.along(s)
                )
            )
        return copies

    def token_third(i, dst, copies):
        for copy in copies:
            copy.wait_recv()
            sent.append(copy)
        mine = pl.ds(pl.multiple_of(at.depth * rows, rows), rows)
        value = t_acc[i, mine, :].astype(F32)
        for s in range(1, depth_size):
            value = value + t_land[i, s - 1].astype(F32)
        dst[:, my_cols] = value.astype(BF)
        return remote(dst.at[:, my_cols], dst.at[:, my_cols], ty_s.at[i], ty_r.at[i], at.twin())

    firsts = [token_first(0, out_in), token_first(1, back_in)]
    copies_of = {k: [g_start(k, last)] for k in range(chunks)}
    z_copies = {}
    seconds = []
    thirds = []
    for step in range(chunks + at.bits):
        for back in range(at.bits):
            k = step - back
            stage = last - back
            if 0 <= k < chunks:
                g_finish(k, stage, copies_of[k][back])
                if stage > 0:
                    copies_of[k].append(g_start(k, stage - 1))
                else:
                    z_copies[k] = z_start(k)
        if step == 1:
            seconds.append(token_second(0, out_in, firsts[0]))
        if step == 2:
            seconds.append(token_second(1, back_in, firsts[1]))
        if step == 4:
            thirds.append(token_third(0, out_sum, seconds[0]))
        if step == 5:
            thirds.append(token_third(1, back_sum, seconds[1]))
    for k in range(chunks):
        for copy in z_copies[k][:-1]:
            copy.wait()
        z_copies[k][-1].wait()
    for copy in thirds:
        copy.wait()
    for copy in sent:
        copy.wait_send()


def reduce_all(depth_size, group, out_part, back_part, grads):
    chunks, _, _, depth_rows, width = grads.shape
    all_rows, columns = out_part.shape
    rows = all_rows // depth_size
    half = columns // 2
    bits = group.bit_length() - 1
    dma = pltpu.SemaphoreType.DMA
    vmem = pl.BlockSpec(memory_space=pltpu.VMEM)
    tokens = jax.ShapeDtypeStruct((rows, columns), BF)
    return pl.pallas_call(
        functools.partial(reduce_kernel, depth_size, group),
        out_shape=(tokens, tokens, jax.ShapeDtypeStruct((chunks, depth_size, depth_rows, width), BF)),
        in_specs=[vmem] * 3,
        out_specs=(vmem, vmem, vmem),
        scratch_shapes=[
            pltpu.VMEM((chunks, group, depth_size, depth_rows, width), BF),
            pltpu.VMEM((chunks, group - 1, depth_size, depth_rows, width), BF),
            dma((chunks, bits)),
            dma((chunks, bits)),
            dma((chunks, depth_size)),
            dma((chunks, depth_size)),
            dma((chunks,)),
            pltpu.VMEM((2, all_rows, half), BF),
            pltpu.VMEM((2, all_rows, half), BF),
            pltpu.VMEM((2, depth_size - 1, rows, half), BF),
            dma((2,)),
            dma((2,)),
            dma((2, depth_size)),
            dma((2, depth_size)),
            dma((2,)),
            dma((2,)),
        ],
        compiler_params=pltpu.CompilerParams(
            collective_id=3, has_side_effects=True, vmem_limit_bytes=60 << 20
        ),
    )(out_part, back_part, grads)


def rotate(values, cosine, sine_table):
    half_rot = ROT // 2
    leading = values[..., :half_rot]
    trailing = values[..., half_rot:ROT]
    return jnp.concatenate(
        [
            leading * cosine - trailing * sine_table,
            trailing * cosine + leading * sine_table,
            values[..., ROT:],
        ],
        -1,
    )


def rope_tables(positions):
    freqs = 10000.0 ** (-(2.0 * jnp.arange(ROT // 2, dtype=F32)) / ROT)
    angles = positions.astype(F32)[:, None] * freqs[None, :]
    return (jnp.cos(angles), jnp.sin(angles))


def gelu_parts(values):
    gate = 0.5 * (1.0 + lax.erf(values * math.sqrt(0.5)))
    slope = gate + values * jnp.exp(-0.5 * values * values) * (1.0 / math.sqrt(2.0 * math.pi))
    return values * gate, slope


def shards(
    layer_input,
    block_order,
    attn_gain,
    attn_shift,
    mlp_gain,
    mlp_shift,
    w_query,
    b_query,
    w_key,
    b_key,
    w_value,
    b_value,
    w_out,
    b_out,
    w_up,
    b_up,
    w_down,
    b_down,
    out_grad,
):
    rows, width = layer_input.shape
    ctx_size = lax.axis_size("ctx")
    tp_size = lax.axis_size("tp")
    depth_size = HEADS // tp_size
    group = ctx_size // depth_size
    bits = group.bit_length() - 1
    depth_rows = width // ctx_size
    hidden_width = w_up.shape[1] // depth_size
    ff_chunks = hidden_width // CHUNK
    at = Place(depth_size, group)
    block_rows = rows // 2

    def permuted(array):
        lead = array.shape[:-1]
        n = len(lead)
        split = array.reshape(lead + (depth_size,) + (2,) * bits + (depth_rows,))
        order = tuple(range(n)) + tuple(n + 1 + b for b in reversed(range(bits))) + (n, n + 1 + bits)
        return split.transpose(order).reshape(lead + (width,))

    def restored(array):
        lead = array.shape[:-1]
        n = len(lead)
        split = array.reshape(lead + (2,) * bits + (depth_size, depth_rows))
        order = tuple(range(n)) + (n + bits,) + tuple(n + b for b in reversed(range(bits))) + (n + bits + 1,)
        return split.transpose(order).reshape(lead + (width,))

    def slot_members():
        table = []
        for slot in range(group):
            member = 0
            for stage in range(bits):
                member += ((slot >> stage) & 1) << (bits - 1 - stage)
            table.append(member)
        return table

    blocks = block_order.reshape(depth_size, group, 2)
    order = jnp.stack([blocks[:, m] for m in slot_members()], 0)
    place = order[..., None] * block_rows + jnp.arange(block_rows, dtype=jnp.int32)
    key_place = place.reshape(group * depth_size * rows)
    token_total = depth_size * rows
    query_place = lax.dynamic_slice_in_dim(key_place, at.slot * token_total, token_total)
    cosine, sine_table = rope_tables(query_place)

    inputs32 = layer_input.astype(F32)
    centered = inputs32 - jnp.mean(inputs32, -1, keepdims=True)
    inverse = lax.rsqrt(jnp.mean(centered * centered, -1, keepdims=True) + norm_epsilon)
    normal32 = centered * inverse

    def halves(array):
        return permuted(array).reshape(rows, tp_size, width // tp_size).transpose(1, 0, 2)

    def by_head(weight):
        return weight.reshape(depth_rows, depth_size, HD).transpose(1, 0, 2)

    def by_chunk(weight):
        return weight.reshape(depth_rows, depth_size, ff_chunks, CHUNK).transpose(2, 1, 0, 3)

    weights = jnp.concatenate(
        [
            jnp.concatenate([by_head(w_query), by_head(w_key)], -1)[None],
            jnp.concatenate([by_head(w_value), by_head(w_out.T)], -1)[None],
            jnp.concatenate([by_chunk(w_up), by_chunk(w_down.T)], -1),
        ],
        0,
    )
    normal, grad, gathered = gather_all(
        depth_size, group, halves(normal32.astype(BF)), halves(out_grad), weights
    )
    full = gathered.reshape(2 + ff_chunks, width, 2 * HD)
    gain_a, shift_a, gain_m, shift_m = permuted(jnp.stack([attn_gain, attn_shift, mlp_gain, mlp_shift]))
    normal_tokens = normal.astype(F32)
    attn_in = (normal_tokens * gain_a + shift_a).astype(BF)
    mlp_in = (normal_tokens * gain_m + shift_m).astype(BF)

    def own_part(vector, size):
        return lax.dynamic_slice_in_dim(vector, at.depth * size, size)

    query_key = mm(attn_in, full[0])
    query = rotate(query_key[:, :HD] + own_part(b_query, HD), cosine, sine_table).astype(BF)
    keys = rotate(query_key[:, HD:] + own_part(b_key, HD), cosine, sine_table).astype(BF)
    values = (mm(attn_in, full[1, :, :HD]) + own_part(b_value, HD)).astype(BF)
    out_t = full[1, :, HD:]
    shared = share_group(depth_size, group, jnp.concatenate([keys, values], -1))
    shared = shared.reshape(group * token_total, 2 * HD)
    all_keys, all_values = shared[:, :HD], shared[:, HD:]
    score_scale = 1.0 / math.sqrt(HD)
    scores = mm_nt(query, all_keys) * score_scale
    allowed = key_place[None, :] <= query_place[:, None]
    scores = jnp.where(allowed, scores, -1e30)
    top = jnp.max(scores, -1, keepdims=True)
    raw = jnp.exp(scores - top)
    probs = raw / jnp.sum(raw, -1, keepdims=True)
    probs_low = probs.astype(BF)
    attended = mm(probs_low, all_values)
    attn_low = attended.astype(BF)

    head_grad = mm(grad, out_t).astype(BF)
    delta = jnp.sum(head_grad.astype(F32) * attended, -1, keepdims=True)
    value_part = mm_tn(probs_low, head_grad)
    score_grad = (probs * (mm_nt(head_grad, all_values) - delta) * score_scale).astype(BF)
    query_acc = mm(score_grad, all_keys)
    key_part = mm_tn(score_grad, query)
    parts = jnp.concatenate([key_part, value_part], -1).astype(BF)
    folded = fold_group(depth_size, group, parts.reshape(group, token_total, 2 * HD))
    own_grads = lax.dynamic_index_in_dim(folded, at.slot, 0, keepdims=False).astype(F32)
    query_lin = rotate(query_acc, cosine, -sine_table)
    key_lin = rotate(own_grads[:, :HD], cosine, -sine_table)
    value_lin = own_grads[:, HD:]
    query_low, key_low, value_low = query_lin.astype(BF), key_lin.astype(BF), value_lin.astype(BF)
    query_key_low = jnp.concatenate([query_low, key_low], -1)
    attn_back = mm_nt(query_key_low, full[0]) + mm_nt(value_low, full[1, :, :HD])
    grad_chunks = [
        mm_tn(attn_in, query_key_low).astype(BF),
        jnp.concatenate([mm_tn(attn_in, value_low), mm_tn(grad, attn_low)], -1).astype(BF),
    ]

    branches = mm_nt(attn_low, out_t)
    mlp_back = jnp.zeros((token_total, width), F32)
    bias_up = own_part(b_up, hidden_width).reshape(ff_chunks, CHUNK)
    up_sums = []
    for i in range(ff_chunks):
        up, down_t = full[2 + i, :, :CHUNK], full[2 + i, :, CHUNK:]
        activated, slope = gelu_parts(mm(mlp_in, up) + bias_up[i])
        hidden = activated.astype(BF)
        up_grad = mm(grad, down_t) * slope
        up_sums.append(jnp.sum(up_grad, 0))
        up_low = up_grad.astype(BF)
        branches = branches + mm_nt(hidden, down_t)
        mlp_back = mlp_back + mm_nt(up_low, up)
        grad_chunks.append(jnp.concatenate([mm_tn(mlp_in, up_low), mm_tn(grad, hidden)], -1).astype(BF))

    normal_tokens2 = normal.astype(F32)
    back = attn_back * gain_a + mlp_back * gain_m
    grads = jnp.stack(grad_chunks).reshape(2 + ff_chunks, group, depth_size, depth_rows, 2 * HD)
    norm_sums = restored(
        jnp.stack(
            [
                jnp.sum(attn_back * normal_tokens2, 0),
                jnp.sum(attn_back, 0),
                jnp.sum(mlp_back * normal_tokens2, 0),
                jnp.sum(mlp_back, 0),
            ]
        )
    )
    own_biases = jnp.concatenate(
        [jnp.sum(query_lin, 0), jnp.sum(key_lin, 0), jnp.sum(value_lin, 0)] + up_sums
    )
    spread = jnp.where(
        jnp.arange(depth_size, dtype=jnp.int32)[:, None] == at.depth, own_biases[None, :], 0.0
    )
    norm_sums = lax.psum(norm_sums, ("ctx", "tp"))
    grad32 = out_grad.astype(F32)
    spread, bias_grad = lax.psum((spread, jnp.sum(grad32, 0)), "ctx")

    out_sum, back_sum, grad_shares = reduce_all(
        depth_size, group, branches.astype(BF), back.astype(BF), grads
    )
    layer_output = (inputs32 + restored(out_sum).astype(F32) + b_out + b_down).astype(BF)
    back_total = restored(back_sum).astype(F32)
    input_grad = grad32 + inverse * (
        back_total
        - jnp.mean(back_total, -1, keepdims=True)
        - normal32 * jnp.mean(back_total * normal32, -1, keepdims=True)
    )

    def from_head(share):
        return share.transpose(1, 0, 2).reshape(depth_rows, depth_size * HD).astype(F32)

    def from_chunk(share):
        return share.transpose(2, 1, 0, 3).reshape(depth_rows, depth_size * hidden_width).astype(F32)

    return (
        layer_output,
        input_grad,
        from_head(grad_shares[0, :, :, :HD]),
        from_head(grad_shares[0, :, :, HD:]),
        from_head(grad_shares[1, :, :, :HD]),
        from_head(grad_shares[1, :, :, HD:]).T,
        from_chunk(grad_shares[2:, :, :, :CHUNK]),
        from_chunk(grad_shares[2:, :, :, CHUNK:]).T,
        spread[:, :HD].reshape(-1),
        spread[:, HD : 2 * HD].reshape(-1),
        spread[:, 2 * HD : 3 * HD].reshape(-1),
        bias_grad,
        spread[:, 3 * HD :].reshape(-1),
        bias_grad,
        norm_sums[0],
        norm_sums[1],
        norm_sums[2],
        norm_sums[3],
    )


def solution(mesh):
    in_specs = (
        P("ctx", None),
        P(),
        P(),
        P(),
        P(),
        P(),
        P("ctx", "tp"),
        P("tp"),
        P("ctx", "tp"),
        P("tp"),
        P("ctx", "tp"),
        P("tp"),
        P("tp", "ctx"),
        P(),
        P("ctx", "tp"),
        P("tp"),
        P("tp", "ctx"),
        P(),
        P("ctx", None),
    )
    out_specs = (
        P("ctx", None),
        P("ctx", None),
        P("ctx", "tp"),
        P("ctx", "tp"),
        P("ctx", "tp"),
        P("tp", "ctx"),
        P("ctx", "tp"),
        P("tp", "ctx"),
        P("tp"),
        P("tp"),
        P("tp"),
        P(),
        P("tp"),
        P(),
        P(),
        P(),
        P(),
        P(),
    )
    return jax.shard_map(shards, mesh=mesh, in_specs=in_specs, out_specs=out_specs, check_vma=False)
```

time: 2220 us -> 617 us (0.28)
  waiting for transfers between devices: 1900 us -> 0 us
  Pallas kernels: 0 us -> 339 us
  matrix products: 214 us -> 73.6 us
  blocking collectives: 0 us -> 101 us
    reduce_scatter x6 -> x0, waiting for transfers between devices: 1110 us -> none  [the longest x1 337 us: shards(): lax.psum_scatter(grad_w_up, 'ctx', scatter_dimension=0, tiled=True)]
    ppermute x64 -> x0, waiting for transfers between devices: 377 us -> none  [passed_along(): return lax.ppermute(block, axis, route)]
    pallas_call x0 -> x4, Pallas kernels: none -> 339 us  [the longest x1 149 us: reduce_all(): pl.pallas_call(functools.partial(reduce_kernel, depth_size, group), out_s...]
    all_gather x8 -> x0, waiting for transfers between devices: 289 us -> none  [the longest x1 51.7 us: shards(): lax.all_gather(values, 'ctx', axis=0, tiled=True)]
    dot_general x130 -> x39, matrix products: 214 us -> 73.6 us  [the longest x13 36.3 us: mm_nt(): lax.dot_general(a, b, (((1,), (1,)), ((), ())), preferred_element_type=F32)]
    psum x2 -> x0, waiting for transfers between devices: 117 us -> none  [the longest x1 79 us: shards(): branches = lax.psum(branches, 'tp')]
    psum x0 -> x2, blocking collectives: none -> 101 us  [the longest x1 63.5 us: shards(): spread, bias_grad = lax.psum((spread, jnp.sum(grad32, 0)), 'ctx')]
    add x90 -> x2, other arithmetic: 23.1 us -> 0.16 us  [the longest x1 0.08 us: shards(): order[..., None] * block_rows + jnp.arange(block_rows, dtype=jnp.int32)]
  transfers between devices with their start and end apart: 80 -> 0, of which waited for: 62 -> 0; matrix products, arithmetic and copies ran while one was open for 10% -> 0% of each run, Pallas kernels for 0% -> 0%
where the time goes in v1:
time: 617 us; the launch traced here: 606 us
  Pallas kernels  339 us (55%)
  blocking collectives  101 us (16%)
  matrix products  73.6 us (12%)
  local copies, waits for them, and re-layouts  55.1 us (9%)
  other arithmetic  36 us (6%)
    pallas_call x1, Pallas kernels, reduce_all(): pl.pallas_call(functools.partial(reduce_kernel, depth_size, group), out_s...  149 us
    pallas_call x1, Pallas kernels, gather_all(): pl.pallas_call(functools.partial(gather_kernel, depth_size, group), out_s...  135 us
    psum x1, blocking collectives, shards(): spread, bias_grad = lax.psum((spread, jnp.sum(grad32, 0)), 'ctx')  63.5 us
    psum x1, blocking collectives, shards(): norm_sums = lax.psum(norm_sums, ('ctx', 'tp'))  37 us
    dot_general x13, matrix products, mm_nt(): lax.dot_general(a, b, (((1,), (1,)), ((), ())), preferred_element_type=F32)  36.3 us
    pallas_call x1, Pallas kernels, share_group(): pl.pallas_call(functools.partial(share_kernel, depth_size, group), out_sh...  34.2 us
    dot_general x13, matrix products, mm(): return jnp.dot(a, b, preferred_element_type=F32)  26 us
    unnamed x166, local copies, waits for them, and re-layouts  20.2 us

profile of v1, /device:TPU:0, one launch (start us, length us, event | category | flops | bytes accessed | tf_op | source)
XLA Modules:
  0.0 606.5 jit_solution(8493801072977433424)
XLA Ops:
  16.8 135.4 %shard_map.322 = (bf16[512,2048]{1,0:T(8,128)(2,1)}, bf16[512,2048]{1,0:T(8,128)(2,1)}, bf16[6,4,4,128,512]{4,3,2,1,0:T(8,128)(2,1)}) custom-call(bf16[2,128,1024]{2,1,0:T(8,128)(2,1)} %bitcast.239, bf16[2,128,1024]{2,1,0:T(8,128)(2,1)} %bitcast.240, bf16[6,4,128,512]{3,2,1,0:T(8,128)(2,1)} %maximum_maximum_fusion.w_in), custom_call_target="tpu_custom_call" | custom-call | tf_op jit(solution)/shard_map/pallas_call | solution.py:181
  153.6 2.6 convolution_add_fusion.2
  156.2 4.2 fusion.31
  162.4 4.2 fusion.29
  169.4 2.1 fusion.13
  180.2 34.2 %shard_map.323 = bf16[4,512,512]{2,1,0:T(8,128)(2,1)} custom-call(bf16[512,512]{1,0:T(8,128)(2,1)} %pad_maximum_fusion.1.kv_in), custom_call_target="tpu_custom_call" | custom-call | tf_op jit(solution)/shard_map/pallas_call | solution.py:224
  214.5 2.2 fusion.116
  219.9 2.1 fusion.25
  224.1 2.2 fusion.27
  226.3 2.1 convolution_add_fusion.1
  228.9 4.1 add_convert_fusion.1.out_in
  233.0 2.6 fusion.119
  235.6 2.1 fusion.30
  237.7 2.6 fusion.117
  240.3 2.1 fusion.26
  242.4 2.6 fusion.118
  247.1 2.8 fusion.120
  249.9 4.3 add_add_fusion
  260.1 20.1 %shard_map.324 = bf16[4,512,512]{2,1,0:T(8,128)(2,1)} custom-call(bf16[4,512,512]{2,1,0:T(8,128)(2,1)} %pad_maximum_fusion.g_in), custom_call_target="tpu_custom_call" | custom-call | tf_op jit(solution)/shard_map/pallas_call | solution.py:264
  288.0 3.6 fusion.4
  311.9 148.9 %shard_map.325 = (bf16[128,2048]{1,0:T(8,128)(2,1)}, bf16[128,2048]{1,0:T(8,128)(2,1)}, bf16[6,4,128,512]{3,2,1,0:T(8,128)(2,1)}) custom-call(bf16[512,2048]{1,0:T(8,128)(2,1)} %add_convert_fusion.1.out_in, bf16[512,2048]{1,0:T(8,128)(2,1)} %get-tuple-element.94.back_in, bf16[6,4,4,128,512]{4,3,2,1,0:T(8,128)(2,1)} %maximum_dynamic-update-slice_fusion.g_in), custom_call_target="tpu_custom_call" | custom-call | tf_op jit(solution)/shard_map/pallas_call | solution.py:415
  464.4 2.1 reshape.463
  468.0 2.9 reshape.470
  470.9 2.7 copy.159
  473.6 3.0 reshape.462
  476.7 3.0 convert_reduce_fusion.1
  479.6 2.2 convert_bitcast_fusion.2
  487.5 3.3 convert_bitcast_fusion
  490.8 2.9 copy.165
  493.7 2.9 copy.171
  501.7 63.5 %all-reduce = (f32[4,1792]{1,0:T(4,128)S(1)}, f32[2048]{0:T(1024)S(1)}) all-reduce(f32[4,1792]{1,0:T(4,128)S(1)} %broadcast_select_fusion, f32[2048]{0:T(1024)S(1)} %get-tuple-element.111), channel_id=1, replica_groups=mesh['ctx'=16,'tp'=2] {'ctx'}, use_global_device_ids=true, to_apply=%region_14.15 | all-reduce | flops 9216 | bytes 73728 | tf_op jit(solution)/shard_map/psum | solution.py:643
  567.8 37.0 %psum.23 = f32[4,2048]{1,0:T(4,128)S(1)} all-reduce(f32[4,2048]{1,0:T(4,128)S(1)} %reshape.460), channel_id=1, replica_groups=mesh['ctx'=16,'tp'=2] {'ctx','tp'}, use_global_device_ids=true, to_apply=%region_21.22 | all-reduce | flops 8192 | bytes 65536 | tf_op jit(solution)/shard_map/psum | solution.py:641
  (271 shorter events, 91.5 us)
Async XLA Ops:
  0.7 5.8 copy-start.10
  0.7 7.5 %copy-start.18 = (bf16[4096,128]{1,0:T(8,128)(2,1)S(1)}, bf16[4096,128]{1,0:T(8,128)(2,1)}, u32[]{:S(2)}) copy-start(bf16[4096,128]{1,0:T(8,128)(2,1)} %param.35) | copy-start | bytes 3145732
  15.0 138.6 %copy-start.50 = (f32[2048]{0:T(1024)S(1)}, f32[2048]{0:T(1024)}, u32[]{:S(2)}) copy-start(f32[2048]{0:T(1024)} %param.24) | copy-start | bytes 24580
  15.0 138.5 %copy-start.51 = (f32[2048]{0:T(1024)S(1)}, f32[2048]{0:T(1024)}, u32[]{:S(2)}) copy-start(f32[2048]{0:T(1024)} %param.23) | copy-start | bytes 24580
  15.0 138.5 %copy-start.52 = (f32[2048]{0:T(1024)S(1)}, f32[2048]{0:T(1024)}, u32[]{:S(2)}) copy-start(f32[2048]{0:T(1024)} %param.22) | copy-start | bytes 24580
  15.0 138.5 %copy-start.53 = (f32[2048]{0:T(1024)S(1)}, f32[2048]{0:T(1024)}, u32[]{:S(2)}) copy-start(f32[2048]{0:T(1024)} %param.21) | copy-start | bytes 24580
  153.6 6.8 %copy-start.42 = (f32[1,2,2,4,128]{4,3,2,1,0:T(4,128)}, f32[1,2,2,4,128]{4,3,2,1,0:T(4,128)S(1)}, u32[]{:S(2)}) copy-start(f32[1,2,2,4,128]{4,3,2,1,0:T(4,128)S(1)} %copy.154) | copy-start | bytes 24580
  156.2 6.1 %copy-start.21 = (f32[512,256]{1,0:T(8,128)}, f32[512,256]{1,0:T(8,128)S(1)}, u32[]{:S(2)}) copy-start(f32[512,256]{1,0:T(8,128)S(1)} %convolution_add_fusion.2) | copy-start | bytes 1572868
  162.4 4.2 copy-start.24
  168.6 4.7 copy-start.45
  168.6 4.7 copy-start.47
  177.3 39.4 %copy-start.56 = (f32[32]{0:T(128)}, f32[32]{0:T(128)S(1)}, u32[]{:S(2)}) copy-start(f32[32]{0:T(128)S(1)} %multiply_power_fusion) | copy-start | bytes 388
  179.1 37.7 %copy-start.38 = (bf16[512,32]{1,0:T(8,128)(2,1)}, bf16[512,32]{1,0:T(8,128)(2,1)S(1)}, u32[]{:S(2)}) copy-start(bf16[512,32]{1,0:T(8,128)(2,1)S(1)} %get-tuple-element.108) | copy-start | bytes 98308
  224.0 13.7 %copy-start.27 = (f32[512,256]{1,0:T(8,128)}, f32[512,256]{1,0:T(8,128)S(1)}, u32[]{:S(2)}) copy-start(f32[512,256]{1,0:T(8,128)S(1)} %convolution_add_fusion.4) | copy-start | bytes 1572868
  224.1 4.4 copy-start.1
  228.9 18.2 %copy-start.19 = (f32[512,256]{1,0:T(8,128)}, f32[512,256]{1,0:T(8,128)S(1)}, u32[]{:S(2)}) copy-start(f32[512,256]{1,0:T(8,128)S(1)} %convolution_add_fusion.1) | copy-start | bytes 1572868
  235.6 4.7 copy-start.32
  240.3 4.7 copy-start.36
  245.0 4.9 copy-start.34
  249.9 4.3 copy-start.29
  283.8 4.2 copy-start.13
  283.8 4.2 copy-start.68
  460.9 5.6 copy-start.2
  460.9 5.6 copy-start.55
  466.4 10.2 %copy-start.11 = (bf16[128,2048]{1,0:T(8,128)(2,1)S(1)}, bf16[128,2048]{1,0:T(8,128)(2,1)}, u32[]{:S(2)}) copy-start(bf16[128,2048]{1,0:T(8,128)(2,1)} %param.37) | copy-start | bytes 1572868
  466.5 10.2 %copy-start.40 = (f32[2048]{0:T(1024)S(1)}, f32[2048]{0:T(1024)}, u32[]{:S(2)}) copy-start(f32[2048]{0:T(1024)} %param.36) | copy-start | bytes 24580
  466.5 10.2 %copy-start.41 = (f32[2048]{0:T(1024)S(1)}, f32[2048]{0:T(1024)}, u32[]{:S(2)}) copy-start(f32[2048]{0:T(1024)} %param.32) | copy-start | bytes 24580
  496.6 4.9 copy-start.60
  496.6 5.0 copy-start.61
  496.6 5.0 copy-start.58
  496.6 5.0 copy-start.59
  565.3 40.7 %copy-start.49 = (f32[2048]{0:T(1024)}, f32[2048]{0:T(1024)S(1)}, u32[]{:S(2)}) copy-start(f32[2048]{0:T(1024)S(1)} %get-tuple-element.192) | copy-start | bytes 24580
  (40 other events, 95.7 us)

commit v2 on v1

--- a/solution.py
+++ b/solution.py
@@ -467,7 +467,978 @@
     return values * gate, slope
 
 
+SMALL_ROWS = 96
+VMEM_BYTES = 64 << 20
+
+
+def slot_member(slot, bits):
+    member = 0
+    for stage in range(bits):
+        member += ((slot >> stage) & 1) << (bits - 1 - stage)
+    return member
+
+
+def natural_blocks(depth_size, group):
+    bits = group.bit_length() - 1
+    return [
+        depth * group + slot_member(slot, bits) for slot in range(group) for depth in range(depth_size)
+    ]
+
+
+def token_places(block_order, depth_size, group, rows):
+    bits = group.bit_length() - 1
+    blocks = block_order.reshape(depth_size, group, 2)
+    order = jnp.stack([blocks[:, slot_member(slot, bits)] for slot in range(group)], 0)
+    place = order[..., None] * (rows // 2) + jnp.arange(rows // 2, dtype=jnp.int32)
+    return place.reshape(group * depth_size * rows)
+
+ROW_TILE = 256
+DROP = -1e30
+
+
+def layout_of(depth_size, group, depth_rows, rows, width, ff_chunks):
+    tokens = depth_size * rows
+    half = width // 2
+    landing = (group - 1) * depth_size * depth_rows
+    heads = 3 + ff_chunks
+    cols = 1 + ff_chunks
+    return [
+        ("wr", (heads, width, CHUNK), BF),
+        ("wc", (cols, CHUNK, width), BF),
+        ("gr", (heads, width, CHUNK), BF),
+        ("gc", (cols, CHUNK, width), BF),
+        ("lr", (heads, landing, CHUNK), BF),
+        ("lc", (cols, CHUNK, landing), BF),
+        ("x", (tokens, width), BF),
+        ("dy", (tokens, width), BF),
+        ("na", (tokens, width), BF),
+        ("nm", (tokens, width), BF),
+        ("nmt", (width, tokens), BF),
+        ("kv", (group * tokens, 2 * HD), BF),
+        ("q", (tokens, HD), BF),
+        ("low", (tokens, 3 * HD), BF),
+        ("al", (tokens, HD), BF),
+        ("hg", (tokens, HD), BF),
+        ("alt", (HD, tokens), BF),
+        ("att", (HD, tokens), F32),
+        ("dqt", (HD, tokens), F32),
+        ("stat", (8, tokens), F32),
+        ("tab", (group * tokens, 128), F32),
+        ("kb", (8, HD), F32),
+        ("hid", (ff_chunks, tokens, CHUNK), BF),
+        ("ul", (ff_chunks, tokens, CHUNK), BF),
+        ("tz", (2, 2, tokens // 2, half // 2), BF),
+        ("te", (2, rows, half), BF),
+        ("fin", (2, rows, width), BF),
+        ("mean", (tokens, 1), F32),
+        ("inv", (tokens, 1), F32),
+        ("gv", (8, width), F32),
+        ("ps", (group.bit_length(), SMALL_ROWS, 128), F32),
+        ("pl", (group.bit_length() - 1, SMALL_ROWS, 128), F32),
+        ("pz", (depth_size, SMALL_ROWS, 128), F32),
+        ("px", (2, SMALL_ROWS, 128), F32),
+    ]
+
+
+def semaphores_of(depth_size, group, items):
+    bits = group.bit_length() - 1
+    return [
+        ("z_s", (items, 2, depth_size)),
+        ("z_r", (items, 2, depth_size)),
+        ("z_l", (items, 2)),
+        ("g_s", (items, 2, bits)),
+        ("g_r", (items, 2, bits)),
+        ("t_s", (2, 3)),
+        ("t_r", (2, 3)),
+        ("w_s", (2, 3)),
+        ("w_r", (2, 3)),
+        ("kv_s", (3, bits)),
+        ("kv_r", (3, bits)),
+        ("f_s", (items, 2, bits)),
+        ("f_r", (items, 2, bits)),
+        ("e_s", (items, 2, depth_size)),
+        ("e_r", (items, 2, depth_size)),
+        ("e_l", (items, 2)),
+        ("o_s", (2, 5)),
+        ("o_r", (2, 5)),
+        ("i_l", (4,)),
+        ("p_s", (bits + depth_size,)),
+        ("p_r", (bits + depth_size,)),
+    ]
+
+
+INPUTS = ("x_in", "dy_in", "vectors", "biases", "places")
+INPUTS += ("w_query", "w_key", "w_value", "w_out", "w_up", "w_down")
+OUTPUTS = ("layer_output", "input_grad", "g_query", "g_key", "g_value", "g_out", "g_up", "g_down")
+OUTPUTS += ("norm_sums", "b_query", "b_key", "b_value", "b_up", "b_sum")
+
+
+class Bag:
+    pass
+
+
+def fused_kernel(names, depth_size, group, *refs):
+    m = Bag()
+    for name, ref in zip(names, refs, strict=True):
+        setattr(m, name, ref)
+    at = Place(depth_size, group)
+    at.greet(at.everyone())
+    bits = at.bits
+    rows, width = m.x_in.shape
+    depth_rows = width // (depth_size * group)
+    tokens = depth_size * rows
+    half = width // 2
+    ff_width = m.w_up.shape[1] // depth_size
+    ff_chunks = ff_width // CHUNK
+    block_count = width // depth_rows
+    own_block = at.slot * depth_size + at.depth
+    natural = natural_blocks(depth_size, group)
+    sends, settled = [], []
+
+    def blocks(first, count):
+        return pl.ds(pl.multiple_of(first * depth_rows, depth_rows), count * depth_rows)
+
+    def token_rows(depth):
+        return pl.ds(pl.multiple_of(depth * rows, rows), rows)
+
+    def peer(step):
+        return lax.rem(at.depth + step, depth_size)
+
+    my_cols = pl.ds(pl.multiple_of(at.tp * half, half), half)
+    her_cols = pl.ds(pl.multiple_of((1 - at.tp) * half, half), half)
+
+    items = [(("r", 0), ("r", 1)), (("r", 2), ("c", 0))]
+    items += [(("r", 3 + i), ("c", 1 + i)) for i in range(ff_chunks)]
+    row_pairs = [(m.w_query, m.g_query), (m.w_key, m.g_key), (m.w_value, m.g_value)]
+
+    def outer(kind, a, depth, which):
+        if kind == "r" and a < 3:
+            return row_pairs[a][which].at[:, pl.ds(pl.multiple_of(depth * HD, HD), HD)]
+        if kind == "r":
+            first = pl.multiple_of(depth * ff_width + (a - 3) * CHUNK, CHUNK)
+            return (m.w_up, m.g_up)[which].at[:, pl.ds(first, CHUNK)]
+        if a == 0:
+            return (m.w_out, m.g_out)[which].at[pl.ds(pl.multiple_of(depth * HD, HD), HD), :]
+        first = pl.multiple_of(depth * ff_width + (a - 1) * CHUNK, CHUNK)
+        return (m.w_down, m.g_down)[which].at[pl.ds(first, CHUNK), :]
+
+    def part(pair, kind, a, first, count):
+        if kind == "r":
+            return pair[0].at[a, blocks(first, count), :]
+        return pair[1].at[a, :, blocks(first, count)]
+
+    weights, grads, landing = (m.wr, m.wc), (m.gr, m.gc), (m.lr, m.lc)
+
+    def z_start(k):
+        copies = []
+        for j, (kind, a) in enumerate(items[k]):
+            for s in range(1, depth_size):
+                copies.append(
+                    remote(
+                        outer(kind, a, peer(s), 0),
+                        part(weights, kind, a, own_block, 1),
+                        m.z_s.at[k, j, s],
+                        m.z_r.at[k, j, s],
+                        at.along(s),
+                    )
+                )
+        for j, (kind, a) in enumerate(items[k]):
+            copies.append(
+                local(outer(kind, a, at.depth, 0), part(weights, kind, a, own_block, 1), m.z_l.at[k, j])
+            )
+        return copies
+
+    def z_wait(copies):
+        for copy in copies[:-2]:
+            copy.wait_recv()
+        sends.extend(copies[:-2])
+        for copy in copies[-2:]:
+            copy.wait()
+
+    def g_start(k, stage):
+        copies = []
+        for j, (kind, a) in enumerate(items[k]):
+            held = part(weights, kind, a, at.base(stage) * depth_size, 2**stage * depth_size)
+            copies.append(
+                remote(held, held, m.g_s.at[k, j, stage], m.g_r.at[k, j, stage], at.across(stage))
+            )
+        return copies
+
+    def received(copies):
+        for copy in copies:
+            copy.wait_recv()
+        sends.extend(copies)
+
+    def settle(copies):
+        for copy in copies:
+            copy.wait_send()
+        settled.extend(copies)
+
+    def fold_start(k, stage):
+        size = 2**stage
+        other = at.base(stage) + (1 - 2 * at.bit(stage)) * size
+        return [
+            remote(
+                part(grads, kind, a, other * depth_size, size * depth_size),
+                part(landing, kind, a, (size - 1) * depth_size, size * depth_size),
+                m.f_s.at[k, j, stage],
+                m.f_r.at[k, j, stage],
+                at.across(stage),
+            )
+            for j, (kind, a) in enumerate(items[k])
+        ]
+
+    def fold_finish(k, stage, copies):
+        received(copies)
+        size = 2**stage
+        own = at.base(stage) * depth_size
+        for kind, a in items[k]:
+
+            def add(i, _, kind=kind, a=a):
+                mine = blocks(own + i, 1)
+                theirs = blocks((size - 1) * depth_size + i, 1)
+                if kind == "r":
+                    total = m.gr[a, mine, :].astype(F32) + m.lr[a, theirs, :].astype(F32)
+                    m.gr[a, mine, :] = total.astype(BF)
+                else:
+                    total = m.gc[a, :, mine].astype(F32) + m.lc[a, :, theirs].astype(F32)
+                    m.gc[a, :, mine] = total.astype(BF)
+                return 0
+
+            lax.fori_loop(0, size * depth_size, add, 0)
+
+    def end_start(k):
+        copies = []
+        for j, (kind, a) in enumerate(items[k]):
+            for s in range(1, depth_size):
+                copies.append(
+                    remote(
+                        part(grads, kind, a, at.slot * depth_size + peer(s), 1),
+                        outer(kind, a, at.depth, 1),
+                        m.e_s.at[k, j, s],
+                        m.e_r.at[k, j, s],
+                        at.along(s),
+                    )
+                )
+        for j, (kind, a) in enumerate(items[k]):
+            copies.append(
+                local(part(grads, kind, a, own_block, 1), outer(kind, a, at.depth, 1), m.e_l.at[k, j])
+            )
+        return copies
+
+    near = {"ctx": at.ctx + (1 - 2 * (at.depth % 2)) * group}
+    far = {"ctx": at.ctx + (2 - 4 * (at.depth // 2)) * group}
+    near_depth = at.depth + 1 - 2 * (at.depth % 2)
+    pair_first = at.depth // 2 * 2
+    my_pair = pl.ds(pl.multiple_of(pair_first * rows, rows), 2 * rows)
+    her_pair = pl.ds(pl.multiple_of((2 - pair_first) * rows, rows), 2 * rows)
+    quarter = half // 2
+    my_quarter = pl.ds(pl.multiple_of(at.tp * half + at.depth % 2 * quarter, quarter), quarter)
+    her_quarter = pl.ds(pl.multiple_of(at.tp * half + (1 - at.depth % 2) * quarter, quarter), quarter)
+
+    def token_step(i, buffer, step, copies):
+        if copies:
+            received(copies[-1:])
+        brought = [
+            None,
+            (token_rows(near_depth), my_cols),
+            (her_pair, my_quarter),
+            (her_pair, her_quarter),
+        ]
+        given = [(token_rows(at.depth), my_cols), (my_pair, my_quarter), (her_pair, my_quarter)]
+        if step < 3:
+            piece = buffer.at[given[step][0], given[step][1]]
+            there = far if step == 1 else near
+            copies.append(remote(piece, piece, m.t_s.at[i, step], m.t_r.at[i, step], there))
+        if step:
+            piece = buffer.at[brought[step][0], brought[step][1]]
+            swapped[i].append(
+                remote(piece, piece, m.w_s.at[i, step - 1], m.w_r.at[i, step - 1], at.twin())
+            )
+        return copies
+
+    def kv_start(stage):
+        size = 2**stage * tokens
+        held = m.kv.at[pl.ds(pl.multiple_of(at.base(stage) * tokens, tokens), size), :]
+        return remote(held, held, m.kv_s.at[0, stage], m.kv_r.at[0, stage], at.across(stage))
+
+    spare = (m.lr.at[1 + ff_chunks], m.lr.at[2 + ff_chunks])
+
+    def dkv_start(stage):
+        size = 2**stage
+        other = at.base(stage) + (1 - 2 * at.bit(stage)) * size
+        given = pl.ds(pl.multiple_of(other * tokens, tokens), size * tokens)
+        taken = pl.ds((size - 1) * tokens, size * tokens)
+        return [
+            remote(
+                m.kv.at[given, slice(h * HD, (h + 1) * HD)],
+                spare[h].at[taken, :],
+                m.kv_s.at[1 + h, stage],
+                m.kv_r.at[1 + h, stage],
+                at.across(stage),
+            )
+            for h in range(2)
+        ]
+
+    def dkv_finish(stage, copies):
+        received(copies)
+        size = 2**stage
+        own = at.base(stage) * tokens
+        step = ROW_TILE
+
+        def add(i, _):
+            mine = pl.ds(pl.multiple_of(own + i * step, step), step)
+            theirs = pl.ds(pl.multiple_of((size - 1) * tokens + i * step, step), step)
+            for h in range(2):
+                cols = slice(h * HD, (h + 1) * HD)
+                total = m.kv[mine, cols].astype(F32) + spare[h][theirs, :].astype(F32)
+                m.kv[mine, cols] = total.astype(BF)
+            return 0
+
+        lax.fori_loop(0, size * tokens // step, add, 0)
+
+    def place_rows():
+        mine = token_rows(at.depth)
+        for b in range(block_count):
+            c = natural[b]
+            into = slice(b * depth_rows, (b + 1) * depth_rows)
+            out_of = slice(c * depth_rows, (c + 1) * depth_rows)
+            m.x[mine, into] = m.x_in[:, out_of]
+            m.dy[mine, into] = m.dy_in[:, out_of]
+            m.gv[:, into] = m.vectors[:, out_of]
+
+    def affine():
+        step = 32
+
+        def stats(i, _):
+            here = pl.ds(pl.multiple_of(i * step, step), step)
+            x = m.x[here, :].astype(F32)
+            mean = jnp.mean(x, -1, keepdims=True)
+            centered = x - mean
+            m.mean[here, :] = mean
+            m.inv[here, :] = lax.rsqrt(jnp.mean(centered * centered, -1, keepdims=True) + norm_epsilon)
+            return 0
+
+        lax.fori_loop(0, tokens // step, stats, 0)
+
+        def body(i, _):
+            here = token_rows(i)
+            for n in range(width // 512):
+                cols = slice(n * 512, (n + 1) * 512)
+                normal = (m.x[here, cols].astype(F32) - m.mean[here, :]) * m.inv[here, :]
+                m.na[here, cols] = (normal * m.gv[0:1, cols] + m.gv[1:2, cols]).astype(BF)
+                mlp = normal * m.gv[2:3, cols] + m.gv[3:4, cols]
+                m.nm[here, cols] = mlp.astype(BF)
+                m.nmt[cols, here] = mlp.T.astype(BF)
+            return 0
+
+        lax.fori_loop(0, depth_size, body, 0)
+
+    lane = lax.broadcasted_iota(jnp.int32, (1, 128), 1)
+
+    def place_column(n):
+        row = jnp.broadcast_to(m.places[pl.ds(n, 1), :].astype(F32), (128, 128))
+        return row.T
+
+    def make_tables():
+        def body(n, _):
+            angles = place_column(n) * m.vectors[5:6, :128]
+            here = pl.ds(pl.multiple_of(n * 128, 128), 128)
+            m.tab[here, :] = jnp.cos(angles - m.vectors[6:7, :128])
+            return 0
+
+        lax.fori_loop(0, group * tokens // 128, body, 0)
+
+    def turned(value, here, sign):
+        head = value[:, :128]
+        left = pltpu.roll(head, 128 - ROT // 2, 1)
+        right = pltpu.roll(head, ROT // 2, 1)
+        table = m.tab[here, :]
+        cosine = jnp.where(lane < ROT, table, 1.0)
+        sine = sign * pltpu.roll(table, ROT, 1)
+        crossed = jnp.where(lane < ROT // 2, -left, jnp.where(lane < ROT, right, 0.0))
+        return head * cosine + crossed * sine
+
+    def project(a):
+        return mm(m.na[...], m.wr[a]) + m.biases[a : a + 1, :]
+
+    kv_own = pl.ds(pl.multiple_of(at.slot * tokens, tokens), tokens)
+    score_scale = 1.0 / math.sqrt(HD)
+
+    def make_query_key():
+        query = project(0)
+        head = turned(query, kv_own, 1.0)
+        m.q[:, :128] = head.astype(BF)
+        m.q[:, 128:] = query[:, 128:].astype(BF)
+        keys = project(1)
+        m.kv[kv_own, :128] = turned(keys, kv_own, 1.0).astype(BF)
+        m.kv[kv_own, 128:HD] = keys[:, 128:].astype(BF)
+
+    def make_values():
+        m.kv[kv_own, HD:] = project(2).astype(BF)
+
+    def key_rows(j):
+        return pl.ds(pl.multiple_of(j * tokens, tokens), tokens)
+
+    def masked_scores(j):
+        scores = mm_nt(m.kv[key_rows(j), :HD], m.q[...]) * score_scale
+        count = tokens // 128
+        column = jnp.concatenate([place_column(j * count + n)[:, :1] for n in range(count)], 0)
+        row = jnp.concatenate([m.places[pl.ds(at.slot * count + n, 1), :] for n in range(count)], 1)
+        return jnp.where(column <= row.astype(F32), scores, DROP)
+
+    def attend(j):
+        scores = masked_scores(j)
+        if j == 0:
+            old = jnp.full((1, tokens), -1e20, F32)
+        else:
+            old = m.stat[0:1, :]
+        new = jnp.maximum(old, jnp.max(scores, 0, keepdims=True))
+        raw = jnp.exp(scores - new)
+        total = jnp.sum(raw, 0, keepdims=True)
+        value = mm(m.kv[key_rows(j), HD:].T, raw.astype(BF))
+        m.stat[0:1, :] = new
+        if j:
+            factor = jnp.exp(old - new)
+            total = total + m.stat[1:2, :] * factor
+            value = value + m.att[...] * factor
+        m.stat[1:2, :] = total
+        m.att[...] = value
+        if j == group - 1:
+            m.stat[2:3, :] = new + jnp.log(total)
+            value = value / total
+            m.att[...] = value
+            m.alt[...] = value.astype(BF)
+            m.al[...] = value.T.astype(BF)
+
+    def head_grads():
+        grad = mm_nt(m.dy[...], m.wc[0])
+        low = grad.astype(BF)
+        m.hg[...] = low
+        m.stat[3:4, :] = jnp.sum(low.astype(F32).T * m.att[...], 0, keepdims=True)
+
+    def attend_back(j):
+        probs = jnp.exp(masked_scores(j) - m.stat[2:3, :])
+        value_part = mm(probs.astype(BF), m.hg[...])
+        prob_grad = mm_nt(m.kv[key_rows(j), HD:], m.hg[...])
+        score_grad = (probs * (prob_grad - m.stat[3:4, :]) * score_scale).astype(BF)
+        query_part = mm(m.kv[key_rows(j), :HD].T, score_grad)
+        key_part = mm(score_grad, m.q[...])
+        head_sum = jnp.sum(turned(key_part, key_rows(j), -1.0), 0, keepdims=True)
+        rest_sum = jnp.sum(key_part[:, 128:], 0, keepdims=True)
+        if j:
+            query_part = query_part + m.dqt[...]
+            head_sum = head_sum + m.kb[0:1, :128]
+            rest_sum = rest_sum + m.kb[0:1, 128:]
+        m.dqt[...] = query_part
+        m.kb[0:1, :128] = head_sum
+        m.kb[0:1, 128:] = rest_sum
+        m.kv[key_rows(j), :HD] = key_part.astype(BF)
+        m.kv[key_rows(j), HD:] = value_part.astype(BF)
+
+    def small_store(first, row):
+        for n in range(row.shape[1] // 128):
+            m.ps[0, first + n : first + n + 1, :] = row[:, n * 128 : (n + 1) * 128]
+
+    def attention_grads():
+        query = m.dqt[...].T
+        head = turned(query, kv_own, -1.0)
+        keys = m.kv[kv_own, :HD].astype(F32)
+        key_head = turned(keys, kv_own, -1.0)
+        m.low[:, :128] = head.astype(BF)
+        m.low[:, 128:HD] = query[:, 128:].astype(BF)
+        m.low[:, HD : HD + 128] = key_head.astype(BF)
+        m.low[:, HD + 128 : 2 * HD] = m.kv[kv_own, 128:HD]
+        m.low[:, 2 * HD :] = m.kv[kv_own, HD:]
+        small_store(64, jnp.sum(head, 0, keepdims=True))
+        small_store(65, jnp.sum(query[:, 128:], 0, keepdims=True))
+        small_store(66, m.kb[0:1, :])
+        small_store(68, jnp.sum(m.kv[kv_own, HD:].astype(F32), 0, keepdims=True))
+
+        def body(n, _):
+            tile = pl.ds(pl.multiple_of(n * ROW_TILE, ROW_TILE), ROW_TILE)
+            turned_in = m.na[:, tile].T
+            for a in range(3):
+                m.gr[a, tile, :] = mm(turned_in, m.low[:, a * HD : (a + 1) * HD]).astype(BF)
+            return 0
+
+        lax.fori_loop(0, width // ROW_TILE, body, 0)
+
+        def body_out(n, _):
+            tile = pl.ds(pl.multiple_of(n * 512, 512), 512)
+            m.gc[0, :, tile] = mm(m.alt[...], m.dy[:, tile]).astype(BF)
+            return 0
+
+        lax.fori_loop(0, width // 512, body_out, 0)
+
+    def feed_forward(i):
+        activated, slope = gelu_parts(mm(m.nm[...], m.wr[3 + i]) + m.biases[3 + i : 4 + i, :])
+        m.hid[i] = activated.astype(BF)
+        up_grad = mm_nt(m.dy[...], m.wc[1 + i]) * slope
+        small_store(70 + 2 * i, jnp.sum(up_grad, 0, keepdims=True))
+        m.ul[i] = up_grad.astype(BF)
+        turned_hidden = activated.T.astype(BF)
+
+        def body(n, _):
+            tile = pl.ds(pl.multiple_of(n * 512, 512), 512)
+            m.gr[3 + i, tile, :] = mm(m.nmt[tile, :], m.ul[i]).astype(BF)
+            m.gc[1 + i, :, tile] = mm(turned_hidden, m.dy[:, tile]).astype(BF)
+            return 0
+
+        lax.fori_loop(0, width // 512, body, 0)
+
+    out, back = m.na, m.dy
+
+    def tile_of(n):
+        return pl.ds(pl.multiple_of(n * ROW_TILE, ROW_TILE), ROW_TILE)
+
+    def small_add_rows(first, n, value):
+        row = jnp.sum(value, 0, keepdims=True)
+        for h in range(ROW_TILE // 128):
+            m.ps[0, pl.ds(first + n * (ROW_TILE // 128) + h, 1), :] = row[:, h * 128 : (h + 1) * 128]
+
+    def end_out(n):
+        tile = tile_of(n)
+        total = mm(m.al[...], m.wc[0, :, tile])
+        for i in range(ff_chunks):
+            total += mm(m.hid[i], m.wc[1 + i, :, tile])
+        out[:, tile] = total.astype(BF)
+
+    def end_back(n):
+        tile = tile_of(n)
+        attn_back = mm_nt(m.low[:, :HD], m.wr[0, tile, :])
+        for a in (1, 2):
+            attn_back += mm_nt(m.low[:, a * HD : (a + 1) * HD], m.wr[a, tile, :])
+        mlp_back = mm_nt(m.ul[0], m.wr[3, tile, :])
+        for i in range(1, ff_chunks):
+            mlp_back += mm_nt(m.ul[i], m.wr[3 + i, tile, :])
+        normal = (m.x[:, tile].astype(F32) - m.mean[...]) * m.inv[...]
+        small_add_rows(0, n, attn_back * normal)
+        small_add_rows(16, n, attn_back)
+        small_add_rows(32, n, mlp_back * normal)
+        small_add_rows(48, n, mlp_back)
+        small_add_rows(78, n, m.dy[:, tile].astype(F32))
+        back[:, tile] = (attn_back * m.gv[0:1, tile] + mlp_back * m.gv[2:3, tile]).astype(BF)
+
+    def end_half(piece, which):
+        count = half // ROW_TILE
+
+        def body(n, _):
+            piece(which * count + n)
+            return 0
+
+        lax.fori_loop(0, count, body, 0)
+
+    swap_in = (m.nm.at[:, 0:half], m.nm.at[:, half : 2 * half])
+
+    def offer():
+        pl.semaphore_signal(m.free, inc=1, device_id=at.twin(), device_id_type=MESH)
+
+    def sum_start(i):
+        if i == 0:
+            pl.semaphore_wait(m.free, 1)
+        return remote(ends[i].at[:, her_cols], swap_in[i], m.o_s.at[i, 0], m.o_r.at[i, 0], at.twin())
+
+    ends = (out, back)
+
+    def sum_step(i, step, copy):
+        received([copy])
+        mine = ends[i]
+        if step == 0:
+
+            def add(z, _):
+                block = token_rows(z)
+                total = mine[block, my_cols].astype(F32) + swap_in[i][block, :].astype(F32)
+                mine[block, my_cols] = total.astype(BF)
+                return 0
+
+            lax.fori_loop(0, depth_size, add, 0)
+            source, into, there = mine.at[her_pair, her_quarter], m.tz.at[i, 0], near
+        elif step == 1:
+            total = mine[her_pair, my_quarter].astype(F32) + m.tz[i, 0].astype(F32)
+            mine[her_pair, my_quarter] = total.astype(BF)
+            source, into, there = mine.at[her_pair, my_quarter], m.tz.at[i, 1], far
+        elif step == 2:
+            total = mine[my_pair, my_quarter].astype(F32) + m.tz[i, 1].astype(F32)
+            mine[my_pair, my_quarter] = total.astype(BF)
+            source, into, there = mine.at[token_rows(near_depth), my_cols], m.te.at[i], near
+        else:
+            total = mine[token_rows(at.depth), my_cols].astype(F32) + m.te[i].astype(F32)
+            m.fin[i, :, my_cols] = total.astype(BF)
+            source, into, there = m.fin.at[i, :, my_cols], m.fin.at[i, :, my_cols], at.twin()
+        return remote(source, into, m.o_s.at[i, 1 + step], m.o_r.at[i, 1 + step], there)
+
+    def stage_of(column):
+        piece = column // tokens
+        return (m.att, m.dqt)[piece // 2], piece % 2 * rows, column % tokens
+
+    def finish_rows():
+        step = 16
+
+        def body(i, _):
+            here = pl.ds(pl.multiple_of(i * step, step), step)
+            x = m.x_in[here, :].astype(F32)
+            dy = m.dy_in[here, :].astype(F32)
+            here_all = pl.ds(pl.multiple_of(at.depth * rows + i * step, step), step)
+            inverse = m.inv[here_all, :]
+            normal = (x - m.mean[here_all, :]) * inverse
+            total = jnp.zeros((step, 1), F32)
+            against = jnp.zeros((step, 1), F32)
+            pieces = {}
+            for b in range(block_count):
+                c = natural[b]
+                out_of = slice(b * depth_rows, (b + 1) * depth_rows)
+                into = slice(c * depth_rows, (c + 1) * depth_rows)
+                m.layer_output[here, into] = (
+                    x[:, into] + m.fin[0, here, out_of].astype(F32) + m.vectors[4:5, into]
+                ).astype(BF)
+                pieces[b] = m.fin[1, here, out_of].astype(F32)
+                total += jnp.sum(pieces[b], -1, keepdims=True)
+                against += jnp.sum(pieces[b] * normal[:, into], -1, keepdims=True)
+            total = total / width
+            against = against / width
+            for b in range(block_count):
+                c = natural[b]
+                into = slice(c * depth_rows, (c + 1) * depth_rows)
+                staged, first, cols = stage_of(c * depth_rows)
+                there = pl.ds(pl.multiple_of(first + i * step, step), step)
+                staged[there, cols : cols + depth_rows] = dy[:, into] + inverse * (
+                    pieces[b] - total - normal[:, into] * against
+                )
+            return 0
+
+        lax.fori_loop(0, rows // step, body, 0)
+        copies = []
+        for n in range(width // tokens):
+            staged, first, _ = stage_of(n * tokens)
+            copies.append(
+                local(
+                    staged.at[first : first + rows, :],
+                    m.input_grad.at[:, n * tokens : (n + 1) * tokens],
+                    m.i_l.at[n],
+                )
+            )
+        for copy in copies:
+            copy.wait()
+
+    def small_group(stage):
+        return remote(m.ps.at[stage], m.pl.at[stage], m.p_s.at[stage], m.p_r.at[stage], at.across(stage))
+
+    def small_add(stage, copy):
+        received([copy])
+        m.ps[stage + 1] = m.ps[stage] + m.pl[stage]
+
+    def small_depth():
+        total = m.ps.at[bits]
+        copies = [
+            remote(total, m.pz.at[at.depth], m.p_s.at[bits + s], m.p_r.at[bits + s], at.along(s))
+            for s in range(1, depth_size)
+        ]
+        m.pz[at.depth] = m.ps[bits]
+        return copies
+
+    def small_twin(copies):
+        received(copies)
+        value = m.pz[0]
+        for z in range(1, depth_size):
+            value = value + m.pz[z]
+        m.px[0] = value
+        return remote(m.px.at[0], m.px.at[1], m.p_s.at[bits], m.p_r.at[bits], at.twin())
+
+    def small_finish(copy):
+        received([copy])
+        for v in range(4):
+            for b in range(block_count):
+                row = v * 16 + b
+                into = v * 16 + natural[b]
+                m.norm_sums[into : into + 1, :] = m.px[0, row : row + 1, :] + m.px[1, row : row + 1, :]
+        for b in range(block_count):
+            m.b_sum[natural[b] : natural[b] + 1, :] = m.ps[bits, 78 + b : 79 + b, :]
+        for z in range(depth_size):
+            m.b_query[2 * z : 2 * z + 2, :] = m.pz[z, 64:66, :]
+            m.b_key[2 * z : 2 * z + 2, :] = m.pz[z, 66:68, :]
+            m.b_value[2 * z : 2 * z + 2, :] = m.pz[z, 68:70, :]
+            m.b_up[8 * z : 8 * z + 8, :] = m.pz[z, 70:78, :]
+
+    live = {}
+    swapped = {0: [], 1: []}
+    buffers = (m.x, m.dy)
+
+    def run(name, n):
+        if name == "zs":
+            live["z", n] = z_start(n)
+        elif name == "zy":
+            z_wait(live["z", n])
+            live["g", n] = g_start(n, 0)
+        elif name == "yc":
+            received(live["g", n])
+            live["g", n] = g_start(n, 1)
+        elif name == "cw":
+            received(live["g", n])
+        elif name == "ta":
+            live["t", n] = token_step(n, buffers[n], 0, [])
+        elif name == "tb":
+            token_step(n, buffers[n], 1, live["t", n])
+        elif name == "tc":
+            token_step(n, buffers[n], 2, live["t", n])
+        elif name == "td":
+            token_step(n, buffers[n], 3, live["t", n])
+        elif name == "te":
+            received(swapped[n])
+        elif name == "norm":
+            m.ps[0] = jnp.zeros_like(m.ps[0])
+            place_rows()
+        elif name == "tab":
+            make_tables()
+        elif name == "aff":
+            affine()
+        elif name == "qk":
+            make_query_key()
+        elif name == "val":
+            make_values()
+        elif name == "ky":
+            live["k", 0] = kv_start(0)
+        elif name == "kc":
+            received([live["k", 0]])
+            live["k", 1] = kv_start(1)
+        elif name == "kw":
+            received([live["k", 1]])
+        elif name == "at":
+            attend(n)
+        elif name == "hg":
+            head_grads()
+        elif name == "bw":
+            if n == 0:
+                settle([live["k", 0], live["k", 1]])
+            attend_back(n)
+        elif name == "dc":
+            live["d"] = dkv_start(1)
+        elif name == "dy":
+            dkv_finish(1, live["d"])
+            live["d"] = dkv_start(0)
+        elif name == "dw":
+            dkv_finish(0, live["d"])
+        elif name == "ag":
+            attention_grads()
+        elif name == "ff":
+            feed_forward(n)
+        elif name == "fc":
+            live["f", n] = fold_start(n, 1)
+        elif name == "fy":
+            fold_finish(n, 1, live["f", n])
+            live["f", n] = fold_start(n, 0)
+        elif name == "fz":
+            fold_finish(n, 0, live["f", n])
+            live["e", n] = end_start(n)
+        elif name == "of":
+            offer()
+        elif name == "eo":
+            end_half(end_out, at.tp if n else 1 - at.tp)
+        elif name == "eb":
+            if n == 0:
+                settle(live["t", 1] + swapped[1])
+            end_half(end_back, at.tp if n else 1 - at.tp)
+        elif name == "sx":
+            live["s", n] = sum_start(n)
+        elif name == "sa":
+            live["s", n] = sum_step(n, 0, live["s", n])
+        elif name == "sb":
+            live["s", n] = sum_step(n, 1, live["s", n])
+        elif name == "sc":
+            live["s", n] = sum_step(n, 2, live["s", n])
+        elif name == "sd":
+            live["s", n] = sum_step(n, 3, live["s", n])
+        elif name == "sw":
+            received([live["s", n]])
+        elif name == "pa":
+            live["p"] = small_group(0)
+        elif name == "pb":
+            small_add(0, live["p"])
+            live["p"] = small_group(1)
+        elif name == "pc":
+            small_add(1, live["p"])
+            live["p"] = small_depth()
+        elif name == "pd":
+            live["p"] = small_twin(live["p"])
+        elif name == "pe":
+            small_finish(live["p"])
+        elif name == "fin":
+            finish_rows()
+        elif name == "ew":
+            received(live["e", n][:-2])
+            for copy in live["e", n][-2:]:
+                copy.wait()
+
+    for entry in SCHEDULE:
+        name = entry.rstrip("0123456789")
+        run(name, int(entry[len(name) :] or 0))
+    for copy in sends:
+        if not any(copy is other for other in settled):
+            copy.wait_send()
+
+
+SCHEDULE = (
+    "zs0", "norm", "ta0", "zy0", "zs1", "tb0", "zs2", "zs5", "zy1", "tc0", "ta1", "yc1",
+    "cw1", "zy2", "td0", "tab", "yc0", "zy5", "tb1", "te0", "aff", "yc2", "cw0", "zs3",
+    "qk", "val", "tc1", "yc5", "ky", "zs4", "zy3", "kc", "td1", "kw", "at0", "at1",
+    "te1", "cw2", "zy4", "ff0", "at2", "fc2", "cw5", "at3", "hg", "bw0", "bw1", "bw2",
+    "bw3", "dc", "ff3", "yc3", "dy", "yc4", "cw3", "fy2", "cw4", "ff2", "ff1", "fc3",
+    "dw", "ag", "eo0", "of0", "sx0", "fc0", "fy3", "eb0", "fz2", "fc1", "fy0", "fz3",
+    "fc4", "sx1", "eb1", "pa", "fc5", "pb", "fz0", "fy4", "ew3", "eo1", "pc", "sa0",
+    "ew0", "fz4", "sb0", "sa1", "fy5", "ew4", "fy1", "sb1", "ew2", "fz5", "pd", "sc0",
+    "sc1", "fz1", "sd0", "sd1", "ew5", "sw0", "pe", "sw1", "fin", "ew1",
+)
+
+
+def fits(depth_size, group, depth_rows, rows, width, ff_chunks):
+    sizes = layout_of(depth_size, group, depth_rows, rows, width, ff_chunks)
+    total = sum(math.prod(shape) * jnp.dtype(kind).itemsize for _, shape, kind in sizes)
+    shaped = group == depth_size == ff_chunks == 4 and depth_rows == rows == 128
+    return shaped and total < VMEM_BYTES
+
+
+def fused_shards(
+    layer_input,
+    block_order,
+    attn_gain,
+    attn_shift,
+    mlp_gain,
+    mlp_shift,
+    w_query,
+    b_query,
+    w_key,
+    b_key,
+    w_value,
+    b_value,
+    w_out,
+    b_out,
+    w_up,
+    b_up,
+    w_down,
+    b_down,
+    out_grad,
+):
+    rows, width = layer_input.shape
+    tp_size = lax.axis_size("tp")
+    depth_size = HEADS // tp_size
+    group = lax.axis_size("ctx") // depth_size
+    depth_rows = width // (depth_size * group)
+    ff_width = w_up.shape[1] // depth_size
+    ff_chunks = ff_width // CHUNK
+    tokens = depth_size * rows
+    at = Place(depth_size, group)
+
+    places = token_places(block_order, depth_size, group, rows).reshape(-1, 128)
+    freqs = 10000.0 ** (-(2.0 * jnp.arange(ROT // 2, dtype=F32)) / ROT)
+    phases = jnp.repeat(jnp.array([0.0, math.pi / 2], F32), 64)
+    vectors = jnp.stack(
+        [attn_gain, attn_shift, mlp_gain, mlp_shift, b_out + b_down]
+        + [jnp.tile(freqs, width // (ROT // 2)), jnp.tile(phases, width // 128), b_out]
+    )
+    per_head = [bias.reshape(depth_size, 1, HD) for bias in (b_query, b_key, b_value)]
+    per_head += [b_up.reshape(depth_size, ff_chunks, CHUNK), jnp.zeros((depth_size, 1, CHUNK), F32)]
+    biases = lax.dynamic_index_in_dim(jnp.concatenate(per_head, 1), at.depth, 0, keepdims=False)
+
+    buffers = layout_of(depth_size, group, depth_rows, rows, width, ff_chunks)
+    semaphores = semaphores_of(depth_size, group, 2 + ff_chunks)
+    names = tuple(INPUTS) + tuple(OUTPUTS) + tuple(b[0] for b in buffers) + tuple(s[0] for s in semaphores) + ("free",)
+    vmem = pl.BlockSpec(memory_space=pltpu.VMEM)
+    hbm = pl.BlockSpec(memory_space=pl.ANY)
+    shape = jax.ShapeDtypeStruct
+    wide, thin = depth_size * HD, depth_size * ff_width
+    results = pl.pallas_call(
+        functools.partial(fused_kernel, names, depth_size, group),
+        out_shape=(
+            shape((rows, width), BF),
+            shape((rows, width), F32),
+            shape((depth_rows, wide), BF),
+            shape((depth_rows, wide), BF),
+            shape((depth_rows, wide), BF),
+            shape((wide, depth_rows), BF),
+            shape((depth_rows, thin), BF),
+            shape((thin, depth_rows), BF),
+            shape((4 * width // 128, 128), F32),
+            shape((wide // 128, 128), F32),
+            shape((wide // 128, 128), F32),
+            shape((wide // 128, 128), F32),
+            shape((thin // 128, 128), F32),
+            shape((width // 128, 128), F32),
+        ),
+        in_specs=[vmem] * 5 + [hbm] * 6,
+        out_specs=(vmem,) + (hbm,) * 7 + (vmem,) * 6,
+        scratch_shapes=[pltpu.VMEM(s, t) for _, s, t in buffers]
+        + [pltpu.SemaphoreType.DMA(s) for _, s in semaphores]
+        + [pltpu.SemaphoreType.REGULAR],
+        compiler_params=pltpu.CompilerParams(
+            collective_id=4, has_side_effects=True, vmem_limit_bytes=VMEM_BYTES
+        ),
+    )(
+        layer_input,
+        out_grad,
+        vectors,
+        biases,
+        places,
+        w_query,
+        w_key,
+        w_value,
+        w_out,
+        w_up,
+        w_down,
+    )
+    output, input_grad = results[:2]
+    weight_grads = [grad.astype(F32) for grad in results[2:8]]
+    norm_sums = results[8].reshape(4, width)
+    small = [result.reshape(-1) for result in results[9:]]
+    return (
+        output,
+        input_grad,
+        *weight_grads,
+        small[0],
+        small[1],
+        small[2],
+        small[4],
+        small[3],
+        small[4],
+        norm_sums[0],
+        norm_sums[1],
+        norm_sums[2],
+        norm_sums[3],
+    )
+
+
 def shards(
+    layer_input,
+    block_order,
+    attn_gain,
+    attn_shift,
+    mlp_gain,
+    mlp_shift,
+    w_query,
+    b_query,
+    w_key,
+    b_key,
+    w_value,
+    b_value,
+    w_out,
+    b_out,
+    w_up,
+    b_up,
+    w_down,
+    b_down,
+    out_grad,
+):
+    rows, width = layer_input.shape
+    depth_size = HEADS // lax.axis_size("tp")
+    group = lax.axis_size("ctx") // depth_size
+    ff_chunks = w_up.shape[1] // depth_size // CHUNK
+    whole = fits(depth_size, group, width // (depth_size * group), rows, width, ff_chunks)
+    chosen = fused_shards if whole else staged_shards
+    return chosen(
+        layer_input, block_order, attn_gain, attn_shift, mlp_gain, mlp_shift, w_query, b_query, w_key, b_key, w_value, b_value, w_out, b_out, w_up, b_up, w_down, b_down, out_grad
+    )
+
+
+def staged_shards(
     layer_input,
     block_order,
     attn_gain,

time: 617 us -> 271 us (0.44); the launches traced: 606 us -> 269 us
  blocking collectives: 101 us -> 0 us
  Pallas kernels: 339 us -> 248 us
  matrix products: 73.6 us -> 0 us
  local copies, waits for them, and re-layouts: 55.1 us -> 12 us
  other arithmetic: 36 us -> 9.01 us
    psum x2 -> x0, blocking collectives: 101 us -> none  [the longest x1 63.5 us: shards(): spread, bias_grad = lax.psum((spread, jnp.sum(grad32, 0)), 'ctx')]
    pallas_call x4 -> x1, Pallas kernels: 339 us -> 248 us  [fused_shards(): pl.pallas_call(functools.partial(fused_kernel, names, depth_size, group),...]
    dot_general x39 -> x0, matrix products: 73.6 us -> none  [the longest x13 36.3 us: mm_nt(): lax.dot_general(a, b, (((1,), (1,)), ((), ())), preferred_element_type=F32)]
    convert_element_type x10 -> x0, local copies, waits for them, and re-layouts: 18.7 us -> none  [the longest x3 8.63 us: shards(): restored(out_sum).astype(F32)]
    unnamed x166 -> x34, local copies, waits for them, and re-layouts: 20.2 us -> 5.4 us
    reduce_sum x9 -> x0, other arithmetic: 10.9 us -> none  [the longest x1 2.99 us: shards(): spread, bias_grad = lax.psum((spread, jnp.sum(grad32, 0)), 'ctx')]
    unnamed x5 -> x0, other arithmetic: 6.19 us -> none
where the time goes in v2:
time: 271 us; the launch traced here: 269 us
  Pallas kernels  248 us (92%)
  local copies, waits for them, and re-layouts  12 us (4%)
  other arithmetic  9.01 us (3%)
    pallas_call x1, Pallas kernels, fused_shards(): pl.pallas_call(functools.partial(fused_kernel, names, depth_size, group),...  248 us
    convert_element_type x6, other arithmetic, fused_shards(): weight_grads = [grad.astype(F32) for grad in results[2:8]]  7.66 us

profile of v2, /device:TPU:0, one launch (start us, length us, event | category | flops | bytes accessed | tf_op | source)
XLA Modules:
  0.0 269.3 jit_solution(16413603066609282650)
XLA Ops:
  0.7 0.7 reshape.122
  1.4 0.8 concatenate.7
  2.2 0.6 dynamic-slice_bitcast_fusion.refs_3_
  2.8 0.7 reshape.123
  3.5 0.1 copy.52
  3.6 0.1 copy.53
  3.7 0.1 copy.54
  3.8 0.1 copy.55
  3.9 0.1 copy.56
  4.1 0.1 add.31
  4.2 0.1 add.33
  4.3 0.6 broadcast_add_fusion.refs_4_
  4.9 0.1 stack_tile.6
  5.0 0.7 broadcast_in_dim.8
  5.8 0.7 add.28
  6.6 1.5 stack.38.refs_2_
  8.0 247.5 %shard_map.331 = (bf16[128,2048]{1,0:T(8,128)(2,1)}, f32[128,2048]{1,0:T(8,128)}, bf16[128,1024]{1,0:T(8,128)(2,1)}, bf16[128,1024]{1,0:T(8,128)(2,1)}, bf16[128...) custom-call(bf16[128,2048]{1,0:T(8,128)(2,1)} %refs_0_.1, ...), custom_call_target="tpu_custom_call" | custom-call | tf_op jit(solution)/shard_map/pallas_call | solution.py:1349
  255.6 2.8 %convert_element_type.22 = f32[128,4096]{1,0:T(8,128)} convert(bf16[128,4096]{1,0:T(8,128)(2,1)} %get-tuple-element.38) | non-fusion elementwise | flops 524288 | bytes 3145728 | tf_op jit(solution)/shard_map/convert_element_type | solution.py:1389
  258.4 1.5 convert_element_type.23
  259.9 0.8 convert_element_type.18
  260.8 0.8 convert_element_type.19
  261.6 0.8 convert_element_type.20
  262.5 0.8 convert_element_type.21
  263.3 0.6 slice_bitcast_fusion
  263.9 0.6 copy.73
  264.5 0.8 copy.74
  265.3 1.0 copy.75
  266.3 0.6 copy.76
  266.9 0.6 copy.77
  267.5 0.6 copy.78
  268.1 0.6 copy.79
  268.7 0.6 copy.80
  (35 shorter events, 0.3 us)
Async XLA Ops:
  255.6 2.9 %copy-start = (bf16[4096,128]{1,0:T(8,128)(2,1)S(1)}, bf16[4096,128]{1,0:T(8,128)(2,1)}, u32[]{:S(2)}) copy-start(bf16[4096,128]{1,0:T(8,128)(2,1)} %get-tuple-element.39) | copy-start | bytes 3145732
  258.4 1.5 copy-start.6
  258.4 2.3 copy-start.5
  258.4 3.2 %copy-start.4 = (bf16[128,1024]{1,0:T(8,128)(2,1)S(1)}, bf16[128,1024]{1,0:T(8,128)(2,1)}, u32[]{:S(2)}) copy-start(bf16[128,1024]{1,0:T(8,128)(2,1)} %get-tuple-element.36) | copy-start | bytes 786436
  258.4 4.0 %copy-start.3 = (bf16[1024,128]{1,0:T(8,128)(2,1)S(1)}, bf16[1024,128]{1,0:T(8,128)(2,1)}, u32[]{:S(2)}) copy-start(bf16[1024,128]{1,0:T(8,128)(2,1)} %get-tuple-element.37) | copy-start | bytes 786436
  259.9 3.4 %copy-start.7 = (f32[64,128]{1,0:T(8,128)S(1)}, f32[64,128]{1,0:T(8,128)}, u32[]{:S(2)}) copy-start(f32[64,128]{1,0:T(8,128)} %get-tuple-element.45) | copy-start | bytes 98308
  259.9 4.0 %copy-start.8 = (f32[16,128]{1,0:T(8,128)S(1)}, f32[16,128]{1,0:T(8,128)}, u32[]{:S(2)}) copy-start(f32[16,128]{1,0:T(8,128)} %get-tuple-element.43) | copy-start | bytes 24580
  259.9 4.6 %copy-start.2 = (bf16[128,2048]{1,0:T(8,128)(2,1)S(1)}, bf16[128,2048]{1,0:T(8,128)(2,1)}, u32[]{:S(2)}) copy-start(bf16[128,2048]{1,0:T(8,128)(2,1)} %get-tuple-element.108) | copy-start | bytes 1572868
  259.9 5.4 %copy-start.1 = (f32[128,2048]{1,0:T(8,128)S(1)}, f32[128,2048]{1,0:T(8,128)}, u32[]{:S(2)}) copy-start(f32[128,2048]{1,0:T(8,128)} %get-tuple-element.109) | copy-start | bytes 3145732
  262.4 3.8 %copy-start.12 = (f32[8,128]{1,0:T(8,128)S(1)}, f32[8,128]{1,0:T(8,128)}, u32[]{:S(2)}) copy-start(f32[8,128]{1,0:T(8,128)} %get-tuple-element.40) | copy-start | bytes 12292
  262.4 4.4 %copy-start.11 = (f32[8,128]{1,0:T(8,128)S(1)}, f32[8,128]{1,0:T(8,128)}, u32[]{:S(2)}) copy-start(f32[8,128]{1,0:T(8,128)} %get-tuple-element.41) | copy-start | bytes 12292
  262.4 5.0 %copy-start.10 = (f32[8,128]{1,0:T(8,128)S(1)}, f32[8,128]{1,0:T(8,128)}, u32[]{:S(2)}) copy-start(f32[8,128]{1,0:T(8,128)} %get-tuple-element.42) | copy-start | bytes 12292
  262.4 6.2 %copy-start.9 = (f32[32,128]{1,0:T(8,128)S(1)}, f32[32,128]{1,0:T(8,128)}, u32[]{:S(2)}) copy-start(f32[32,128]{1,0:T(8,128)} %get-tuple-element.44) | copy-start | bytes 49156

commit v3 on v2

--- a/solution.py
+++ b/solution.py
@@ -3,6 +3,7 @@
 
 import jax
 import jax.numpy as jnp
+import numpy as np
 from jax import lax
 from jax.experimental import pallas as pl
 from jax.experimental.pallas import tpu as pltpu
@@ -484,14 +485,6 @@
         depth * group + slot_member(slot, bits) for slot in range(group) for depth in range(depth_size)
     ]
 
-
-def token_places(block_order, depth_size, group, rows):
-    bits = group.bit_length() - 1
-    blocks = block_order.reshape(depth_size, group, 2)
-    order = jnp.stack([blocks[:, slot_member(slot, bits)] for slot in range(group)], 0)
-    place = order[..., None] * (rows // 2) + jnp.arange(rows // 2, dtype=jnp.int32)
-    return place.reshape(group * depth_size * rows)
-
 ROW_TILE = 256
 DROP = -1e30
 
@@ -529,10 +522,11 @@
         ("ul", (ff_chunks, tokens, CHUNK), BF),
         ("tz", (2, 2, tokens // 2, half // 2), BF),
         ("te", (2, rows, half), BF),
-        ("fin", (2, rows, width), BF),
         ("mean", (tokens, 1), F32),
         ("inv", (tokens, 1), F32),
         ("gv", (8, width), F32),
+        ("biases", (8, HD), F32),
+        ("places", (group * tokens // 128, 128), F32),
         ("ps", (group.bit_length(), SMALL_ROWS, 128), F32),
         ("pl", (group.bit_length() - 1, SMALL_ROWS, 128), F32),
         ("pz", (depth_size, SMALL_ROWS, 128), F32),
@@ -543,34 +537,35 @@
 def semaphores_of(depth_size, group, items):
     bits = group.bit_length() - 1
     return [
-        ("z_s", (items, 2, depth_size)),
-        ("z_r", (items, 2, depth_size)),
-        ("z_l", (items, 2)),
-        ("g_s", (items, 2, bits)),
-        ("g_r", (items, 2, bits)),
+        ("z_s", (items, depth_size)),
+        ("z_r", (items, depth_size)),
+        ("z_l", (items,)),
+        ("g_s", (items, bits)),
+        ("g_r", (items, bits)),
         ("t_s", (2, 3)),
         ("t_r", (2, 3)),
         ("w_s", (2, 3)),
         ("w_r", (2, 3)),
-        ("kv_s", (3, bits)),
-        ("kv_r", (3, bits)),
-        ("f_s", (items, 2, bits)),
-        ("f_r", (items, 2, bits)),
-        ("e_s", (items, 2, depth_size)),
-        ("e_r", (items, 2, depth_size)),
-        ("e_l", (items, 2)),
-        ("o_s", (2, 5)),
-        ("o_r", (2, 5)),
-        ("i_l", (4,)),
+        ("kv_s", (2, 2, bits)),
+        ("kv_r", (2, 2, bits)),
+        ("f_s", (items, bits)),
+        ("f_r", (items, bits)),
+        ("e_s", (items, depth_size)),
+        ("e_r", (items, depth_size)),
+        ("e_l", (items,)),
+        ("o_s", (2, 6)),
+        ("o_r", (2, 6)),
         ("p_s", (bits + depth_size,)),
         ("p_r", (bits + depth_size,)),
     ]
 
 
-INPUTS = ("x_in", "dy_in", "vectors", "biases", "places")
+VECTORS = ("attn_gain", "attn_shift", "mlp_gain", "mlp_shift")
+BIASES = ("b_query", "b_key", "b_value", "b_up")
+INPUTS = ("blocks", "x_in", "dy_in", "freqs") + VECTORS + BIASES
 INPUTS += ("w_query", "w_key", "w_value", "w_out", "w_up", "w_down")
-OUTPUTS = ("layer_output", "input_grad", "g_query", "g_key", "g_value", "g_out", "g_up", "g_down")
-OUTPUTS += ("norm_sums", "b_query", "b_key", "b_value", "b_up", "b_sum")
+OUTPUTS = ("fin", "g_query", "g_key", "g_value", "g_out", "g_up", "g_down")
+OUTPUTS += ("norm_sums", "s_query", "s_key", "s_value", "s_up", "s_dy")
 
 
 class Bag:
@@ -607,8 +602,9 @@
     my_cols = pl.ds(pl.multiple_of(at.tp * half, half), half)
     her_cols = pl.ds(pl.multiple_of((1 - at.tp) * half, half), half)
 
-    items = [(("r", 0), ("r", 1)), (("r", 2), ("c", 0))]
-    items += [(("r", 3 + i), ("c", 1 + i)) for i in range(ff_chunks)]
+    units = [("r", 0), ("r", 1), ("r", 2), ("c", 0)]
+    for i in range(ff_chunks):
+        units += [("r", 3 + i), ("c", 1 + i)]
     row_pairs = [(m.w_query, m.g_query), (m.w_key, m.g_key), (m.w_value, m.g_value)]
 
     def outer(kind, a, depth, which):
@@ -630,39 +626,23 @@
     weights, grads, landing = (m.wr, m.wc), (m.gr, m.gc), (m.lr, m.lc)
 
     def z_start(k):
-        copies = []
-        for j, (kind, a) in enumerate(items[k]):
-            for s in range(1, depth_size):
-                copies.append(
-                    remote(
-                        outer(kind, a, peer(s), 0),
-                        part(weights, kind, a, own_block, 1),
-                        m.z_s.at[k, j, s],
-                        m.z_r.at[k, j, s],
-                        at.along(s),
-                    )
-                )
-        for j, (kind, a) in enumerate(items[k]):
-            copies.append(
-                local(outer(kind, a, at.depth, 0), part(weights, kind, a, own_block, 1), m.z_l.at[k, j])
-            )
+        kind, a = units[k]
+        into = part(weights, kind, a, own_block, 1)
+        copies = [
+            remote(outer(kind, a, peer(s), 0), into, m.z_s.at[k, s], m.z_r.at[k, s], at.along(s))
+            for s in range(1, depth_size)
+        ]
+        copies.append(local(outer(kind, a, at.depth, 0), into, m.z_l.at[k]))
         return copies
 
     def z_wait(copies):
-        for copy in copies[:-2]:
-            copy.wait_recv()
-        sends.extend(copies[:-2])
-        for copy in copies[-2:]:
-            copy.wait()
+        received(copies[:-1])
+        copies[-1].wait()
 
     def g_start(k, stage):
-        copies = []
-        for j, (kind, a) in enumerate(items[k]):
-            held = part(weights, kind, a, at.base(stage) * depth_size, 2**stage * depth_size)
-            copies.append(
-                remote(held, held, m.g_s.at[k, j, stage], m.g_r.at[k, j, stage], at.across(stage))
-            )
-        return copies
+        kind, a = units[k]
+        held = part(weights, kind, a, at.base(stage) * depth_size, 2**stage * depth_size)
+        return [remote(held, held, m.g_s.at[k, stage], m.g_r.at[k, stage], at.across(stage))]
 
     def received(copies):
         for copy in copies:
@@ -675,55 +655,52 @@
         settled.extend(copies)
 
     def fold_start(k, stage):
+        kind, a = units[k]
         size = 2**stage
         other = at.base(stage) + (1 - 2 * at.bit(stage)) * size
         return [
             remote(
                 part(grads, kind, a, other * depth_size, size * depth_size),
                 part(landing, kind, a, (size - 1) * depth_size, size * depth_size),
-                m.f_s.at[k, j, stage],
-                m.f_r.at[k, j, stage],
+                m.f_s.at[k, stage],
+                m.f_r.at[k, stage],
                 at.across(stage),
             )
-            for j, (kind, a) in enumerate(items[k])
         ]
 
     def fold_finish(k, stage, copies):
         received(copies)
+        kind, a = units[k]
         size = 2**stage
         own = at.base(stage) * depth_size
-        for kind, a in items[k]:
-
-            def add(i, _, kind=kind, a=a):
-                mine = blocks(own + i, 1)
-                theirs = blocks((size - 1) * depth_size + i, 1)
-                if kind == "r":
-                    total = m.gr[a, mine, :].astype(F32) + m.lr[a, theirs, :].astype(F32)
-                    m.gr[a, mine, :] = total.astype(BF)
-                else:
-                    total = m.gc[a, :, mine].astype(F32) + m.lc[a, :, theirs].astype(F32)
-                    m.gc[a, :, mine] = total.astype(BF)
-                return 0
-
-            lax.fori_loop(0, size * depth_size, add, 0)
+
+        def add(i, _):
+            mine = blocks(own + i, 1)
+            theirs = blocks((size - 1) * depth_size + i, 1)
+            if kind == "r":
+                total = m.gr[a, mine, :].astype(F32) + m.lr[a, theirs, :].astype(F32)
+                m.gr[a, mine, :] = total.astype(BF)
+            else:
+                total = m.gc[a, :, mine].astype(F32) + m.lc[a, :, theirs].astype(F32)
+                m.gc[a, :, mine] = total.astype(BF)
+            return 0
+
+        lax.fori_loop(0, size * depth_size, add, 0)
 
     def end_start(k):
-        copies = []
-        for j, (kind, a) in enumerate(items[k]):
-            for s in range(1, depth_size):
-                copies.append(
-                    remote(
-                        part(grads, kind, a, at.slot * depth_size + peer(s), 1),
-                        outer(kind, a, at.depth, 1),
-                        m.e_s.at[k, j, s],
-                        m.e_r.at[k, j, s],
-                        at.along(s),
-                    )
-                )
-        for j, (kind, a) in enumerate(items[k]):
-            copies.append(
-                local(part(grads, kind, a, own_block, 1), outer(kind, a, at.depth, 1), m.e_l.at[k, j])
+        kind, a = units[k]
+        into = outer(kind, a, at.depth, 1)
+        copies = [
+            remote(
+                part(grads, kind, a, at.slot * depth_size + peer(s), 1),
+                into,
+                m.e_s.at[k, s],
+                m.e_r.at[k, s],
+                at.along(s),
             )
+            for s in range(1, depth_size)
+        ]
+        copies.append(local(part(grads, kind, a, own_block, 1), into, m.e_l.at[k]))
         return copies
 
     near = {"ctx": at.ctx + (1 - 2 * (at.depth % 2)) * group}
@@ -757,10 +734,11 @@
             )
         return copies
 
-    def kv_start(stage):
+    def kv_start(h, stage):
         size = 2**stage * tokens
-        held = m.kv.at[pl.ds(pl.multiple_of(at.base(stage) * tokens, tokens), size), :]
-        return remote(held, held, m.kv_s.at[0, stage], m.kv_r.at[0, stage], at.across(stage))
+        rows_held = pl.ds(pl.multiple_of(at.base(stage) * tokens, tokens), size)
+        held = m.kv.at[rows_held, slice(h * HD, (h + 1) * HD)]
+        return remote(held, held, m.kv_s.at[0, h, stage], m.kv_r.at[0, h, stage], at.across(stage))
 
     spare = (m.lr.at[1 + ff_chunks], m.lr.at[2 + ff_chunks])
 
@@ -773,8 +751,8 @@
             remote(
                 m.kv.at[given, slice(h * HD, (h + 1) * HD)],
                 spare[h].at[taken, :],
-                m.kv_s.at[1 + h, stage],
-                m.kv_r.at[1 + h, stage],
+                m.kv_s.at[1, h, stage],
+                m.kv_r.at[1, h, stage],
                 at.across(stage),
             )
             for h in range(2)
@@ -797,6 +775,8 @@
 
         lax.fori_loop(0, size * tokens // step, add, 0)
 
+    lane = lax.broadcasted_iota(jnp.int32, (1, 128), 1)
+
     def place_rows():
         mine = token_rows(at.depth)
         for b in range(block_count):
@@ -805,7 +785,27 @@
             out_of = slice(c * depth_rows, (c + 1) * depth_rows)
             m.x[mine, into] = m.x_in[:, out_of]
             m.dy[mine, into] = m.dy_in[:, out_of]
-            m.gv[:, into] = m.vectors[:, out_of]
+
+    def place_vectors():
+        m.ps[0] = jnp.zeros_like(m.ps[0])
+        for row, name in enumerate(VECTORS):
+            for b in range(block_count):
+                c = natural[b]
+                m.gv[row : row + 1, b * depth_rows : (b + 1) * depth_rows] = getattr(m, name)[c : c + 1, :]
+        per_head = HD // 128
+        for a in range(3):
+            for h in range(per_head):
+                row = getattr(m, BIASES[a])[pl.ds(at.depth * per_head + h, 1), :]
+                m.biases[a : a + 1, h * 128 : (h + 1) * 128] = row
+        for i in range(ff_chunks):
+            for h in range(per_head):
+                row = m.b_up[pl.ds((at.depth * ff_chunks + i) * per_head + h, 1), :]
+                m.biases[3 + i : 4 + i, h * 128 : (h + 1) * 128] = row
+        block_rows = rows // 2
+        for n in range(group * depth_size):
+            c = natural[n]
+            first = jnp.where(lane < block_rows, m.blocks[2 * c], m.blocks[2 * c + 1])
+            m.places[n : n + 1, :] = (first * block_rows + lane % block_rows).astype(F32)
 
     def affine():
         step = 32
@@ -834,17 +834,14 @@
 
         lax.fori_loop(0, depth_size, body, 0)
 
-    lane = lax.broadcasted_iota(jnp.int32, (1, 128), 1)
-
     def place_column(n):
-        row = jnp.broadcast_to(m.places[pl.ds(n, 1), :].astype(F32), (128, 128))
-        return row.T
+        return jnp.broadcast_to(m.places[pl.ds(n, 1), :], (128, 128)).T
 
     def make_tables():
         def body(n, _):
-            angles = place_column(n) * m.vectors[5:6, :128]
+            angles = place_column(n) * m.freqs[0:1, :]
             here = pl.ds(pl.multiple_of(n * 128, 128), 128)
-            m.tab[here, :] = jnp.cos(angles - m.vectors[6:7, :128])
+            m.tab[here, :] = jnp.cos(angles - jnp.where(lane < ROT, 0.0, math.pi / 2))
             return 0
 
         lax.fori_loop(0, group * tokens // 128, body, 0)
@@ -865,11 +862,12 @@
     kv_own = pl.ds(pl.multiple_of(at.slot * tokens, tokens), tokens)
     score_scale = 1.0 / math.sqrt(HD)
 
-    def make_query_key():
+    def make_query():
         query = project(0)
-        head = turned(query, kv_own, 1.0)
-        m.q[:, :128] = head.astype(BF)
+        m.q[:, :128] = turned(query, kv_own, 1.0).astype(BF)
         m.q[:, 128:] = query[:, 128:].astype(BF)
+
+    def make_keys():
         keys = project(1)
         m.kv[kv_own, :128] = turned(keys, kv_own, 1.0).astype(BF)
         m.kv[kv_own, 128:HD] = keys[:, 128:].astype(BF)
@@ -885,7 +883,7 @@
         count = tokens // 128
         column = jnp.concatenate([place_column(j * count + n)[:, :1] for n in range(count)], 0)
         row = jnp.concatenate([m.places[pl.ds(at.slot * count + n, 1), :] for n in range(count)], 1)
-        return jnp.where(column <= row.astype(F32), scores, DROP)
+        return jnp.where(column <= row, scores, DROP)
 
     def attend(j):
         scores = masked_scores(j)
@@ -964,12 +962,13 @@
 
         lax.fori_loop(0, width // ROW_TILE, body, 0)
 
-        def body_out(n, _):
+    def out_grads():
+        def body(n, _):
             tile = pl.ds(pl.multiple_of(n * 512, 512), 512)
             m.gc[0, :, tile] = mm(m.alt[...], m.dy[:, tile]).astype(BF)
             return 0
 
-        lax.fori_loop(0, width // 512, body_out, 0)
+        lax.fori_loop(0, width // 512, body, 0)
 
     def feed_forward(i):
         activated, slope = gelu_parts(mm(m.nm[...], m.wr[3 + i]) + m.biases[3 + i : 4 + i, :])
@@ -1020,39 +1019,54 @@
         small_add_rows(78, n, m.dy[:, tile].astype(F32))
         back[:, tile] = (attn_back * m.gv[0:1, tile] + mlp_back * m.gv[2:3, tile]).astype(BF)
 
-    def end_half(piece, which):
-        count = half // ROW_TILE
-
-        def body(n, _):
-            piece(which * count + n)
+    def end_quarter(piece, which, n):
+        count = quarter // ROW_TILE
+        odd = at.depth % 2
+        first = which * 2 + (odd if n else 1 - odd)
+
+        def body(i, _):
+            piece(first * count + i)
             return 0
 
         lax.fori_loop(0, count, body, 0)
 
-    swap_in = (m.nm.at[:, 0:half], m.nm.at[:, half : 2 * half])
+    ends = (out, back)
+
+    def quarter_of(which, n):
+        odd = at.depth % 2
+        return pl.ds(pl.multiple_of(which * half + (odd if n else 1 - odd) * quarter, quarter), quarter)
 
     def offer():
         pl.semaphore_signal(m.free, inc=1, device_id=at.twin(), device_id_type=MESH)
 
-    def sum_start(i):
-        if i == 0:
+    def sum_start(i, n):
+        if i == n == 0:
             pl.semaphore_wait(m.free, 1)
-        return remote(ends[i].at[:, her_cols], swap_in[i], m.o_s.at[i, 0], m.o_r.at[i, 0], at.twin())
-
-    ends = (out, back)
+        return remote(
+            ends[i].at[:, quarter_of(1 - at.tp, n)],
+            m.nm.at[:, quarter_of(i, n)],
+            m.o_s.at[i, n],
+            m.o_r.at[i, n],
+            at.twin(),
+        )
+
+    def sum_add(i, n):
+        mine = ends[i]
+        into, source = quarter_of(at.tp, n), quarter_of(i, n)
+
+        def add(z, _):
+            block = token_rows(z)
+            total = mine[block, into].astype(F32) + m.nm[block, source].astype(F32)
+            mine[block, into] = total.astype(BF)
+            return 0
+
+        lax.fori_loop(0, depth_size, add, 0)
 
     def sum_step(i, step, copy):
         received([copy])
         mine = ends[i]
         if step == 0:
-
-            def add(z, _):
-                block = token_rows(z)
-                total = mine[block, my_cols].astype(F32) + swap_in[i][block, :].astype(F32)
-                mine[block, my_cols] = total.astype(BF)
-                return 0
-
-            lax.fori_loop(0, depth_size, add, 0)
+            sum_add(i, 0)
             source, into, there = mine.at[her_pair, her_quarter], m.tz.at[i, 0], near
         elif step == 1:
             total = mine[her_pair, my_quarter].astype(F32) + m.tz[i, 0].astype(F32)
@@ -1066,60 +1080,7 @@
             total = mine[token_rows(at.depth), my_cols].astype(F32) + m.te[i].astype(F32)
             m.fin[i, :, my_cols] = total.astype(BF)
             source, into, there = m.fin.at[i, :, my_cols], m.fin.at[i, :, my_cols], at.twin()
-        return remote(source, into, m.o_s.at[i, 1 + step], m.o_r.at[i, 1 + step], there)
-
-    def stage_of(column):
-        piece = column // tokens
-        return (m.att, m.dqt)[piece // 2], piece % 2 * rows, column % tokens
-
-    def finish_rows():
-        step = 16
-
-        def body(i, _):
-            here = pl.ds(pl.multiple_of(i * step, step), step)
-            x = m.x_in[here, :].astype(F32)
-            dy = m.dy_in[here, :].astype(F32)
-            here_all = pl.ds(pl.multiple_of(at.depth * rows + i * step, step), step)
-            inverse = m.inv[here_all, :]
-            normal = (x - m.mean[here_all, :]) * inverse
-            total = jnp.zeros((step, 1), F32)
-            against = jnp.zeros((step, 1), F32)
-            pieces = {}
-            for b in range(block_count):
-                c = natural[b]
-                out_of = slice(b * depth_rows, (b + 1) * depth_rows)
-                into = slice(c * depth_rows, (c + 1) * depth_rows)
-                m.layer_output[here, into] = (
-                    x[:, into] + m.fin[0, here, out_of].astype(F32) + m.vectors[4:5, into]
-                ).astype(BF)
-                pieces[b] = m.fin[1, here, out_of].astype(F32)
-                total += jnp.sum(pieces[b], -1, keepdims=True)
-                against += jnp.sum(pieces[b] * normal[:, into], -1, keepdims=True)
-            total = total / width
-            against = against / width
-            for b in range(block_count):
-                c = natural[b]
-                into = slice(c * depth_rows, (c + 1) * depth_rows)
-                staged, first, cols = stage_of(c * depth_rows)
-                there = pl.ds(pl.multiple_of(first + i * step, step), step)
-                staged[there, cols : cols + depth_rows] = dy[:, into] + inverse * (
-                    pieces[b] - total - normal[:, into] * against
-                )
-            return 0
-
-        lax.fori_loop(0, rows // step, body, 0)
-        copies = []
-        for n in range(width // tokens):
-            staged, first, _ = stage_of(n * tokens)
-            copies.append(
-                local(
-                    staged.at[first : first + rows, :],
-                    m.input_grad.at[:, n * tokens : (n + 1) * tokens],
-                    m.i_l.at[n],
-                )
-            )
-        for copy in copies:
-            copy.wait()
+        return remote(source, into, m.o_s.at[i, 2 + step], m.o_r.at[i, 2 + step], there)
 
     def small_group(stage):
         return remote(m.ps.at[stage], m.pl.at[stage], m.p_s.at[stage], m.p_r.at[stage], at.across(stage))
@@ -1153,12 +1114,12 @@
                 into = v * 16 + natural[b]
                 m.norm_sums[into : into + 1, :] = m.px[0, row : row + 1, :] + m.px[1, row : row + 1, :]
         for b in range(block_count):
-            m.b_sum[natural[b] : natural[b] + 1, :] = m.ps[bits, 78 + b : 79 + b, :]
+            m.s_dy[natural[b] : natural[b] + 1, :] = m.ps[bits, 78 + b : 79 + b, :]
         for z in range(depth_size):
-            m.b_query[2 * z : 2 * z + 2, :] = m.pz[z, 64:66, :]
-            m.b_key[2 * z : 2 * z + 2, :] = m.pz[z, 66:68, :]
-            m.b_value[2 * z : 2 * z + 2, :] = m.pz[z, 68:70, :]
-            m.b_up[8 * z : 8 * z + 8, :] = m.pz[z, 70:78, :]
+            m.s_query[2 * z : 2 * z + 2, :] = m.pz[z, 64:66, :]
+            m.s_key[2 * z : 2 * z + 2, :] = m.pz[z, 66:68, :]
+            m.s_value[2 * z : 2 * z + 2, :] = m.pz[z, 68:70, :]
+            m.s_up[8 * z : 8 * z + 8, :] = m.pz[z, 70:78, :]
 
     live = {}
     swapped = {0: [], 1: []}
@@ -1186,30 +1147,35 @@
         elif name == "te":
             received(swapped[n])
         elif name == "norm":
-            m.ps[0] = jnp.zeros_like(m.ps[0])
             place_rows()
+        elif name == "vec":
+            place_vectors()
         elif name == "tab":
             make_tables()
         elif name == "aff":
             affine()
-        elif name == "qk":
-            make_query_key()
+        elif name == "qq":
+            make_query()
+        elif name == "kk":
+            make_keys()
+        elif name == "go":
+            out_grads()
         elif name == "val":
             make_values()
         elif name == "ky":
-            live["k", 0] = kv_start(0)
+            live["k", n] = [kv_start(n, 0)]
         elif name == "kc":
-            received([live["k", 0]])
-            live["k", 1] = kv_start(1)
+            received(live["k", n])
+            live["k", n].append(kv_start(n, 1))
         elif name == "kw":
-            received([live["k", 1]])
+            received(live["k", n][1:])
         elif name == "at":
             attend(n)
         elif name == "hg":
             head_grads()
         elif name == "bw":
             if n == 0:
-                settle([live["k", 0], live["k", 1]])
+                settle(live["k", 0] + live["k", 1])
             attend_back(n)
         elif name == "dc":
             live["d"] = dkv_start(1)
@@ -1233,15 +1199,18 @@
         elif name == "of":
             offer()
         elif name == "eo":
-            end_half(end_out, at.tp if n else 1 - at.tp)
+            end_quarter(end_out, at.tp if n >= 2 else 1 - at.tp, n % 2)
         elif name == "eb":
             if n == 0:
                 settle(live["t", 1] + swapped[1])
-            end_half(end_back, at.tp if n else 1 - at.tp)
+            end_quarter(end_back, at.tp if n >= 2 else 1 - at.tp, n % 2)
         elif name == "sx":
-            live["s", n] = sum_start(n)
+            live["sx", n] = sum_start(n // 2, n % 2)
         elif name == "sa":
-            live["s", n] = sum_step(n, 0, live["s", n])
+            live["s", n] = sum_step(n, 0, live["sx", 2 * n])
+        elif name == "sm":
+            received([live["sx", 2 * n + 1]])
+            sum_add(n, 1)
         elif name == "sb":
             live["s", n] = sum_step(n, 1, live["s", n])
         elif name == "sc":
@@ -1262,12 +1231,9 @@
             live["p"] = small_twin(live["p"])
         elif name == "pe":
             small_finish(live["p"])
-        elif name == "fin":
-            finish_rows()
         elif name == "ew":
-            received(live["e", n][:-2])
-            for copy in live["e", n][-2:]:
-                copy.wait()
+            received(live["e", n][:-1])
+            live["e", n][-1].wait()
 
     for entry in SCHEDULE:
         name = entry.rstrip("0123456789")
@@ -1278,15 +1244,20 @@
 
 
 SCHEDULE = (
-    "zs0", "norm", "ta0", "zy0", "zs1", "tb0", "zs2", "zs5", "zy1", "tc0", "ta1", "yc1",
-    "cw1", "zy2", "td0", "tab", "yc0", "zy5", "tb1", "te0", "aff", "yc2", "cw0", "zs3",
-    "qk", "val", "tc1", "yc5", "ky", "zs4", "zy3", "kc", "td1", "kw", "at0", "at1",
-    "te1", "cw2", "zy4", "ff0", "at2", "fc2", "cw5", "at3", "hg", "bw0", "bw1", "bw2",
-    "bw3", "dc", "ff3", "yc3", "dy", "yc4", "cw3", "fy2", "cw4", "ff2", "ff1", "fc3",
-    "dw", "ag", "eo0", "of0", "sx0", "fc0", "fy3", "eb0", "fz2", "fc1", "fy0", "fz3",
-    "fc4", "sx1", "eb1", "pa", "fc5", "pb", "fz0", "fy4", "ew3", "eo1", "pc", "sa0",
-    "ew0", "fz4", "sb0", "sa1", "fy5", "ew4", "fy1", "sb1", "ew2", "fz5", "pd", "sc0",
-    "sc1", "fz1", "sd0", "sd1", "ew5", "sw0", "pe", "sw1", "fin", "ew1",
+    "zs1", "vec", "zs6", "zs4", "zy1", "norm", "ta0", "zy6", "zs7", "zs5", "tb0", "zs2",
+    "yc1", "ta1", "zs3", "zy4", "tab", "zy5", "zy7", "yc5", "tc0", "zs9", "cw1", "yc7",
+    "zy2", "zs0", "zy3", "td0", "yc2", "cw2", "tb1", "zy9", "yc6", "te0", "zs8", "zy0",
+    "aff", "kk", "ky0", "val", "ky1", "yc0", "yc4", "tc1", "yc3", "cw3", "zs11", "kc0",
+    "zy8", "cw0", "cw4", "yc9", "td1", "zs10", "kc1", "qq", "zy11", "kw1", "cw7", "kw0",
+    "cw6", "at0", "cw9", "at1", "at2", "yc8", "at3", "te1", "ff1", "fc6", "fc7", "zy10",
+    "hg", "bw0", "cw8", "bw1", "bw2", "bw3", "dc", "cw5", "fy7", "go", "fc3", "yc10",
+    "ff0", "dy", "fz7", "ff2", "yc11", "fc4", "cw10", "fy3", "cw11", "ff3", "dw", "of0",
+    "fy6", "fc9", "ag", "eo0", "fz3", "sx0", "fc0", "eb0", "eb1", "fy9", "fc2", "fz6",
+    "fy0", "fc8", "eb2", "sx2", "fc5", "eo2", "fy4", "fz9", "sx3", "fc10", "fz0", "fy5",
+    "fz4", "fc11", "sa1", "fy11", "eb3", "pa", "fz5", "eo3", "sm1", "fc1", "pb", "eo1",
+    "sb1", "sx1", "sa0", "fy8", "fy1", "fz11", "ew4", "fz1", "fy2", "ew9", "sm0", "ew5",
+    "fy10", "sb0", "pc", "fz8", "sc1", "ew7", "sc0", "ew0", "ew11", "fz2", "ew3", "fz10",
+    "sd1", "sd0", "pd", "pe", "sw0", "ew8", "sw1", "ew2", "ew10", "ew1", "ew6",
 )
 
 
@@ -1328,19 +1299,14 @@
     tokens = depth_size * rows
     at = Place(depth_size, group)
 
-    places = token_places(block_order, depth_size, group, rows).reshape(-1, 128)
-    freqs = 10000.0 ** (-(2.0 * jnp.arange(ROT // 2, dtype=F32)) / ROT)
-    phases = jnp.repeat(jnp.array([0.0, math.pi / 2], F32), 64)
-    vectors = jnp.stack(
-        [attn_gain, attn_shift, mlp_gain, mlp_shift, b_out + b_down]
-        + [jnp.tile(freqs, width // (ROT // 2)), jnp.tile(phases, width // 128), b_out]
-    )
-    per_head = [bias.reshape(depth_size, 1, HD) for bias in (b_query, b_key, b_value)]
-    per_head += [b_up.reshape(depth_size, ff_chunks, CHUNK), jnp.zeros((depth_size, 1, CHUNK), F32)]
-    biases = lax.dynamic_index_in_dim(jnp.concatenate(per_head, 1), at.depth, 0, keepdims=False)
+    freqs = (10000.0 ** (-(2.0 * np.arange(ROT // 2, dtype=np.float32)) / ROT)).astype(np.float32)
+    freqs = np.tile(freqs, (8, 128 // (ROT // 2)))
+
+    def in_rows(vector):
+        return vector.reshape(-1, 128)
 
     buffers = layout_of(depth_size, group, depth_rows, rows, width, ff_chunks)
-    semaphores = semaphores_of(depth_size, group, 2 + ff_chunks)
+    semaphores = semaphores_of(depth_size, group, 4 + 2 * ff_chunks)
     names = tuple(INPUTS) + tuple(OUTPUTS) + tuple(b[0] for b in buffers) + tuple(s[0] for s in semaphores) + ("free",)
     vmem = pl.BlockSpec(memory_space=pltpu.VMEM)
     hbm = pl.BlockSpec(memory_space=pl.ANY)
@@ -1349,8 +1315,7 @@
     results = pl.pallas_call(
         functools.partial(fused_kernel, names, depth_size, group),
         out_shape=(
-            shape((rows, width), BF),
-            shape((rows, width), F32),
+            shape((2, rows, width), BF),
             shape((depth_rows, wide), BF),
             shape((depth_rows, wide), BF),
             shape((depth_rows, wide), BF),
@@ -1364,8 +1329,8 @@
             shape((thin // 128, 128), F32),
             shape((width // 128, 128), F32),
         ),
-        in_specs=[vmem] * 5 + [hbm] * 6,
-        out_specs=(vmem,) + (hbm,) * 7 + (vmem,) * 6,
+        in_specs=[pl.BlockSpec(memory_space=pltpu.SMEM)] + [vmem] * 11 + [hbm] * 6,
+        out_specs=(vmem,) + (hbm,) * 6 + (vmem,) * 6,
         scratch_shapes=[pltpu.VMEM(s, t) for _, s, t in buffers]
         + [pltpu.SemaphoreType.DMA(s) for _, s in semaphores]
         + [pltpu.SemaphoreType.REGULAR],
@@ -1373,11 +1338,12 @@
             collective_id=4, has_side_effects=True, vmem_limit_bytes=VMEM_BYTES
         ),
     )(
+        block_order,
         layer_input,
         out_grad,
-        vectors,
-        biases,
-        places,
+        freqs,
+        *[in_rows(v) for v in (attn_gain, attn_shift, mlp_gain, mlp_shift)],
+        *[in_rows(v) for v in (b_query, b_key, b_value, b_up)],
         w_query,
         w_key,
         w_value,
@@ -1385,25 +1351,87 @@
         w_up,
         w_down,
     )
-    output, input_grad = results[:2]
-    weight_grads = [grad.astype(F32) for grad in results[2:8]]
-    norm_sums = results[8].reshape(4, width)
-    small = [result.reshape(-1) for result in results[9:]]
-    return (
-        output,
-        input_grad,
-        *weight_grads,
-        small[0],
-        small[1],
-        small[2],
-        small[4],
-        small[3],
-        small[4],
-        norm_sums[0],
-        norm_sums[1],
-        norm_sums[2],
-        norm_sums[3],
+    sums, *parts = results
+    output, input_grad, *rest = close(
+        depth_size, group, layer_input, out_grad, sums, in_rows(b_out), in_rows(b_down), parts
     )
+    small = [vector.reshape(-1) for vector in rest[6:]]
+    norms, (to_query, to_key, to_value, to_up, to_dy, again) = small[:4], small[4:]
+    return (output, input_grad, *rest[:6], to_query, to_key, to_value, to_dy, to_up, again, *norms)
+
+
+def close_kernel(depth_size, group, x_in, dy_in, sums, b_out, b_down, *refs):
+    grads, (norm_sums, *small), results = refs[:6], refs[6:12], refs[12:]
+    layer_output, input_grad, wide, norms, others = (
+        results[0],
+        results[1],
+        results[2:8],
+        results[8:12],
+        results[12:],
+    )
+    for source, into in zip(grads, wide, strict=True):
+        into[...] = source[...].astype(F32)
+    for v, into in enumerate(norms):
+        count = into.shape[0]
+        into[...] = norm_sums[v * count : (v + 1) * count, :]
+    for source, into in zip(small + small[-1:], others, strict=True):
+        into[...] = source[...]
+    x = x_in[...].astype(F32)
+    width = x.shape[1]
+    natural = natural_blocks(depth_size, group)
+    size = width // len(natural)
+    centered = x - jnp.mean(x, -1, keepdims=True)
+    inverse = lax.rsqrt(jnp.mean(centered * centered, -1, keepdims=True) + norm_epsilon)
+    normal = centered * inverse
+    total = jnp.zeros((x.shape[0], 1), F32)
+    against = jnp.zeros((x.shape[0], 1), F32)
+    for b, c in enumerate(natural):
+        out_of, into = slice(b * size, (b + 1) * size), slice(c * size, (c + 1) * size)
+        bias = b_out[c : c + 1, :] + b_down[c : c + 1, :]
+        layer_output[:, into] = (x[:, into] + sums[0, :, out_of].astype(F32) + bias).astype(BF)
+        piece = sums[1, :, out_of].astype(F32)
+        total += jnp.sum(piece, -1, keepdims=True)
+        against += jnp.sum(piece * normal[:, into], -1, keepdims=True)
+    total, against = total / width, against / width
+    for b, c in enumerate(natural):
+        out_of, into = slice(b * size, (b + 1) * size), slice(c * size, (c + 1) * size)
+        piece = sums[1, :, out_of].astype(F32) - total - normal[:, into] * against
+        input_grad[:, into] = dy_in[:, into].astype(F32) + inverse * piece
+
+
+def close(depth_size, group, x_in, dy_in, sums, b_out, b_down, parts):
+    rows, width = x_in.shape
+    steps = rows // 64
+    grads, small = parts[:6], parts[6:]
+    norms = [jax.ShapeDtypeStruct((width // 128, 128), F32)] * 4
+    copies = [jax.ShapeDtypeStruct(s.shape, F32) for s in small[1:] + small[-1:]]
+
+    def by_rows(shape):
+        block = shape[:-2] + (shape[-2] // steps, shape[-1])
+        return pl.BlockSpec(block, lambda i: (0,) * (len(shape) - 2) + (i, 0))
+
+    def all_of(shape):
+        return pl.BlockSpec(shape, lambda i: (0,) * len(shape))
+
+    return pl.pallas_call(
+        functools.partial(close_kernel, depth_size, group),
+        grid=(steps,),
+        out_shape=[
+            jax.ShapeDtypeStruct(x_in.shape, BF),
+            jax.ShapeDtypeStruct(x_in.shape, F32),
+            *[jax.ShapeDtypeStruct(g.shape, F32) for g in grads],
+            *norms,
+            *copies,
+        ],
+        in_specs=[by_rows(x_in.shape)] * 2
+        + [by_rows(sums.shape), all_of(b_out.shape), all_of(b_down.shape)]
+        + [by_rows(g.shape) for g in grads]
+        + [all_of(s.shape) for s in small],
+        out_specs=[by_rows(x_in.shape)] * 2
+        + [by_rows(g.shape) for g in grads]
+        + [all_of(s.shape) for s in norms + copies],
+        compiler_params=pltpu.CompilerParams(vmem_limit_bytes=VMEM_BYTES),
+    )(x_in, dy_in, sums, b_out, b_down, *grads, *small)
 
 
 def shards(

time: 271 us -> 240 us (0.89)
  local copies, waits for them, and re-layouts: 12 us -> 0 us
  other arithmetic: 9.01 us -> 0 us
  Pallas kernels: 248 us -> 239 us
    pallas_call x1, Pallas kernels: 248 us -> 233 us  [fused_shards(): pl.pallas_call(functools.partial(fused_kernel, names, depth_size, group),...]
    convert_element_type x6 -> x0, other arithmetic: 7.66 us -> none  [fused_shards(): weight_grads = [grad.astype(F32) for grad in results[2:8]]]
    pallas_call x0 -> x1, Pallas kernels: none -> 5.59 us  [close(): pl.pallas_call(functools.partial(close_kernel, depth_size, group), grid=(...]
    unnamed x34 -> x0, local copies, waits for them, and re-layouts: 5.4 us -> none
where the time goes in v3:
time: 240 us
  Pallas kernels  239 us (100%)
    pallas_call x1, Pallas kernels, fused_shards(): pl.pallas_call(functools.partial(fused_kernel, names, depth_size, group),...  233 us
    pallas_call x1, Pallas kernels, close(): pl.pallas_call(functools.partial(close_kernel, depth_size, group), grid=(...  5.59 us

profile of v3, /device:TPU:0, one launch (start us, length us, event | category | flops | bytes accessed | tf_op | source)
XLA Modules:
  0.0 239.8 jit_solution(3862233816176874598)
XLA Ops:
  0.7 233.4 %shard_map.331 = (bf16[2,128,2048]{2,1,0:T(8,128)(2,1)}, bf16[128,1024]{1,0:T(8,128)(2,1)}, bf16[128,1024]{1,0:T(8,128)(2,1)}, bf16[128,1024]{1,0:T(8,128)(2,1)}...) custom-call(s32[32]{0:T(128)} %refs_0_.1, ...), custom_call_target="tpu_custom_call" | custom-call | tf_op jit(solution)/shard_map/pallas_call | solution.py:1315
  234.1 5.6 %shard_map.332 = (bf16[128,2048]{1,0:T(8,128)(2,1)}, f32[128,2048]{1,0:T(8,128)}, f32[128,1024]{1,0:T(8,128)}, f32[128,1024]{1,0:T(8,128)}, f32[128,1024]{1,0:T(...) custom-call(bf16[128,2048]{1,0:T(8,128)(2,1)} %x_in.1, ...), custom_call_target="tpu_custom_call" | custom-call | tf_op jit(solution)/shard_map/pallas_call | solution.py:1416

commit v4 on v3

--- a/solution.py
+++ b/solution.py
@@ -1121,144 +1121,300 @@
             m.s_value[2 * z : 2 * z + 2, :] = m.pz[z, 68:70, :]
             m.s_up[8 * z : 8 * z + 8, :] = m.pz[z, 70:78, :]
 
-    live = {}
+    z_live, g_live, t_live, k_live, f_live, e_live, x_live, s_live, d_live, p_live = ({} for _ in range(10))
     swapped = {0: [], 1: []}
     buffers = (m.x, m.dy)
 
-    def run(name, n):
-        if name == "zs":
-            live["z", n] = z_start(n)
-        elif name == "zy":
-            z_wait(live["z", n])
-            live["g", n] = g_start(n, 0)
-        elif name == "yc":
-            received(live["g", n])
-            live["g", n] = g_start(n, 1)
-        elif name == "cw":
-            received(live["g", n])
-        elif name == "ta":
-            live["t", n] = token_step(n, buffers[n], 0, [])
-        elif name == "tb":
-            token_step(n, buffers[n], 1, live["t", n])
-        elif name == "tc":
-            token_step(n, buffers[n], 2, live["t", n])
-        elif name == "td":
-            token_step(n, buffers[n], 3, live["t", n])
-        elif name == "te":
-            received(swapped[n])
-        elif name == "norm":
-            place_rows()
-        elif name == "vec":
-            place_vectors()
-        elif name == "tab":
-            make_tables()
-        elif name == "aff":
-            affine()
-        elif name == "qq":
-            make_query()
-        elif name == "kk":
-            make_keys()
-        elif name == "go":
-            out_grads()
-        elif name == "val":
-            make_values()
-        elif name == "ky":
-            live["k", n] = [kv_start(n, 0)]
-        elif name == "kc":
-            received(live["k", n])
-            live["k", n].append(kv_start(n, 1))
-        elif name == "kw":
-            received(live["k", n][1:])
-        elif name == "at":
-            attend(n)
-        elif name == "hg":
-            head_grads()
-        elif name == "bw":
-            if n == 0:
-                settle(live["k", 0] + live["k", 1])
-            attend_back(n)
-        elif name == "dc":
-            live["d"] = dkv_start(1)
-        elif name == "dy":
-            dkv_finish(1, live["d"])
-            live["d"] = dkv_start(0)
-        elif name == "dw":
-            dkv_finish(0, live["d"])
-        elif name == "ag":
-            attention_grads()
-        elif name == "ff":
-            feed_forward(n)
-        elif name == "fc":
-            live["f", n] = fold_start(n, 1)
-        elif name == "fy":
-            fold_finish(n, 1, live["f", n])
-            live["f", n] = fold_start(n, 0)
-        elif name == "fz":
-            fold_finish(n, 0, live["f", n])
-            live["e", n] = end_start(n)
-        elif name == "of":
-            offer()
-        elif name == "eo":
-            end_quarter(end_out, at.tp if n >= 2 else 1 - at.tp, n % 2)
-        elif name == "eb":
-            if n == 0:
-                settle(live["t", 1] + swapped[1])
-            end_quarter(end_back, at.tp if n >= 2 else 1 - at.tp, n % 2)
-        elif name == "sx":
-            live["sx", n] = sum_start(n // 2, n % 2)
-        elif name == "sa":
-            live["s", n] = sum_step(n, 0, live["sx", 2 * n])
-        elif name == "sm":
-            received([live["sx", 2 * n + 1]])
-            sum_add(n, 1)
-        elif name == "sb":
-            live["s", n] = sum_step(n, 1, live["s", n])
-        elif name == "sc":
-            live["s", n] = sum_step(n, 2, live["s", n])
-        elif name == "sd":
-            live["s", n] = sum_step(n, 3, live["s", n])
-        elif name == "sw":
-            received([live["s", n]])
-        elif name == "pa":
-            live["p"] = small_group(0)
-        elif name == "pb":
-            small_add(0, live["p"])
-            live["p"] = small_group(1)
-        elif name == "pc":
-            small_add(1, live["p"])
-            live["p"] = small_depth()
-        elif name == "pd":
-            live["p"] = small_twin(live["p"])
-        elif name == "pe":
-            small_finish(live["p"])
-        elif name == "ew":
-            received(live["e", n][:-1])
-            live["e", n][-1].wait()
-
-    for entry in SCHEDULE:
-        name = entry.rstrip("0123456789")
-        run(name, int(entry[len(name) :] or 0))
+    def do_zs(n):
+        z_live[n] = z_start(n)
+
+    def do_zy(n):
+        z_wait(z_live[n])
+        g_live[n] = g_start(n, 0)
+
+    def do_yc(n):
+        received(g_live[n])
+        g_live[n] = g_start(n, 1)
+
+    def do_cw(n):
+        received(g_live[n])
+
+    def do_ta(n):
+        t_live[n] = token_step(n, buffers[n], 0, [])
+
+    def do_tb(n):
+        token_step(n, buffers[n], 1, t_live[n])
+
+    def do_tc(n):
+        token_step(n, buffers[n], 2, t_live[n])
+
+    def do_td(n):
+        token_step(n, buffers[n], 3, t_live[n])
+
+    def do_te(n):
+        received(swapped[n])
+
+    do_norm, do_vec, do_tab, do_aff = place_rows, place_vectors, make_tables, affine
+    do_qq, do_kk, do_val, do_hg = make_query, make_keys, make_values, head_grads
+    do_at, do_ag, do_go, do_ff, do_of = attend, attention_grads, out_grads, feed_forward, offer
+
+    def do_ky(n):
+        k_live[n] = [kv_start(n, 0)]
+
+    def do_kc(n):
+        received(k_live[n])
+        k_live[n].append(kv_start(n, 1))
+
+    def do_kw(n):
+        received(k_live[n][1:])
+
+    def do_bw(n):
+        if n == 0:
+            settle(k_live[0] + k_live[1])
+        attend_back(n)
+
+    def do_dc():
+        d_live[1] = dkv_start(1)
+
+    def do_dy():
+        dkv_finish(1, d_live[1])
+        d_live[0] = dkv_start(0)
+
+    def do_dw():
+        dkv_finish(0, d_live[0])
+
+    def do_fc(n):
+        f_live[n] = fold_start(n, 1)
+
+    def do_fy(n):
+        fold_finish(n, 1, f_live[n])
+        f_live[n] = fold_start(n, 0)
+
+    def do_fz(n):
+        fold_finish(n, 0, f_live[n])
+        e_live[n] = end_start(n)
+
+    def do_ew(n):
+        received(e_live[n][:-1])
+        e_live[n][-1].wait()
+
+    def do_eo(n):
+        end_quarter(end_out, at.tp if n >= 2 else 1 - at.tp, n % 2)
+
+    def do_eb(n):
+        if n == 0:
+            settle(t_live[1] + swapped[1])
+        end_quarter(end_back, at.tp if n >= 2 else 1 - at.tp, n % 2)
+
+    def do_sx(n):
+        x_live[n] = sum_start(n // 2, n % 2)
+
+    def do_sa(n):
+        s_live[n] = sum_step(n, 0, x_live[2 * n])
+
+    def do_sm(n):
+        received([x_live[2 * n + 1]])
+        sum_add(n, 1)
+
+    def do_sb(n):
+        s_live[n] = sum_step(n, 1, s_live[n])
+
+    def do_sc(n):
+        s_live[n] = sum_step(n, 2, s_live[n])
+
+    def do_sd(n):
+        s_live[n] = sum_step(n, 3, s_live[n])
+
+    def do_sw(n):
+        received([s_live[n]])
+
+    def do_pa():
+        p_live[0] = small_group(0)
+
+    def do_pb():
+        small_add(0, p_live[0])
+        p_live[1] = small_group(1)
+
+    def do_pc():
+        small_add(1, p_live[1])
+        p_live[2] = small_depth()
+
+    def do_pd():
+        p_live[3] = small_twin(p_live[2])
+
+    def do_pe():
+        small_finish(p_live[3])
+
+    do_zs(1)
+    do_vec()
+    do_zs(6)
+    do_zs(4)
+    do_zy(1)
+    do_norm()
+    do_ta(0)
+    do_zy(6)
+    do_zs(7)
+    do_zs(5)
+    do_tb(0)
+    do_zs(2)
+    do_yc(1)
+    do_ta(1)
+    do_zs(3)
+    do_zy(4)
+    do_tab()
+    do_zy(5)
+    do_zy(7)
+    do_yc(5)
+    do_tc(0)
+    do_zs(9)
+    do_cw(1)
+    do_yc(7)
+    do_zy(2)
+    do_zs(0)
+    do_zy(3)
+    do_td(0)
+    do_yc(2)
+    do_cw(2)
+    do_tb(1)
+    do_zy(9)
+    do_yc(6)
+    do_te(0)
+    do_zs(8)
+    do_zy(0)
+    do_aff()
+    do_kk()
+    do_ky(0)
+    do_val()
+    do_ky(1)
+    do_yc(0)
+    do_yc(4)
+    do_tc(1)
+    do_yc(3)
+    do_cw(3)
+    do_zs(11)
+    do_kc(0)
+    do_zy(8)
+    do_cw(0)
+    do_cw(4)
+    do_yc(9)
+    do_td(1)
+    do_zs(10)
+    do_kc(1)
+    do_qq()
+    do_zy(11)
+    do_kw(1)
+    do_cw(7)
+    do_kw(0)
+    do_cw(6)
+    do_at(0)
+    do_cw(9)
+    do_at(1)
+    do_at(2)
+    do_yc(8)
+    do_at(3)
+    do_te(1)
+    do_ff(1)
+    do_fc(6)
+    do_fc(7)
+    do_zy(10)
+    do_hg()
+    do_bw(0)
+    do_cw(8)
+    do_bw(1)
+    do_bw(2)
+    do_bw(3)
+    do_dc()
+    do_cw(5)
+    do_fy(7)
+    do_go()
+    do_fc(3)
+    do_yc(10)
+    do_ff(0)
+    do_dy()
+    do_fz(7)
+    do_ff(2)
+    do_yc(11)
+    do_fc(4)
+    do_cw(10)
+    do_fy(3)
+    do_cw(11)
+    do_ff(3)
+    do_dw()
+    do_of()
+    do_fy(6)
+    do_fc(9)
+    do_ag()
+    do_eo(0)
+    do_fz(3)
+    do_sx(0)
+    do_fc(0)
+    do_eb(0)
+    do_eb(1)
+    do_fy(9)
+    do_fc(2)
+    do_fz(6)
+    do_fy(0)
+    do_fc(8)
+    do_eb(2)
+    do_sx(2)
+    do_fc(5)
+    do_eo(2)
+    do_fy(4)
+    do_fz(9)
+    do_sx(3)
+    do_fc(10)
+    do_fz(0)
+    do_fy(5)
+    do_fz(4)
+    do_fc(11)
+    do_sa(1)
+    do_fy(11)
+    do_eb(3)
+    do_pa()
+    do_fz(5)
+    do_eo(3)
+    do_sm(1)
+    do_fc(1)
+    do_pb()
+    do_eo(1)
+    do_sb(1)
+    do_sx(1)
+    do_sa(0)
+    do_fy(8)
+    do_fy(1)
+    do_fz(11)
+    do_ew(4)
+    do_fz(1)
+    do_fy(2)
+    do_ew(9)
+    do_sm(0)
+    do_ew(5)
+    do_fy(10)
+    do_sb(0)
+    do_pc()
+    do_fz(8)
+    do_sc(1)
+    do_ew(7)
+    do_sc(0)
+    do_ew(0)
+    do_ew(11)
+    do_fz(2)
+    do_ew(3)
+    do_fz(10)
+    do_sd(1)
+    do_sd(0)
+    do_pd()
+    do_pe()
+    do_sw(0)
+    do_ew(8)
+    do_sw(1)
+    do_ew(2)
+    do_ew(10)
+    do_ew(1)
+    do_ew(6)
     for copy in sends:
         if not any(copy is other for other in settled):
             copy.wait_send()
-
-
-SCHEDULE = (
-    "zs1", "vec", "zs6", "zs4", "zy1", "norm", "ta0", "zy6", "zs7", "zs5", "tb0", "zs2",
-    "yc1", "ta1", "zs3", "zy4", "tab", "zy5", "zy7", "yc5", "tc0", "zs9", "cw1", "yc7",
-    "zy2", "zs0", "zy3", "td0", "yc2", "cw2", "tb1", "zy9", "yc6", "te0", "zs8", "zy0",
-    "aff", "kk", "ky0", "val", "ky1", "yc0", "yc4", "tc1", "yc3", "cw3", "zs11", "kc0",
-    "zy8", "cw0", "cw4", "yc9", "td1", "zs10", "kc1", "qq", "zy11", "kw1", "cw7", "kw0",
-    "cw6", "at0", "cw9", "at1", "at2", "yc8", "at3", "te1", "ff1", "fc6", "fc7", "zy10",
-    "hg", "bw0", "cw8", "bw1", "bw2", "bw3", "dc", "cw5", "fy7", "go", "fc3", "yc10",
-    "ff0", "dy", "fz7", "ff2", "yc11", "fc4", "cw10", "fy3", "cw11", "ff3", "dw", "of0",
-    "fy6", "fc9", "ag", "eo0", "fz3", "sx0", "fc0", "eb0", "eb1", "fy9", "fc2", "fz6",
-    "fy0", "fc8", "eb2", "sx2", "fc5", "eo2", "fy4", "fz9", "sx3", "fc10", "fz0", "fy5",
-    "fz4", "fc11", "sa1", "fy11", "eb3", "pa", "fz5", "eo3", "sm1", "fc1", "pb", "eo1",
-    "sb1", "sx1", "sa0", "fy8", "fy1", "fz11", "ew4", "fz1", "fy2", "ew9", "sm0", "ew5",
-    "fy10", "sb0", "pc", "fz8", "sc1", "ew7", "sc0", "ew0", "ew11", "fz2", "ew3", "fz10",
-    "sd1", "sd0", "pd", "pe", "sw0", "ew8", "sw1", "ew2", "ew10", "ew1", "ew6",
-)
 
 
 def fits(depth_size, group, depth_rows, rows, width, ff_chunks):

time: 240 us -> 240 us (level)
  no operation moved by 1% of the time
where the time goes in v4:
time: 240 us
  Pallas kernels  239 us (100%)
    pallas_call x1, Pallas kernels, fused_shards(): pl.pallas_call(functools.partial(fused_kernel, names, depth_size, group),...  233 us
    pallas_call x1, Pallas kernels, close(): pl.pallas_call(functools.partial(close_kernel, depth_size, group), grid=(...  5.59 us

profile of v4, /device:TPU:0, one launch (start us, length us, event | category | flops | bytes accessed | tf_op | source)
XLA Modules:
  0.0 239.8 jit_solution(3862233816176874598)
XLA Ops:
  0.7 233.4 %shard_map.331 = (bf16[2,128,2048]{2,1,0:T(8,128)(2,1)}, bf16[128,1024]{1,0:T(8,128)(2,1)}, bf16[128,1024]{1,0:T(8,128)(2,1)}, bf16[128,1024]{1,0:T(8,128)(2,1)}...) custom-call(s32[32]{0:T(128)} %refs_0_.1, ...), custom_call_target="tpu_custom_call" | custom-call | tf_op jit(solution)/shard_map/pallas_call | solution.py:1471
  234.1 5.6 %shard_map.332 = (bf16[128,2048]{1,0:T(8,128)(2,1)}, f32[128,2048]{1,0:T(8,128)}, f32[128,1024]{1,0:T(8,128)}, f32[128,1024]{1,0:T(8,128)}, f32[128,1024]{1,0:T(...) custom-call(bf16[128,2048]{1,0:T(8,128)(2,1)} %x_in.1, ...), custom_call_target="tpu_custom_call" | custom-call | tf_op jit(solution)/shard_map/pallas_call | solution.py:1572

commit v5 on v4

--- a/solution.py
+++ b/solution.py
@@ -469,6 +469,9 @@
 
 
 SMALL_ROWS = 96
+LATE = (3, 7,)
+LATE_ROWS = 1
+LATE_COLS = 2
 VMEM_BYTES = 64 << 20
 
 
@@ -531,6 +534,8 @@
         ("pl", (group.bit_length() - 1, SMALL_ROWS, 128), F32),
         ("pz", (depth_size, SMALL_ROWS, 128), F32),
         ("px", (2, SMALL_ROWS, 128), F32),
+        ("dr", (LATE_ROWS, 2, depth_size * depth_rows, CHUNK), BF),
+        ("dc", (LATE_COLS, 2, CHUNK, depth_size * depth_rows), BF),
     ]
 
 
@@ -553,6 +558,9 @@
         ("e_s", (items, depth_size)),
         ("e_r", (items, depth_size)),
         ("e_l", (items,)),
+        ("d_s", (LATE_ROWS + LATE_COLS, 2, depth_size)),
+        ("d_r", (LATE_ROWS + LATE_COLS, 2, depth_size)),
+        ("d_l", (LATE_ROWS + LATE_COLS, depth_size)),
         ("o_s", (2, 6)),
         ("o_r", (2, 6)),
         ("p_s", (bits + depth_size,)),
@@ -668,7 +676,7 @@
             )
         ]
 
-    def fold_finish(k, stage, copies):
+    def fold_add(k, stage, copies):
         received(copies)
         kind, a = units[k]
         size = 2**stage
@@ -702,6 +710,60 @@
         ]
         copies.append(local(part(grads, kind, a, own_block, 1), into, m.e_l.at[k]))
         return copies
+
+    late = {k: n for n, k in enumerate(LATE)}
+    other_slot = at.base(1) + 1 - at.bit(0)
+
+    def depth_buffer(k, h, first, count):
+        kind, a = units[k]
+        same = [j for j in LATE if units[j][0] == kind].index(k)
+        if kind == "r":
+            return m.dr.at[same, h, blocks(first, count), :]
+        return m.dc.at[same, h, :, blocks(first, count)]
+
+    def depth_first_start(k, copies):
+        fold_add(k, 1, copies)
+        kind, a = units[k]
+        n = late[k]
+        copies = []
+        for h, slot in enumerate((at.slot, other_slot)):
+            for s in range(1, depth_size):
+                copies.append(
+                    remote(
+                        part(grads, kind, a, slot * depth_size + peer(s), 1),
+                        depth_buffer(k, h, at.depth, 1),
+                        m.d_s.at[n, h, s],
+                        m.d_r.at[n, h, s],
+                        at.along(s),
+                    )
+                )
+            own = part(grads, kind, a, slot * depth_size + at.depth, 1)
+            depth_buffer(k, h, at.depth, 1)[...] = own[...]
+        return copies
+
+    def depth_first_fold(k, copies):
+        received(copies)
+        kind, a = units[k]
+        return [
+            remote(
+                depth_buffer(k, 1, 0, depth_size),
+                part(landing, kind, a, 0, depth_size),
+                m.f_s.at[k, 0],
+                m.f_r.at[k, 0],
+                at.across(0),
+            )
+        ]
+
+    def depth_first_end(k, copies):
+        received(copies)
+        kind, a = units[k]
+        ends = []
+        for z in range(depth_size):
+            mine = depth_buffer(k, 0, z, 1)
+            theirs = part(landing, kind, a, z, 1)
+            mine[...] = (mine[...].astype(F32) + theirs[...].astype(F32)).astype(BF)
+            ends.append(local(mine, outer(kind, a, z, 1), m.d_l.at[late[k], z]))
+        return ends
 
     near = {"ctx": at.ctx + (1 - 2 * (at.depth % 2)) * group}
     far = {"ctx": at.ctx + (2 - 4 * (at.depth // 2)) * group}
@@ -1187,16 +1249,27 @@
         f_live[n] = fold_start(n, 1)
 
     def do_fy(n):
-        fold_finish(n, 1, f_live[n])
+        fold_add(n, 1, f_live[n])
         f_live[n] = fold_start(n, 0)
 
     def do_fz(n):
-        fold_finish(n, 0, f_live[n])
+        fold_add(n, 0, f_live[n])
         e_live[n] = end_start(n)
 
+    def do_fq(n):
+        f_live[n] = depth_first_start(n, f_live[n])
+
+    def do_fr(n):
+        f_live[n] = depth_first_fold(n, f_live[n])
+
+    def do_fs(n):
+        e_live[n] = depth_first_end(n, f_live[n])
+
     def do_ew(n):
-        received(e_live[n][:-1])
-        e_live[n][-1].wait()
+        here = depth_size if n in late else 1
+        received(e_live[n][:-here])
+        for copy in e_live[n][-here:]:
+            copy.wait()
 
     def do_eo(n):
         end_quarter(end_out, at.tp if n >= 2 else 1 - at.tp, n % 2)
@@ -1246,172 +1319,174 @@
         small_finish(p_live[3])
 
     do_zs(1)
+    do_zs(2)
+    do_norm()
+    do_zs(10)
+    do_zy(1)
+    do_ta(0)
     do_vec()
-    do_zs(6)
+    do_zy(2)
     do_zs(4)
-    do_zy(1)
-    do_norm()
-    do_ta(0)
-    do_zy(6)
-    do_zs(7)
-    do_zs(5)
     do_tb(0)
-    do_zs(2)
-    do_yc(1)
     do_ta(1)
+    do_zy(10)
+    do_yc(2)
+    do_tab()
+    do_zy(4)
     do_zs(3)
-    do_zy(4)
-    do_tab()
-    do_zy(5)
-    do_zy(7)
-    do_yc(5)
     do_tc(0)
-    do_zs(9)
-    do_cw(1)
-    do_yc(7)
-    do_zy(2)
+    do_cw(2)
     do_zs(0)
     do_zy(3)
+    do_zs(9)
     do_td(0)
-    do_yc(2)
-    do_cw(2)
     do_tb(1)
-    do_zy(9)
-    do_yc(6)
+    do_yc(10)
+    do_yc(1)
+    do_zy(0)
+    do_zs(11)
+    do_yc(4)
     do_te(0)
     do_zs(8)
-    do_zy(0)
+    do_zy(9)
+    do_zs(6)
     do_aff()
-    do_kk()
-    do_ky(0)
+    do_yc(3)
     do_val()
     do_ky(1)
+    do_cw(1)
+    do_kk()
+    do_tc(1)
+    do_ky(0)
+    do_zs(7)
     do_yc(0)
-    do_yc(4)
-    do_tc(1)
-    do_yc(3)
-    do_cw(3)
-    do_zs(11)
+    do_cw(0)
+    do_kc(1)
+    do_zy(11)
     do_kc(0)
     do_zy(8)
-    do_cw(0)
-    do_cw(4)
+    do_qq()
+    do_kw(0)
+    do_td(1)
     do_yc(9)
-    do_td(1)
-    do_zs(10)
-    do_kc(1)
-    do_qq()
-    do_zy(11)
     do_kw(1)
-    do_cw(7)
-    do_kw(0)
-    do_cw(6)
     do_at(0)
-    do_cw(9)
     do_at(1)
     do_at(2)
+    do_cw(3)
+    do_zs(5)
+    do_zy(6)
+    do_yc(11)
+    do_cw(4)
+    do_at(3)
     do_yc(8)
-    do_at(3)
     do_te(1)
-    do_ff(1)
-    do_fc(6)
-    do_fc(7)
-    do_zy(10)
+    do_go()
+    do_fc(3)
     do_hg()
+    do_cw(10)
     do_bw(0)
+    do_zy(7)
+    do_bw(1)
     do_cw(8)
-    do_bw(1)
+    do_cw(11)
     do_bw(2)
     do_bw(3)
     do_dc()
+    do_zy(5)
+    do_ff(3)
+    do_yc(6)
+    do_cw(9)
+    do_fq(3)
+    do_ff(2)
+    do_fc(9)
+    do_cw(6)
+    do_yc(7)
+    do_dy()
+    do_yc(5)
+    do_cw(7)
+    do_ff(1)
+    do_fc(7)
     do_cw(5)
-    do_fy(7)
-    do_go()
-    do_fc(3)
-    do_yc(10)
     do_ff(0)
-    do_dy()
-    do_fz(7)
-    do_ff(2)
-    do_yc(11)
+    do_fc(5)
+    do_of()
+    do_fc(6)
+    do_fy(9)
+    do_fq(7)
+    do_fy(5)
+    do_dw()
+    do_ag()
+    do_fc(0)
+    do_eo(0)
+    do_sx(0)
     do_fc(4)
-    do_cw(10)
-    do_fy(3)
-    do_cw(11)
-    do_ff(3)
-    do_dw()
-    do_of()
+    do_eo(1)
+    do_fz(9)
+    do_sx(1)
+    do_eb(0)
+    do_fy(0)
+    do_eb(1)
+    do_eo(2)
+    do_eb(3)
+    do_fc(1)
+    do_fz(5)
+    do_eb(2)
+    do_pa()
+    do_ew(9)
+    do_fc(11)
+    do_pb()
+    do_fc(2)
+    do_fy(1)
+    do_fc(10)
+    do_fy(4)
+    do_sx(2)
+    do_fz(0)
+    do_pc()
+    do_fy(10)
+    do_eo(3)
+    do_sa(0)
+    do_fz(1)
+    do_fz(4)
+    do_sm(0)
+    do_pd()
+    do_fy(11)
+    do_fc(8)
+    do_sx(3)
+    do_ew(0)
+    do_fr(7)
+    do_sb(0)
+    do_sa(1)
+    do_fz(11)
+    do_fy(2)
+    do_ew(1)
+    do_sm(1)
+    do_sb(1)
+    do_fs(7)
+    do_fy(8)
+    do_ew(5)
+    do_fr(3)
+    do_pe()
+    do_sc(0)
     do_fy(6)
-    do_fc(9)
-    do_ag()
-    do_eo(0)
-    do_fz(3)
-    do_sx(0)
-    do_fc(0)
-    do_eb(0)
-    do_eb(1)
-    do_fy(9)
-    do_fc(2)
+    do_fz(8)
+    do_fz(10)
+    do_sc(1)
     do_fz(6)
-    do_fy(0)
-    do_fc(8)
-    do_eb(2)
-    do_sx(2)
-    do_fc(5)
-    do_eo(2)
-    do_fy(4)
-    do_fz(9)
-    do_sx(3)
-    do_fc(10)
-    do_fz(0)
-    do_fy(5)
-    do_fz(4)
-    do_fc(11)
-    do_sa(1)
-    do_fy(11)
-    do_eb(3)
-    do_pa()
-    do_fz(5)
-    do_eo(3)
-    do_sm(1)
-    do_fc(1)
-    do_pb()
-    do_eo(1)
-    do_sb(1)
-    do_sx(1)
-    do_sa(0)
-    do_fy(8)
-    do_fy(1)
-    do_fz(11)
+    do_sd(0)
+    do_fs(3)
+    do_fz(2)
+    do_ew(10)
+    do_ew(11)
     do_ew(4)
-    do_fz(1)
-    do_fy(2)
-    do_ew(9)
-    do_sm(0)
-    do_ew(5)
-    do_fy(10)
-    do_sb(0)
-    do_pc()
-    do_fz(8)
-    do_sc(1)
+    do_ew(8)
+    do_sd(1)
+    do_ew(2)
+    do_sw(0)
+    do_ew(6)
     do_ew(7)
-    do_sc(0)
-    do_ew(0)
-    do_ew(11)
-    do_fz(2)
+    do_sw(1)
     do_ew(3)
-    do_fz(10)
-    do_sd(1)
-    do_sd(0)
-    do_pd()
-    do_pe()
-    do_sw(0)
-    do_ew(8)
-    do_sw(1)
-    do_ew(2)
-    do_ew(10)
-    do_ew(1)
-    do_ew(6)
     for copy in sends:
         if not any(copy is other for other in settled):
             copy.wait_send()

time: 240 us -> 227 us (0.946)
  Pallas kernels: 239 us -> 226 us
    pallas_call x1, Pallas kernels: 233 us -> 221 us  [fused_shards(): pl.pallas_call(functools.partial(fused_kernel, names, depth_size, group),...]
where the time goes in v5:
time: 227 us
  Pallas kernels  226 us (100%)
    pallas_call x1, Pallas kernels, fused_shards(): pl.pallas_call(functools.partial(fused_kernel, names, depth_size, group),...  221 us
    pallas_call x1, Pallas kernels, close(): pl.pallas_call(functools.partial(close_kernel, depth_size, group), grid=(...  5.59 us

profile of v5, /device:TPU:0, one launch (start us, length us, event | category | flops | bytes accessed | tf_op | source)
XLA Modules:
  0.0 227.2 jit_solution(12520072363438337911)
XLA Ops:
  0.7 220.7 %shard_map.331 = (bf16[2,128,2048]{2,1,0:T(8,128)(2,1)}, bf16[128,1024]{1,0:T(8,128)(2,1)}, bf16[128,1024]{1,0:T(8,128)(2,1)}, bf16[128,1024]{1,0:T(8,128)(2,1)}...) custom-call(s32[32]{0:T(128)} %refs_0_.1, ...), custom_call_target="tpu_custom_call" | custom-call | tf_op jit(solution)/shard_map/pallas_call | solution.py:1546
  221.4 5.6 %shard_map.332 = (bf16[128,2048]{1,0:T(8,128)(2,1)}, f32[128,2048]{1,0:T(8,128)}, f32[128,1024]{1,0:T(8,128)}, f32[128,1024]{1,0:T(8,128)}, f32[128,1024]{1,0:T(...) custom-call(bf16[128,2048]{1,0:T(8,128)(2,1)} %x_in.1, ...), custom_call_target="tpu_custom_call" | custom-call | tf_op jit(solution)/shard_map/pallas_call | solution.py:1647

commit v6 on v5

--- a/solution.py
+++ b/solution.py
@@ -469,6 +469,7 @@
 
 
 SMALL_ROWS = 96
+SMALL_SENT = 80
 LATE = (3, 7,)
 LATE_ROWS = 1
 LATE_COLS = 2
@@ -527,13 +528,14 @@
         ("te", (2, rows, half), BF),
         ("mean", (tokens, 1), F32),
         ("inv", (tokens, 1), F32),
+        ("xl", (2, rows, width), BF),
         ("gv", (8, width), F32),
         ("biases", (8, HD), F32),
         ("places", (group * tokens // 128, 128), F32),
         ("ps", (group.bit_length(), SMALL_ROWS, 128), F32),
         ("pl", (group.bit_length() - 1, SMALL_ROWS, 128), F32),
-        ("pz", (depth_size, SMALL_ROWS, 128), F32),
-        ("px", (2, SMALL_ROWS, 128), F32),
+        ("pz", (depth_size, SMALL_SENT, 128), F32),
+        ("px", (2, SMALL_SENT, 128), F32),
         ("dr", (LATE_ROWS, 2, depth_size * depth_rows, CHUNK), BF),
         ("dc", (LATE_COLS, 2, CHUNK, depth_size * depth_rows), BF),
     ]
@@ -558,6 +560,7 @@
         ("e_s", (items, depth_size)),
         ("e_r", (items, depth_size)),
         ("e_l", (items,)),
+        ("x_l", (2,)),
         ("d_s", (LATE_ROWS + LATE_COLS, 2, depth_size)),
         ("d_r", (LATE_ROWS + LATE_COLS, 2, depth_size)),
         ("d_l", (LATE_ROWS + LATE_COLS, depth_size)),
@@ -585,6 +588,7 @@
     for name, ref in zip(names, refs, strict=True):
         setattr(m, name, ref)
     at = Place(depth_size, group)
+    loads = [local(source, m.xl.at[i], m.x_l.at[i]) for i, source in enumerate((m.x_in, m.dy_in))]
     at.greet(at.everyone())
     bits = at.bits
     rows, width = m.x_in.shape
@@ -841,12 +845,14 @@
 
     def place_rows():
         mine = token_rows(at.depth)
+        for copy in loads:
+            copy.wait()
         for b in range(block_count):
             c = natural[b]
             into = slice(b * depth_rows, (b + 1) * depth_rows)
             out_of = slice(c * depth_rows, (c + 1) * depth_rows)
-            m.x[mine, into] = m.x_in[:, out_of]
-            m.dy[mine, into] = m.dy_in[:, out_of]
+            m.x[mine, into] = m.xl[0, :, out_of]
+            m.dy[mine, into] = m.xl[1, :, out_of]
 
     def place_vectors():
         m.ps[0] = jnp.zeros_like(m.ps[0])
@@ -1152,12 +1158,12 @@
         m.ps[stage + 1] = m.ps[stage] + m.pl[stage]
 
     def small_depth():
-        total = m.ps.at[bits]
+        total = m.ps.at[bits, 0:SMALL_SENT, :]
         copies = [
             remote(total, m.pz.at[at.depth], m.p_s.at[bits + s], m.p_r.at[bits + s], at.along(s))
             for s in range(1, depth_size)
         ]
-        m.pz[at.depth] = m.ps[bits]
+        m.pz[at.depth] = m.ps[bits, 0:SMALL_SENT, :]
         return copies
 
     def small_twin(copies):
@@ -1560,7 +1566,7 @@
             shape((thin // 128, 128), F32),
             shape((width // 128, 128), F32),
         ),
-        in_specs=[pl.BlockSpec(memory_space=pltpu.SMEM)] + [vmem] * 11 + [hbm] * 6,
+        in_specs=[pl.BlockSpec(memory_space=pltpu.SMEM)] + [hbm] * 2 + [vmem] * 9 + [hbm] * 6,
         out_specs=(vmem,) + (hbm,) * 6 + (vmem,) * 6,
         scratch_shapes=[pltpu.VMEM(s, t) for _, s, t in buffers]
         + [pltpu.SemaphoreType.DMA(s) for _, s in semaphores]

time: 227 us -> 226 us (level)
  no operation moved by 1% of the time
where the time goes in v6:
time: 226 us
  Pallas kernels  225 us (100%)
    pallas_call x1, Pallas kernels, fused_shards(): pl.pallas_call(functools.partial(fused_kernel, names, depth_size, group),...  220 us
    pallas_call x1, Pallas kernels, close(): pl.pallas_call(functools.partial(close_kernel, depth_size, group), grid=(...  5.59 us

profile of v6, /device:TPU:0, one launch (start us, length us, event | category | flops | bytes accessed | tf_op | source)
XLA Modules:
  0.0 226.2 jit_solution(6753799845836516198)
XLA Ops:
  0.7 219.8 %shard_map.331 = (bf16[2,128,2048]{2,1,0:T(8,128)(2,1)}, bf16[128,1024]{1,0:T(8,128)(2,1)}, bf16[128,1024]{1,0:T(8,128)(2,1)}, bf16[128,1024]{1,0:T(8,128)(2,1)}...) custom-call(s32[32]{0:T(128)} %refs_0_.1, ...), custom_call_target="tpu_custom_call" | custom-call | tf_op jit(solution)/shard_map/pallas_call | solution.py:1552
  220.4 5.6 %shard_map.332 = (bf16[128,2048]{1,0:T(8,128)(2,1)}, f32[128,2048]{1,0:T(8,128)}, f32[128,1024]{1,0:T(8,128)}, f32[128,1024]{1,0:T(8,128)}, f32[128,1024]{1,0:T(...) custom-call(bf16[128,2048]{1,0:T(8,128)(2,1)} %x_in.1, ...), custom_call_target="tpu_custom_call" | custom-call | tf_op jit(solution)/shard_map/pallas_call | solution.py:1653

commit v7 on v6

--- a/solution.py
+++ b/solution.py
@@ -1328,11 +1328,11 @@
     do_zs(2)
     do_norm()
     do_zs(10)
+    do_ta(0)
     do_zy(1)
-    do_ta(0)
-    do_vec()
     do_zy(2)
     do_zs(4)
+    do_vec()
     do_tb(0)
     do_ta(1)
     do_zy(10)
@@ -1341,11 +1341,11 @@
     do_zy(4)
     do_zs(3)
     do_tc(0)
-    do_cw(2)
     do_zs(0)
     do_zy(3)
     do_zs(9)
     do_td(0)
+    do_cw(2)
     do_tb(1)
     do_yc(10)
     do_yc(1)
@@ -1368,10 +1368,10 @@
     do_yc(0)
     do_cw(0)
     do_kc(1)
+    do_qq()
     do_zy(11)
     do_kc(0)
     do_zy(8)
-    do_qq()
     do_kw(0)
     do_td(1)
     do_yc(9)
@@ -1390,8 +1390,8 @@
     do_go()
     do_fc(3)
     do_hg()
+    do_bw(0)
     do_cw(10)
-    do_bw(0)
     do_zy(7)
     do_bw(1)
     do_cw(8)
@@ -1402,8 +1402,8 @@
     do_zy(5)
     do_ff(3)
     do_yc(6)
+    do_fq(3)
     do_cw(9)
-    do_fq(3)
     do_ff(2)
     do_fc(9)
     do_cw(6)
@@ -1428,12 +1428,12 @@
     do_sx(0)
     do_fc(4)
     do_eo(1)
+    do_sx(1)
     do_fz(9)
-    do_sx(1)
+    do_eo(2)
     do_eb(0)
     do_fy(0)
     do_eb(1)
-    do_eo(2)
     do_eb(3)
     do_fc(1)
     do_fz(5)
@@ -1468,23 +1468,23 @@
     do_ew(1)
     do_sm(1)
     do_sb(1)
-    do_fs(7)
     do_fy(8)
     do_ew(5)
     do_fr(3)
+    do_fs(7)
     do_pe()
     do_sc(0)
     do_fy(6)
     do_fz(8)
     do_fz(10)
     do_sc(1)
-    do_fz(6)
     do_sd(0)
     do_fs(3)
     do_fz(2)
+    do_ew(4)
     do_ew(10)
+    do_fz(6)
     do_ew(11)
-    do_ew(4)
     do_ew(8)
     do_sd(1)
     do_ew(2)

time: 226 us -> 225 us (level)
  no operation moved by 1% of the time
where the time goes in v7:
time: 225 us
  Pallas kernels  224 us (100%)
    pallas_call x1, Pallas kernels, fused_shards(): pl.pallas_call(functools.partial(fused_kernel, names, depth_size, group),...  218 us
    pallas_call x1, Pallas kernels, close(): pl.pallas_call(functools.partial(close_kernel, depth_size, group), grid=(...  5.59 us

profile of v7, /device:TPU:0, one launch (start us, length us, event | category | flops | bytes accessed | tf_op | source)
XLA Modules:
  0.0 224.5 jit_solution(86956253769457426)
XLA Ops:
  0.7 218.1 %shard_map.331 = (bf16[2,128,2048]{2,1,0:T(8,128)(2,1)}, bf16[128,1024]{1,0:T(8,128)(2,1)}, bf16[128,1024]{1,0:T(8,128)(2,1)}, bf16[128,1024]{1,0:T(8,128)(2,1)}...) custom-call(s32[32]{0:T(128)} %refs_0_.1, ...), custom_call_target="tpu_custom_call" | custom-call | tf_op jit(solution)/shard_map/pallas_call | solution.py:1552
  218.8 5.6 %shard_map.332 = (bf16[128,2048]{1,0:T(8,128)(2,1)}, f32[128,2048]{1,0:T(8,128)}, f32[128,1024]{1,0:T(8,128)}, f32[128,1024]{1,0:T(8,128)}, f32[128,1024]{1,0:T(...) custom-call(bf16[128,2048]{1,0:T(8,128)(2,1)} %x_in.1, ...), custom_call_target="tpu_custom_call" | custom-call | tf_op jit(solution)/shard_map/pallas_call | solution.py:1653

commit v8 on v7

--- a/solution.py
+++ b/solution.py
@@ -1425,8 +1425,8 @@
     do_ag()
     do_fc(0)
     do_eo(0)
+    do_fc(4)
     do_sx(0)
-    do_fc(4)
     do_eo(1)
     do_sx(1)
     do_fz(9)

time: 225 us -> 225 us (level)
  no operation moved by 1% of the time
where the time goes in v8:
time: 225 us
  Pallas kernels  224 us (100%)
    pallas_call x1, Pallas kernels, fused_shards(): pl.pallas_call(functools.partial(fused_kernel, names, depth_size, group),...  218 us
    pallas_call x1, Pallas kernels, close(): pl.pallas_call(functools.partial(close_kernel, depth_size, group), grid=(...  5.59 us

profile of v8, /device:TPU:0, one launch (start us, length us, event | category | flops | bytes accessed | tf_op | source)
XLA Modules:
  0.0 224.5 jit_solution(17602462838084238355)
XLA Ops:
  0.7 218.1 %shard_map.331 = (bf16[2,128,2048]{2,1,0:T(8,128)(2,1)}, bf16[128,1024]{1,0:T(8,128)(2,1)}, bf16[128,1024]{1,0:T(8,128)(2,1)}, bf16[128,1024]{1,0:T(8,128)(2,1)}...) custom-call(s32[32]{0:T(128)} %refs_0_.1, ...), custom_call_target="tpu_custom_call" | custom-call | tf_op jit(solution)/shard_map/pallas_call | solution.py:1552
  218.8 5.6 %shard_map.332 = (bf16[128,2048]{1,0:T(8,128)(2,1)}, f32[128,2048]{1,0:T(8,128)}, f32[128,1024]{1,0:T(8,128)}, f32[128,1024]{1,0:T(8,128)}, f32[128,1024]{1,0:T(...) custom-call(bf16[128,2048]{1,0:T(8,128)(2,1)} %x_in.1, ...), custom_call_target="tpu_custom_call" | custom-call | tf_op jit(solution)/shard_map/pallas_call | solution.py:1653
